TPU v7x, 256 devices: a whole 4x4x8 slice. The times are simulated.
256 devices in a mesh: dom: 64 (over y, z, core), feat: 4 (over x).
Axes of the slice: x: 4, y: 4, z: 8, core: 2. Of those that a mesh axis runs over, the one named last changes fastest.
Arguments:
- features: bfloat16 [16384, 512], P('dom', 'feat'), may hold values from -6 to 6
- hub_feats: bfloat16 [2048, 256], P('dom'), may hold values from -6 to 6
- nbr_owner: int32 [8, 32768, 1], P(None, 'dom'), may hold values from 0 to 63; in each aligned block of 512 rows (0 to 511, 512 to 1023, ..., all dimensions but the last counted through in order) at most 16 rows name the same one
- nbr_row: int32 [8, 32768], P(None, 'dom'), may hold values from 0 to 511
- hub_ids: int32 [32768, 4], P('dom'), may hold values from 0 to 2047
- w_self: bfloat16 [256, 256], replicated, may hold values from -0.375 to 0.375
- w_nbr: bfloat16 [256, 256], replicated, may hold values from -0.375 to 0.375
- grad_out: bfloat16 [16384, 512], P('dom', 'feat'), may hold values from -6 to 6
Outputs:
- outputs: bfloat16 [16384, 512], P('dom', 'feat')
- grad_features: bfloat16 [16384, 512], P('dom', 'feat')
- grad_hubs: float32 [2048, 256], P('dom', 'feat')
- grad_self: float32 [256, 256], P('feat')
- grad_nbr: float32 [256, 256], P('feat')
Inputs may be any that keep to these rules, and one draw needn't show every extreme that they name: `nbr_owner`: for each sample index k, among the 512 targets of one partition at most 16 have their k-th neighbour on one owner; that many is reached.
All inputs are finite; a program needn't handle non-finite values.
Results may differ from a plain program's by a relative error of at most 0.0054.
Values may be sent and summed in bfloat16 or wider, within the bound.
No kernel may reach another device: no remote copies, remote signals or barrier semaphores. Data moves between devices by JAX's collectives and lax.ppermute only.
A program may use at most 64 MiB of HBM per device.

v0:
```python
import jax
import jax.numpy as jnp
from jax import lax
from jax.sharding import PartitionSpec as P


def edge_slots(owners, capacity, peer_count):
    level_count, vertices = owners.shape

    def rank_level(owner_row):
        ordering = jnp.argsort(owner_row, stable=True)
        ordered = owner_row[ordering]
        group_start = jnp.searchsorted(
            ordered, jnp.arange(peer_count, dtype=jnp.int32), side="left"
        )
        rank_sorted = jnp.arange(vertices, dtype=jnp.int32) - group_start[ordered]
        return jnp.zeros((vertices,), jnp.int32).at[ordering].set(rank_sorted)

    ranking = jax.vmap(rank_level)(owners)
    level_index = jnp.arange(level_count, dtype=jnp.int32)[:, None]
    return owners * (level_count * capacity) + level_index * capacity + ranking


def request_buffer(slot_ids, row_ids, peer_count, level_count, capacity):
    flat_slots = slot_ids.reshape(-1)
    total = peer_count * level_count * capacity
    send_ids = jnp.zeros((total,), jnp.int32).at[flat_slots].set(row_ids.reshape(-1))
    vertex_ids = jnp.broadcast_to(
        jnp.arange(slot_ids.shape[1], dtype=jnp.int32)[None, :], slot_ids.shape
    ).reshape(-1)
    slot_vertex = jnp.full((total,), -1, jnp.int32).at[flat_slots].set(vertex_ids)
    return (slot_vertex, send_ids.reshape(peer_count, level_count * capacity))


def block_count(total, vertices):
    count = max(1, total // vertices)
    return count


def slot_rows(index_slots, table):
    vertices = table.shape[0]
    total = index_slots.shape[0]
    count = block_count(total, vertices)
    blocks = index_slots.reshape(count, total // count)
    vertex_range = jnp.arange(vertices, dtype=jnp.int32)[None, :]

    def one_block(block_ids):
        selector = (block_ids[:, None] == vertex_range).astype(table.dtype)
        return jnp.dot(selector, table, preferred_element_type=jnp.float32).astype(table.dtype)

    return lax.map(one_block, blocks).reshape(total, table.shape[1])


def slot_sums(index_slots, rows, vertices):
    total, columns = rows.shape
    count = block_count(total, vertices)
    blocks = index_slots.reshape(count, total // count)
    row_blocks = rows.reshape(count, total // count, columns)
    vertex_range = jnp.arange(vertices, dtype=jnp.int32)[None, :]
    contract_first = (((0,), (0,)), ((), ()))

    def add_block(carry, pair):
        block_ids, block_rows = pair
        selector = (block_ids[:, None] == vertex_range).astype(block_rows.dtype)
        return (
            carry
            + lax.dot_general(
                selector, block_rows, contract_first, preferred_element_type=jnp.float32
            ),
            None,
        )

    summed, unused = lax.scan(
        add_block, jnp.zeros((vertices, columns), jnp.float32), (blocks, row_blocks)
    )
    return summed


def pick_rows(matrix, parity):
    paired = matrix.reshape(matrix.shape[0] // 2, 2, matrix.shape[1])
    return lax.dynamic_index_in_dim(paired, parity, 1, keepdims=False)


def body(features, hub_feats, nbr_owner, nbr_row, hub_ids, w_self, w_nbr, grad_out):
    half_rows, piece = features.shape
    vertices = 2 * half_rows
    peer_count = lax.axis_size("dom")
    full_width = w_self.shape[0]
    quarter = full_width // lax.axis_size("feat")
    nbr_count = nbr_owner.shape[0]
    hub_count = hub_ids.shape[1]
    capacity = 2 * vertices // peer_count
    feat_index = lax.axis_index("feat")
    parity = feat_index * piece // full_width
    col_start = feat_index * piece % full_width
    q_start = feat_index * quarter
    divisor = float(nbr_count + hub_count)
    owners = nbr_owner.reshape(nbr_count, vertices)
    features_full = lax.all_gather(features, "feat", axis=1, tiled=True).reshape(
        vertices, full_width
    )
    hub_table = lax.all_gather(hub_feats, "dom", axis=0, tiled=True)
    hub_total = hub_table.shape[0]
    hub_range = jnp.arange(hub_total, dtype=jnp.int32)[None, :]
    hub_counts = jnp.zeros((vertices, hub_total), jnp.bfloat16)
    for column in range(hub_count):
        hub_counts = hub_counts + (hub_ids[:, column : column + 1] == hub_range).astype(
            jnp.bfloat16
        )
    hub_cols = lax.dynamic_slice_in_dim(hub_table, col_start, piece, 1)
    hub_block = jnp.dot(pick_rows(hub_counts, parity), hub_cols, preferred_element_type=jnp.float32)
    slot_ids = edge_slots(owners, capacity, peer_count)
    slot_vertex, send_ids = request_buffer(slot_ids, nbr_row, peer_count, nbr_count, capacity)
    feat_cols = lax.dynamic_slice_in_dim(features_full, col_start, piece, 1)
    asked_rows = lax.all_to_all(send_ids, "dom", split_axis=0, concat_axis=0, tiled=True)
    served = slot_rows(asked_rows.reshape(-1), feat_cols).reshape(asked_rows.shape + (piece,))
    replies, asked_rows = (
        lax.all_to_all(served, "dom", split_axis=0, concat_axis=0, tiled=True),
        asked_rows,
    )
    neigh_block = pick_rows(slot_sums(slot_vertex, replies.reshape(-1, piece), vertices), parity)
    mean_block = ((neigh_block + hub_block) / divisor).astype(jnp.bfloat16)
    mean_full = lax.all_gather(mean_block, "feat", axis=1, tiled=True).reshape(vertices, full_width)
    self_cols = lax.dynamic_slice_in_dim(w_self, col_start, piece, 1)
    nbr_cols = lax.dynamic_slice_in_dim(w_nbr, col_start, piece, 1)
    pre_act = jnp.dot(
        pick_rows(features_full, parity), self_cols, preferred_element_type=jnp.float32
    ) + jnp.dot(pick_rows(mean_full, parity), nbr_cols, preferred_element_type=jnp.float32)
    outputs = jax.nn.silu(pre_act).astype(jnp.bfloat16)
    gate_sig = jax.nn.sigmoid(pre_act)
    grad_pre = (
        grad_out.astype(jnp.float32) * gate_sig * (1.0 + pre_act * (1.0 - gate_sig))
    ).astype(jnp.bfloat16)
    grad_pre_full = lax.all_gather(grad_pre, "feat", axis=1, tiled=True).reshape(
        vertices, full_width
    )
    self_rows = lax.dynamic_slice_in_dim(w_self, col_start, piece, 0)
    contract_last = (((1,), (1,)), ((), ()))
    contract_first = (((0,), (0,)), ((), ()))
    self_term = lax.dot_general(
        pick_rows(grad_pre_full, parity),
        self_rows,
        contract_last,
        preferred_element_type=jnp.float32,
    )
    grad_mean_full = (
        lax.dot_general(grad_pre_full, w_nbr, contract_last, preferred_element_type=jnp.float32)
        / divisor
    ).astype(jnp.bfloat16)
    feat_quarter = lax.dynamic_slice_in_dim(features_full, q_start, quarter, 1)
    mean_quarter = lax.dynamic_slice_in_dim(mean_full, q_start, quarter, 1)
    grad_self_part = lax.dot_general(
        feat_quarter, grad_pre_full, contract_first, preferred_element_type=jnp.float32
    )
    grad_nbr_part = lax.dot_general(
        mean_quarter, grad_pre_full, contract_first, preferred_element_type=jnp.float32
    )
    grad_mean_quarter = lax.dynamic_slice_in_dim(grad_mean_full, q_start, quarter, 1)
    hub_grad_part = lax.dot_general(
        hub_counts, grad_mean_quarter, contract_first, preferred_element_type=jnp.float32
    )
    grad_mean_cols = lax.dynamic_slice_in_dim(grad_mean_full, col_start, piece, 1)
    payload = slot_rows(slot_vertex, grad_mean_cols).reshape(peer_count, -1, piece)
    received = lax.all_to_all(payload, "dom", split_axis=0, concat_axis=0, tiled=True)
    local_grad = slot_sums(asked_rows.reshape(-1), received.reshape(-1, piece), vertices)
    neighbour_block = pick_rows(local_grad, parity)
    grad_features = (self_term + neighbour_block).astype(jnp.bfloat16)
    grad_hubs = lax.psum_scatter(hub_grad_part, "dom", scatter_dimension=0, tiled=True)
    grad_self, grad_nbr = lax.psum((grad_self_part, grad_nbr_part), "dom")
    return (outputs, grad_features, grad_hubs, grad_self, grad_nbr)


def solution(mesh):
    in_specs = (
        P("dom", "feat"),
        P("dom", None),
        P(None, "dom", None),
        P(None, "dom"),
        P("dom", None),
        P(),
        P(),
        P("dom", "feat"),
    )
    out_specs = (
        P("dom", "feat"),
        P("dom", "feat"),
        P("dom", "feat"),
        P("feat", None),
        P("feat", None),
    )
    return jax.shard_map(body, mesh=mesh, in_specs=in_specs, out_specs=out_specs, check_vma=False)
```

profile of v0, /device:TPU:4, one launch (start us, length us, event | category | flops | bytes accessed | tf_op | source)
XLA Modules:
  0.0 670.8 jit_solution(10990250330473973243)
XLA Ops:
  11.0 12.6 %all_gather.12 = bf16[256,512]{0,1:T(8,128)(2,1)S(1)} all-gather(bf16[256,128]{0,1:T(8,128)(2,1)S(1)} %copy.48), channel_id=1, replica_groups=mesh['dom'=64,'feat'=4] {'feat'}, dimensions={1}, use_global_device_ids=true | all-gather | bytes 327680 | tf_op jit(solution)/shard_map/all_gather | solution.py:99
  25.3 25.5 %gather_fusion.1 = s32[4096]{0:T(1024)S(1)} fusion(s32[8,512]{1,0:T(8,128)S(1)} %bitcast.118, s32[4096]{0:T(1024)S(1)} %bitcast.120), kind=kCustom, calls=%fused_computation.1 | custom fusion | bytes 65536 | tf_op jit(solution)/shard_map/vmap()/gather | solution.py:12
  50.9 38.0 %while.70 = (s32[]{:T(128)}, u32[8,64]{1,0:T(8,128)S(1)}, u32[8,64]{1,0:T(8,128)S(1)}, s32[8,512]{1,0:T(8,128)S(1)}, s32[]{:T(128)}, /*index=5*/s32[]{:T(128)}) while((s32[]{:T(128)}, u32[8,64]{1,0:T(8,128)S(1)}, u32[8,64]{1,0:T(8,128)S(1)}, s32[8,512]{1,0:T(8,128)S(1)}, s32[]{:T(128)}, /*index=5*/s32[]{:T(128)}) %tuple.118), condition=%wide.region_2.3_spmd.clone, body=%wide.region_1.2_spmd.clone.sunk | while | flops 11779 | bytes 42065 | solution.py:13
  54.8 3.6 gather_fusion
  62.4 3.6 gather_fusion
  89.0 17.7 %gather_fusion.2 = s32[4096]{0:T(1024)S(1)} fusion(s32[8,64]{1,0:T(8,128)S(1)} %convert_element_type.62, s32[4096]{0:T(1024)S(1)} %bitcast.119), kind=kCustom, calls=%fused_computation.2 | custom fusion | bytes 65536 | tf_op jit(solution)/shard_map/vmap()/gather | solution.py:16
  106.9 15.5 %scatter_custom_fusion.2 = s32[4096]{0:T(1024)S(1)} fusion(s32[4096]{0:T(1024)S(1)} %bitcast.139, s32[4096]{0:T(1024)S(1)} %bitcast.138, s32[]{:T(128)} %constant.121.clone.1), kind=kCustom, calls=%fused_computation.121 | custom fusion | bytes 16388
  122.6 16.1 %scatter_custom_fusion.1 = s32[8192]{0:T(1024)} fusion(s32[4096]{0:T(1024)S(1)} %bitcast.134, s32[4096]{0:T(1024)S(1)} %bitcast.136, s32[]{:T(128)} %constant.121.clone.1), kind=kCustom, calls=%fused_computation.114 | custom fusion | bytes 32772 | tf_op jit(solution)/shard_map/scatter | solution.py:27
  138.7 10.6 %all-to-all-start = ((s32[64,1,128]{2,1,0:T(1,128)}), s32[64,1,128]{2,1,0:T(1,128)S(1)}, u32[]{:S(2)}, u32[]{:S(2)}) async-start(s32[64,1,128]{2,1,0:T(1,128)} %bitcast.4), calls=%async_computation | async-start | bytes 65536 | tf_op jit(solution)/shard_map/all_to_all | solution.py:115
  149.4 9.4 %all-to-all-done = s32[64,1,128]{2,1,0:T(1,128)S(1)} async-done(((s32[64,1,128]{2,1,0:T(1,128)}), s32[64,1,128]{2,1,0:T(1,128)S(1)}, u32[]{:S(2)}, u32[]{:S(2)}) %all-to-all-start) | async-done | bytes 32800 | tf_op jit(solution)/shard_map/all_to_all | solution.py:115
  161.8 16.3 %while.68 = (s32[]{:T(128)}, bf16[16,512,128]{2,1,0:T(8,128)(2,1)}, s32[16,512]{1,0:T(8,128)S(1)}, bf16[512,128]{1,0:T(8,128)(2,1)S(1)}, s32[]{:T(128)}) while((s32[]{:T(128)}, bf16[16,512,128]{2,1,0:T(8,128)(2,1)}, s32[16,512]{1,0:T(8,128)S(1)}, bf16[512,128]{1,0:T(8,128)(2,1)S(1)}, s32[]{:T(128)}) %tuple.121), condition=%wide.region_7.8_spmd.clone, body=%wide.region_6.7_spmd.clone.sunk | while | flops 67436544 | bytes 268865 | solution.py:51
  178.7 4.7 all-to-all-start.1
  185.3 15.5 %scatter_custom_fusion = s32[8192]{0:T(1024)S(1)} fusion(s32[4096]{0:T(1024)S(1)} %bitcast.135, s32[4096]{0:T(1024)S(1)} %bitcast.137, s32[]{:T(128)} %constant.127.clone.1), kind=kCustom, calls=%fused_computation.119 | custom fusion | bytes 32772 | tf_op jit(solution)/shard_map/scatter | solution.py:31
  200.8 34.3 %all-to-all-done.1 = bf16[64,128,128]{2,1,0:T(8,128)(2,1)S(1)} async-done(((bf16[64,128,128]{2,1,0:T(8,128)(2,1)}), bf16[64,128,128]{2,1,0:T(8,128)(2,1)S(1)}, u32[]{:S(2)}, u32[]{:S(2)}) %all-to-all-start.1) | async-done | bytes 2097184 | tf_op jit(solution)/shard_map/all_to_all | solution.py:118
  235.1 10.0 %while.71 = (s32[]{:T(128)}, f32[512,128]{1,0:T(8,128)S(1)}, s32[16,512]{1,0:T(8,128)S(1)}, bf16[16,512,128]{2,1,0:T(8,128)(2,1)S(1)}, s32[]{:T(128)}, /*index=5*/s32[]{:T(128)}) while((s32[]{:T(128)}, f32[512,128]{1,0:T(8,128)S(1)}, s32[16,512]{1,0:T(8,128)S(1)}, bf16[16,512,128]{2,1,0:T(8,128)(2,1)S(1)}, s32[]{:T(128)}, ...), condition=%wide.region_9.10_spmd.clone, body=%wide.region_8.9_spmd.clone.sunk | while | flops 67502080 | bytes 661591 | solution.py:73
  245.8 24.7 %all-gather.2.cloned.1.call-done = bf16[2048,256]{1,0:T(8,128)(2,1)} async-done(((bf16[32,256]{1,0:T(8,128)(2,1)}), bf16[2048,256]{1,0:T(8,128)(2,1)}) %all-gather.2.cloned.1.call-update) | async-done | bytes 1048592 | tf_op jit(solution)/shard_map/all_gather | solution.py:102
  272.9 11.2 %all_gather.14 = bf16[256,512]{1,0:T(8,128)(2,1)S(1)} all-gather(bf16[256,128]{1,0:T(8,128)(2,1)S(1)} %fusion.46), channel_id=1, replica_groups=mesh['dom'=64,'feat'=4] {'feat'}, dimensions={1}, use_global_device_ids=true | all-gather | bytes 327680 | tf_op jit(solution)/shard_map/all_gather | solution.py:123
  285.3 11.5 %all_gather.15 = bf16[256,512]{1,0:T(8,128)(2,1)S(1)} all-gather(bf16[256,128]{1,0:T(8,128)(2,1)S(1)} %get-tuple-element.324), channel_id=1, replica_groups=mesh['dom'=64,'feat'=4] {'feat'}, dimensions={1}, use_global_device_ids=true | all-gather | bytes 327680 | tf_op jit(solution)/shard_map/all_gather | solution.py:134
  299.2 27.7 %while.69 = (s32[]{:T(128)}, bf16[16,512,128]{2,1,0:T(8,128)(2,1)}, s32[16,512]{1,0:T(8,128)}, bf16[512,128]{1,0:T(8,128)(2,1)S(1)}, s32[]{:T(128)}) while((s32[]{:T(128)}, bf16[16,512,128]{2,1,0:T(8,128)(2,1)}, s32[16,512]{1,0:T(8,128)}, bf16[512,128]{1,0:T(8,128)(2,1)S(1)}, s32[]{:T(128)}) %tuple.147), condition=%wide.region_11.12_spmd.clone, body=%wide.region_10.11_spmd.clone.sunk | while | flops 67436544 | bytes 268865 | solution.py:51
  326.9 6.9 %all-to-all-start.2 = ((bf16[64,128,128]{2,1,0:T(8,128)(2,1)}), bf16[64,128,128]{2,1,0:T(8,128)(2,1)S(1)}, u32[]{:S(2)}, u32[]{:S(2)}) async-start(bf16[64,128,128]{2,1,0:T(8,128)(2,1)} %bitcast.12), calls=%async_computation.2 | async-start | bytes 4194304 | tf_op jit(solution)/shard_map/all_to_all | solution.py:164
  341.0 44.1 %all-to-all-done.2 = bf16[64,128,128]{2,1,0:T(8,128)(2,1)S(1)} async-done(((bf16[64,128,128]{2,1,0:T(8,128)(2,1)}), bf16[64,128,128]{2,1,0:T(8,128)(2,1)S(1)}, u32[]{:S(2)}, u32[]{:S(2)}) %all-to-all-start.2) | async-done | bytes 2097184 | tf_op jit(solution)/shard_map/all_to_all | solution.py:164
  385.2 21.2 %while.72 = (s32[]{:T(128)}, f32[512,128]{1,0:T(8,128)S(1)}, s32[16,512]{1,0:T(8,128)}, bf16[16,512,128]{2,1,0:T(8,128)(2,1)S(1)}, s32[]{:T(128)}, /*index=5*/s32[]{:T(128)}) while((s32[]{:T(128)}, f32[512,128]{1,0:T(8,128)S(1)}, s32[16,512]{1,0:T(8,128)}, bf16[16,512,128]{2,1,0:T(8,128)(2,1)S(1)}, s32[]{:T(128)}, ...), condition=%wide.region_13.14_spmd.clone, body=%wide.region_12.13_spmd.clone.sunk | while | flops 67502080 | bytes 661591 | solution.py:73
  407.4 110.0 %all-reduce.3.cloned.1.call-done = (f32[64,256]{1,0:T(8,128)}, f32[64,256]{1,0:T(8,128)}) async-done(((f32[64,256]{1,0:T(8,128)}, f32[64,256]{1,0:T(8,128)}), (f32[64,256]{1,0:T(8,128)}, f32[64,256]{1,0:T(8,128)})) %all-reduce.3.cloned.1.call-update) | async-done | bytes 131088 | tf_op jit(solution)/shard_map/psum | solution.py:169
  517.4 142.8 %reduce-scatter.2.cloned.1.call-done = f32[32,64]{1,0:T(8,128)} async-done(((f32[2048,64]{1,0:T(8,128)}), f32[32,64]{1,0:T(8,128)}) %reduce-scatter.2.cloned.1.call-update) | async-done | bytes 8208 | tf_op jit(solution)/shard_map/reduce_scatter | solution.py:168
  (302 shorter events, 132.8 us)
Async XLA Ops:
  8.0 276.5 %copy-start = (bf16[256,256]{1,0:T(8,128)(2,1)S(1)}, bf16[256,256]{1,0:T(8,128)(2,1)}, u32[]{:S(2)}) copy-start(bf16[256,256]{1,0:T(8,128)(2,1)} %param.24) | copy-start | bytes 393220
  8.0 16.5 %sort.19.cloned.1.call-start = ((), (), s32[]{:S(2)}) async-start(), calls=%async_computation.7 | async-start | bytes 98336 | tf_op jit(solution)/shard_map/vmap(jit(argsort))/sort | solution.py:11
  9.4 15.9 %copy-start.1 = (s32[8,512,1]{1,0,2:T(8,128)S(1)}, s32[8,512,1]{1,0,2:T(8,128)}, u32[]{:S(2)}) copy-start(s32[8,512,1]{1,0,2:T(8,128)} %copy.81) | copy-start | bytes 49156
  25.3 25.5 %copy-start.8 = (s32[8,512]{1,0:T(8,128)S(1)}, s32[8,512]{1,0:T(8,128)}, u32[]{:S(2)}) copy-start(s32[8,512]{1,0:T(8,128)} %get-tuple-element.179) | copy-start | bytes 49156
  88.9 17.8 %copy-start.11 = (s32[2]{0:T(128)S(1)}, s32[2]{0:T(128)}, u32[]{:S(2)}) copy-start(s32[2]{0:T(128)} %constant.141) | copy-start | bytes 28
  88.9 17.9 %copy-start.10 = (s32[2]{0:T(128)S(1)}, s32[2]{0:T(128)}, u32[]{:S(2)}) copy-start(s32[2]{0:T(128)} %constant.144) | copy-start | bytes 28
  88.9 33.5 %copy-start.6 = (s32[8,512,1]{1,2,0:T(1,128)S(1)}, s32[8,512,1]{1,2,0:T(1,128)}, u32[]{:S(2)}) copy-start(s32[8,512,1]{1,2,0:T(1,128)} %param.20) | copy-start | bytes 49156
  138.7 20.0 %all-to-all-start = ((s32[64,1,128]{2,1,0:T(1,128)}), s32[64,1,128]{2,1,0:T(1,128)S(1)}, u32[]{:S(2)}, u32[]{:S(2)}) async-start(s32[64,1,128]{2,1,0:T(1,128)} %bitcast.4), calls=%async_computation | async-start | bytes 65536 | tf_op jit(solution)/shard_map/all_to_all | solution.py:115
  178.1 0.6 copy-start.4
  178.1 6.0 copy-start.9
  178.1 6.9 %copy-start.2 = (bf16[256,256]{1,0:T(8,128)(2,1)S(1)}, bf16[256,256]{1,0:T(8,128)(2,1)}, u32[]{:S(2)}) copy-start(bf16[256,256]{1,0:T(8,128)(2,1)} %param.23) | copy-start | bytes 393220
  178.7 56.5 %all-to-all-start.1 = ((bf16[64,128,128]{2,1,0:T(8,128)(2,1)}), bf16[64,128,128]{2,1,0:T(8,128)(2,1)S(1)}, u32[]{:S(2)}, u32[]{:S(2)}) async-start(bf16[64,128,128]{2,1,0:T(8,128)(2,1)} %bitcast.5), calls=%async_computation.1 | async-start | bytes 4194304 | tf_op jit(solution)/shard_map/all_to_all | solution.py:118
  183.4 87.2 %all-gather.2.cloned.1.call-start = ((), (), s32[]{:S(2)}) async-start(), calls=%async_computation.4 | async-start | bytes 1064960 | tf_op jit(solution)/shard_map/all_gather | solution.py:102
  245.1 0.6 copy-start.5
  270.6 13.9 %copy-start.12 = (bf16[256,128]{1,0:T(8,128)(2,1)S(1)}, bf16[256,128]{1,0:T(8,128)(2,1)}, u32[]{:S(2)}) copy-start(bf16[256,128]{1,0:T(8,128)(2,1)} %param.25) | copy-start | bytes 196612
  326.9 58.3 %all-to-all-start.2 = ((bf16[64,128,128]{2,1,0:T(8,128)(2,1)}), bf16[64,128,128]{2,1,0:T(8,128)(2,1)S(1)}, u32[]{:S(2)}, u32[]{:S(2)}) async-start(bf16[64,128,128]{2,1,0:T(8,128)(2,1)} %bitcast.12), calls=%async_computation.2 | async-start | bytes 4194304 | tf_op jit(solution)/shard_map/all_to_all | solution.py:164
  333.8 183.6 %all-reduce.3.cloned.1.call-start = ((), (), s32[]{:S(2)}) async-start(), calls=%async_computation.6 | async-start | bytes 262144 | tf_op jit(solution)/shard_map/psum | solution.py:169
  337.4 322.9 %reduce-scatter.2.cloned.1.call-start = ((), (), s32[]{:S(2)}) async-start(), calls=%async_computation.5 | async-start | bytes 1064960 | tf_op jit(solution)/shard_map/reduce_scatter | solution.py:168
  340.6 44.5 %copy-start.7 = (f32[512,128]{1,0:T(8,128)S(1)}, f32[512,128]{1,0:T(8,128)}, u32[]{:S(2)}) copy-start(f32[512,128]{1,0:T(8,128)} %custom-call.9) | copy-start | bytes 786436
  341.0 65.5 %copy-start.3 = (bf16[256,256]{1,0:T(8,128)(2,1)S(1)}, bf16[256,256]{1,0:T(8,128)(2,1)}, u32[]{:S(2)}) copy-start(bf16[256,256]{1,0:T(8,128)(2,1)} %param.23) | copy-start | bytes 393220
Sparse Core Ops, SparseCore 0:
  11.8 2.7 sort.21.cloned.1.call-done
  (1 shorter events, 0.0 us)
Sparse Core Ops, SparseCore 1:
  186.6 83.9 all-gather.1
  338.4 179.0 all-reduce.2
  521.8 138.3 reduce-scatter.1
where the time goes:
time: 674 us; the launch traced here: 671 us
  waiting for transfers between devices  366 us (54%)
  local copies, waits for them, and re-layouts  166 us (25%)
  matrix products  61.3 us (9%)
  blocking collectives  35.3 us (5%)
  starting transfers between devices  22.3 us (3%)
  between operations  16.2 us (2%)
    reduce_scatter x1, waiting for transfers between devices, body(): lax.psum_scatter(hub_grad_part, 'dom', scatter_dimension=0, tiled=True)  143 us
    psum x1, waiting for transfers between devices, body(): grad_self, grad_nbr = lax.psum((grad_self_part, grad_nbr_part), 'dom')  110 us
    all_to_all x1, waiting for transfers between devices, body(): lax.all_to_all(payload, 'dom', split_axis=0, concat_axis=0, tiled=True)  44.1 us
    gather x20, local copies, waits for them, and re-layouts, rank_level(): jnp.searchsorted(ordered, jnp.arange(peer_count, dtype=jnp.int32), side='...  36.6 us
    all_to_all x1, waiting for transfers between devices, body(): lax.all_to_all(served, 'dom', split_axis=0, concat_axis=0, tiled=True)  34.3 us
    dot_general x32, matrix products, one_block(): jnp.dot(selector, table, preferred_element_type=jnp.float32)  32.4 us
    gather x3, local copies, waits for them, and re-layouts, rank_level(): ordered = owner_row[ordering]  25.5 us
    all_gather x1, waiting for transfers between devices, body(): hub_table = lax.all_gather(hub_feats, 'dom', axis=0, tiled=True)  24.7 us
  transfers between devices with their start and end apart: 6, of which 6 were waited for; matrix products, arithmetic and copies ran while one was open for 8% of the time, Pallas kernels for 0%

commit v1 on v0

v1 whole, which is shorter than its diff:
```python
import functools

import jax
import jax.numpy as jnp
from jax import lax
from jax.experimental import pallas as pl
from jax.experimental.pallas import tpu as pltpu
from jax.sharding import Mesh, PartitionSpec as P

NY, NZ, NC, NX = 4, 8, 2, 4
V = 512
HALF = 256
COLS = 128
PLANE = NY * NC * V
HUB_ROWS = 16
BLOCK = HALF + HUB_ROWS
BF = jnp.bfloat16
F32 = jnp.float32


def shift(x, axis, size, step):
    return lax.ppermute(x, axis, [(i, (i + step) % size) for i in range(size)])


def swap(x, axis, size, mask):
    return lax.ppermute(x, axis, [(i, i ^ mask) for i in range(size)])


def count_kernel(place, ids_ref, out_ref, *, first):
    delta = pl.program_id(0) + first
    owner = place[0] * (NZ * NC) + ((place[1] + delta) % NZ) * NC + place[2]
    parity = place[3] // 2
    rows = lax.broadcasted_iota(jnp.int32, (16, 16, 128), 0) * 16 + lax.broadcasted_iota(
        jnp.int32, (16, 16, 128), 1
    )
    rows = rows.astype(F32).astype(BF)

    def multiplicity(keys):
        total = jnp.zeros(keys.shape, F32)
        for k in range(keys.shape[0]):
            total = total + (keys == keys[k : k + 1]).astype(F32)
        return total

    def spread(row):
        return jnp.broadcast_to(row, (16, 128)).astype(BF)

    def tile(index, carry):
        part = index // 4
        lane = pl.multiple_of((index % 4) * 128, 128)
        ids = ids_ref[part, :, pl.ds(lane, 128)]
        flat = ids[0:8]
        row = flat % V
        mine = (flat // V == owner) & (row % 2 == parity)
        keys = jnp.where(mine, row // 2, -1).astype(F32)
        times = multiplicity(keys)
        block = jnp.zeros((16, 16, 128), BF)
        for k in range(8):
            block = jnp.where(spread(keys[k : k + 1])[None] == rows, spread(times[k : k + 1])[None], block)
        dest = pl.ds(pl.multiple_of(index * 128, 128), 128)
        out_ref[0, 0:HALF, dest] = block.reshape(HALF, 128)
        hub = ids[8:16]
        hub_row = hub % (2 * HUB_ROWS)
        here = hub // (2 * HUB_ROWS) == owner
        for which in range(2):
            side = parity if which == 0 else 1 - parity
            hub_keys = jnp.where(here & (hub_row % 2 == side), hub_row // 2, -1).astype(F32)
            hub_times = multiplicity(hub_keys[0:4])
            hub_block = jnp.zeros((16, 128), BF)
            for j in range(4):
                hub_block = jnp.where(
                    spread(hub_keys[j : j + 1]) == rows[0], spread(hub_times[j : j + 1]), hub_block
                )
            start = HALF + which * HUB_ROWS
            out_ref[0, start : start + HUB_ROWS, dest] = hub_block
        return carry

    lax.fori_loop(0, PLANE // 128, tile, 0)


def counts_of(ids, place, first, number):
    rows = HALF + 2 * HUB_ROWS
    return pl.pallas_call(
        functools.partial(count_kernel, first=first),
        out_shape=jax.ShapeDtypeStruct((number, rows, PLANE), BF),
        grid_spec=pltpu.PrefetchScalarGridSpec(
            num_scalar_prefetch=1,
            grid=(number,),
            in_specs=[pl.BlockSpec((NY * NC, 16, V), lambda d, s: (0, 0, 0))],
            out_specs=pl.BlockSpec((1, rows, PLANE), lambda d, s: (d, 0, 0)),
        ),
        compiler_params=pltpu.CompilerParams(vmem_limit_bytes=24 << 20),
        cost_estimate=pl.CostEstimate(
            flops=number * rows * PLANE * 16, bytes_accessed=number * rows * PLANE * 2, transcendentals=0
        ),
        name="counts",
    )(place, ids)


def dense_kernel(
    place, f0, f1, f2, f3, g0, g1, g2, g3, s0, s1, s2, s3, ws_ref, wn_ref,
    out_ref, grad_ref, self_ref, weight_ref,
    f_scr, g_scr, s_scr, o_scr, w_scr,
):
    x = place[3]
    parity, half = x // 2, x % 2
    for mask, (fr, gr, sr) in enumerate(((f0, g0, s0), (f1, g1, s1), (f2, g2, s2), (f3, g3, s3))):
        f_scr[x ^ mask] = fr[...]
        g_scr[x ^ mask] = gr[...]
        s_scr[x ^ mask] = sr[...]
    feats = jnp.concatenate(
        [jnp.concatenate([f_scr[0], f_scr[1]], 1), jnp.concatenate([f_scr[2], f_scr[3]], 1)], 0
    )
    cot = jnp.concatenate(
        [jnp.concatenate([g_scr[0], g_scr[1]], 1), jnp.concatenate([g_scr[2], g_scr[3]], 1)], 0
    ).astype(F32)
    mean_t = jnp.concatenate(
        [
            s_scr[0].astype(F32) + s_scr[2].astype(F32),
            s_scr[1].astype(F32) + s_scr[3].astype(F32),
        ],
        0,
    )
    mean_t = (mean_t / 12.0).astype(BF)
    ordered = lax.broadcasted_iota(jnp.int32, (V, V), 0)
    natural = lax.broadcasted_iota(jnp.int32, (V, V), 1)
    order = ((ordered % HALF) * 2 + ordered // HALF == natural).astype(F32).astype(BF)
    last = (((1,), (1,)), ((), ()))
    firsts = (((0,), (0,)), ((), ()))
    dot = functools.partial(lax.dot_general, preferred_element_type=F32)
    mean = dot(order, mean_t, last).astype(BF)
    w_self, w_nbr = ws_ref[...], wn_ref[...]
    plain = (((1,), (0,)), ((), ()))
    pre = dot(feats, w_self, plain) + dot(mean, w_nbr, plain)
    sig = jax.nn.sigmoid(pre)
    value = (pre * sig).astype(BF)
    grad_pre = (cot * sig * (1.0 + pre * (1.0 - sig))).astype(BF)
    for q in range(2):
        for h in range(2):
            o_scr[q * 2 + h] = value[q * HALF : (q + 1) * HALF, h * COLS : (h + 1) * COLS]
    out_ref[...] = o_scr[x]
    rows = pl.ds(pl.multiple_of(half * COLS, COLS), COLS)
    grad_mean = (dot(grad_pre, wn_ref[rows, :], last) / 12.0).astype(BF)
    grad_ref[...] = dot(order, grad_mean, firsts).astype(BF)
    own_self = dot(grad_pre, ws_ref[rows, :], last)
    self_ref[...] = jnp.where(parity == 0, own_self[0:HALF], own_self[HALF:V])
    w_scr[0] = dot(feats, grad_pre, firsts)
    w_scr[1] = dot(mean, grad_pre, firsts)
    quarter = pl.ds(pl.multiple_of(x * 64, 64), 64)
    for which in range(2):
        part = w_scr[which, quarter, :]
        for h in range(2):
            start = which * 128 + h * 64
            weight_ref[start : start + 64, :] = part[:, h * COLS : (h + 1) * COLS].astype(BF)


def dense(place, feats, cots, sums, w_self, w_nbr):
    vm = pl.BlockSpec(memory_space=pltpu.VMEM)
    return pl.pallas_call(
        dense_kernel,
        out_shape=(
            jax.ShapeDtypeStruct((HALF, COLS), BF),
            jax.ShapeDtypeStruct((V, COLS), BF),
            jax.ShapeDtypeStruct((HALF, COLS), F32),
            jax.ShapeDtypeStruct((256, COLS), BF),
        ),
        in_specs=[pl.BlockSpec(memory_space=pltpu.SMEM)] + [vm] * 14,
        out_specs=(vm, vm, vm, vm),
        scratch_shapes=[
            pltpu.VMEM((4, HALF, COLS), BF),
            pltpu.VMEM((4, HALF, COLS), BF),
            pltpu.VMEM((4, COLS, V), BF),
            pltpu.VMEM((4, HALF, COLS), BF),
            pltpu.VMEM((2, 256, 256), F32),
        ],
        compiler_params=pltpu.CompilerParams(vmem_limit_bytes=24 << 20),
        name="dense",
    )(place, *feats, *cots, *sums, w_self, w_nbr)


def final_kernel(
    place, self_ref, nbr0, nbr1, nbr2, hub0, hub1, hub2, w0, w1, w2, w3, w4, w5, w6, w7,
    feat_ref, hub_ref, gself_ref, gnbr_ref, w_scr,
):
    z = place[1]
    total = nbr0[...] + nbr1[...].astype(F32) + nbr2[...].astype(F32)
    feat_ref[...] = (self_ref[...] + total).astype(BF)
    hub_ref[...] = hub0[...].astype(F32) + hub1[...].astype(F32) + hub2[...].astype(F32)
    for step, ref in enumerate((w0, w1, w2, w3, w4, w5, w6, w7)):
        w_scr[(z + step) % NZ] = ref[...]
    weight = w_scr[0].astype(F32)
    for step in range(1, NZ):
        weight = weight + w_scr[step].astype(F32)
    gself_ref[...] = jnp.concatenate([weight[0:64], weight[64:128]], 1)
    gnbr_ref[...] = jnp.concatenate([weight[128:192], weight[192:256]], 1)


def final(place, self_term, nbrs, hubs, weights):
    vm = pl.BlockSpec(memory_space=pltpu.VMEM)
    return pl.pallas_call(
        final_kernel,
        out_shape=(
            jax.ShapeDtypeStruct((HALF, COLS), BF),
            jax.ShapeDtypeStruct((HUB_ROWS, COLS), F32),
            jax.ShapeDtypeStruct((64, 256), F32),
            jax.ShapeDtypeStruct((64, 256), F32),
        ),
        in_specs=[pl.BlockSpec(memory_space=pltpu.SMEM)] + [vm] * 15,
        out_specs=(vm, vm, vm, vm),
        scratch_shapes=[pltpu.VMEM((NZ, 256, COLS), BF)],
        name="last_sums",
    )(place, self_term, *nbrs, *hubs, *weights)


def body(features, hub_feats, nbr_owner, nbr_row, hub_ids, w_self, w_nbr, grad_out):
    y, z, c, x = (lax.axis_index(a) for a in ("y", "z", "c", "x"))
    parity, half = x // 2, x % 2
    place = jnp.stack([y, z, c, x]).astype(jnp.int32)

    flat = nbr_owner.reshape(8, V) * V + nbr_row
    ids = jnp.concatenate([flat, hub_ids.T, jnp.full((4, V), -1, jnp.int32)], 0)
    ids_y = jnp.stack([ids] + [swap(ids, "y", NY, m) for m in range(1, NY)])
    ids_plane = jnp.concatenate([ids_y, swap(ids_y, "c", NC, 1)], 0)

    hub_own = lax.dynamic_slice(
        lax.dynamic_index_in_dim(hub_feats.reshape(HUB_ROWS, 2, 256), parity, 1, keepdims=False),
        (0, half * COLS),
        (HUB_ROWS, COLS),
    )
    mine = jnp.concatenate([features, hub_own], 0)
    ahead, behind = [mine], [mine]
    for step in range(4):
        ahead.append(shift(ahead[-1], "z", NZ, -1))
        if step < 3:
            behind.append(shift(behind[-1], "z", NZ, 1))
    tables = ahead + behind[:0:-1]

    counts = counts_of(ids_plane, place, 0, NZ)
    firsts = (((0,), (0,)), ((), ()))
    table = jnp.stack(tables)
    part = lax.dot_general(
        table, counts[:, :BLOCK], (((0, 1), (0, 1)), ((), ())), preferred_element_type=F32
    )
    both = part[:, : PLANE // 2] + swap(part[:, PLANE // 2 :].astype(BF), "c", NC, 1).astype(F32)
    mine_sum = both[:, :V]
    for m in range(1, NY):
        mine_sum = mine_sum + swap(both[:, m * V : (m + 1) * V].astype(BF), "y", NY, m).astype(F32)
    mine_sum = mine_sum.astype(BF)

    feats = [features] + [swap(features, "x", NX, m) for m in range(1, NX)]
    cots = [grad_out] + [swap(grad_out, "x", NX, m) for m in range(1, NX)]
    sums = [mine_sum] + [swap(mine_sum, "x", NX, m) for m in range(1, NX)]
    outputs, grad_mean, self_term, weight = dense(place, feats, cots, sums, w_self, w_nbr)

    message = jnp.concatenate([grad_mean, weight], 0)
    got = [message] + [swap(message, "y", NY, m) for m in range(1, NY)]
    weight = (got[0][V:].astype(F32) + got[1][V:].astype(F32)) + (
        got[2][V:].astype(F32) + got[3][V:].astype(F32)
    )
    grads = jnp.concatenate([g[:V] for g in got], 0)
    message = jnp.concatenate([grads, weight.astype(BF)], 0)
    other = swap(message, "c", NC, 1)
    weight = (message[NY * V :].astype(F32) + other[NY * V :].astype(F32)).astype(BF)
    grads = jnp.concatenate([grads, other[: NY * V]], 0)

    lane = lax.broadcasted_iota(jnp.int32, (HUB_ROWS, COLS), 1)

    def term(delta):
        rows = jnp.dot(counts[delta], grads, preferred_element_type=F32)
        own = rows[HALF:BLOCK]
        rest = jnp.roll(rows[BLOCK:], 64, 1)
        hub = jnp.where((lane < 64) == (parity == 0), own, rest)
        return rows[:HALF], hub

    def cross(hub, step):
        pairs = []
        for a in range(NZ):
            for b in range(NX):
                target = {0: 0, 1: 2, 2: 1, 3: 3}[b]
                pairs.append((a * NX + b, ((a + step) % NZ) * NX + target))
        return lax.ppermute(hub, ("z", "x"), pairs)

    def travel(deltas, step):
        passing, seen = weight, []
        total, hub = term(deltas[0])
        for index in range(len(deltas)):
            pieces = [total.astype(BF), passing]
            final_hop = index == len(deltas) - 1
            if not final_hop:
                pieces.insert(1, hub.astype(BF))
            arrived = shift(jnp.concatenate(pieces, 0), "z", NZ, step)
            passing = arrived[-256:]
            seen.append(passing)
            if final_hop:
                return arrived[:HALF], cross(hub.astype(BF), step), seen
            more, more_hub = term(deltas[index + 1])
            total = arrived[:HALF].astype(F32) + more
            hub = arrived[HALF:BLOCK].astype(F32) + more_hub

    nbr_up, hub_up, seen_up = travel([4, 3, 2, 1], 1)
    nbr_down, hub_down, seen_down = travel([5, 6, 7], -1)
    nbr_here, hub_here = term(0)
    hub_here = cross(hub_here.astype(BF), 0)
    weights = [weight] + seen_down + seen_up[::-1]
    grad_features, hub_rows, grad_self, grad_nbr = final(
        place, self_term, (nbr_here, nbr_up, nbr_down), (hub_here, hub_up, hub_down), weights
    )
    return outputs, grad_features, hub_rows.reshape(2 * HUB_ROWS, 64), grad_self, grad_nbr


def solution(mesh):
    fine = Mesh(mesh.devices.reshape(NY, NZ, NC, NX), ("y", "z", "c", "x"))
    dom = ("y", "z", "c")
    in_specs = (
        P(dom, "x"),
        P(dom, None),
        P(None, dom, None),
        P(None, dom),
        P(dom, None),
        P(),
        P(),
        P(dom, "x"),
    )
    out_specs = (P(dom, "x"), P(dom, "x"), P(dom, "x"), P("x", None), P("x", None))
    return jax.shard_map(body, mesh=fine, in_specs=in_specs, out_specs=out_specs, check_vma=False)
```

time: 674 us -> 176 us (0.26)
  waiting for transfers between devices: 366 us -> 39.4 us
  local copies, waits for them, and re-layouts: 166 us -> 12.2 us
  starting transfers between devices: 22.3 us -> 62.2 us
  blocking collectives: 35.3 us -> 0 us
  matrix products: 61.3 us -> 27 us
  Pallas kernels: 0 us -> 27.5 us
  between operations: 16.2 us -> 1.29 us
    reduce_scatter x1 -> x0, waiting for transfers between devices: 143 us -> none  [body(): lax.psum_scatter(hub_grad_part, 'dom', scatter_dimension=0, tiled=True)]
    psum x1 -> x0, waiting for transfers between devices: 110 us -> none  [body(): grad_self, grad_nbr = lax.psum((grad_self_part, grad_nbr_part), 'dom')]
    all_to_all x3 -> x0, waiting for transfers between devices: 87.8 us -> none  [the longest x1 44.1 us: body(): lax.all_to_all(payload, 'dom', split_axis=0, concat_axis=0, tiled=True)]
    gather x25 -> x0, local copies, waits for them, and re-layouts: 79.8 us -> none  [the longest x20 36.6 us: rank_level(): jnp.searchsorted(ordered, jnp.arange(peer_count, dtype=jnp.int32), side='...]
    ppermute x0 -> x38, starting transfers between devices: none -> 62.2 us  [the longest x21 27.9 us: swap(): return lax.ppermute(x, axis, [(i, i ^ mask) for i in range(size)])]
    ppermute x0 -> x38, waiting for transfers between devices: none -> 39.4 us  [the longest x21 21.4 us: swap(): return lax.ppermute(x, axis, [(i, i ^ mask) for i in range(size)])]
    all_gather x3 -> x0, blocking collectives: 35.3 us -> none  [the longest x1 12.6 us: body(): lax.all_gather(features, 'feat', axis=1, tiled=True)]
    dot_general x72 -> x9, matrix products: 61.3 us -> 27 us  [the longest x8 19.5 us: term(): rows = jnp.dot(counts[delta], grads, preferred_element_type=F32)]
  transfers between devices with their start and end apart: 6 -> 38, of which waited for: 6 -> 15; matrix products, arithmetic and copies ran while one was open for 8% -> 3% of each run, Pallas kernels for 0% -> 13%
where the time goes in v1:
time: 176 us; the launch traced here: 174 us
  starting transfers between devices  62.2 us (35%)
  waiting for transfers between devices  39.4 us (22%)
  Pallas kernels  27.5 us (16%)
  matrix products  27 us (15%)
  local copies, waits for them, and re-layouts  12.2 us (7%)
  other arithmetic  4.92 us (3%)
    ppermute x21, starting transfers between devices, swap(): return lax.ppermute(x, axis, [(i, i ^ mask) for i in range(size)])  27.9 us
    ppermute x14, starting transfers between devices, shift(): return lax.ppermute(x, axis, [(i, (i + step) % size) for i in range(size)])  26.8 us
    pallas_call x1, Pallas kernels, counts_of(): pl.pallas_call(functools.partial(count_kernel, first=first), out_shape=ja...  23 us
    ppermute x21, waiting for transfers between devices, swap(): return lax.ppermute(x, axis, [(i, i ^ mask) for i in range(size)])  21.4 us
    dot_general x8, matrix products, term(): rows = jnp.dot(counts[delta], grads, preferred_element_type=F32)  19.5 us
    ppermute x14, waiting for transfers between devices, shift(): return lax.ppermute(x, axis, [(i, (i + step) % size) for i in range(size)])  17.8 us
    dot_general x1, matrix products, body(): lax.dot_general(table, counts[:, :BLOCK], (((0, 1), (0, 1)), ((), ())), p...  7.57 us
    ppermute x3, starting transfers between devices, cross(): return lax.ppermute(hub, ('z', 'x'), pairs)  7.48 us
  transfers between devices with their start and end apart: 38, of which 15 were waited for; matrix products, arithmetic and copies ran while one was open for 3% of the time, Pallas kernels for 13%

profile of v1, /device:TPU:4, one launch (start us, length us, event | category | flops | bytes accessed | tf_op | source)
XLA Modules:
  0.0 174.5 jit_solution(670692558769288903)
XLA Ops:
  2.4 5.9 %collective-permute-start.6 = (bf16[272,128]{1,0:T(8,128)(2,1)S(1)}, bf16[272,128]{1,0:T(8,128)(2,1)S(1)}, u32[]{:S(2)}, u32[]{:S(2)}) collective-permute-start(bf16[272,128]{1,0:T(8,128)(2,1)S(1)} %pad_maximum_fusion.7), channel_id=1, source_target_pairs={{0,56},{8,0},{16,8},{24,16},{32,24},{40,32},{48,40},{56,48},{1,57}... | collective-permute-start | bytes 208904 | tf_op jit(solution)/shard_map/ppermute | solution.py:22
  11.4 2.9 %collective-permute-start.14 = (s32[16,512]{1,0:T(8,128)S(1)}, s32[16,512]{1,0:T(8,128)S(1)}, u32[]{:S(2)}, u32[]{:S(2)}) collective-permute-start(s32[16,512]{1,0:T(8,128)S(1)} %get-tuple-element.60), channel_id=1, source_target_pairs={{0,128},{64,192},{128,0},{192,64},{1,129},{65,193},{129,1},{193,65... | collective-permute-start | bytes 98312 | tf_op jit(solution)/shard_map/ppermute | solution.py:26
  16.8 2.6 %collective-permute-done.15 = s32[16,512]{1,0:T(8,128)S(1)} collective-permute-done((s32[16,512]{1,0:T(8,128)S(1)}, s32[16,512]{1,0:T(8,128)S(1)}, u32[]{:S(2)}, u32[]{:S(2)}) %collective-permute-start.15) | collective-permute-done | bytes 32800 | tf_op jit(solution)/shard_map/ppermute | solution.py:26
  19.6 3.3 %collective-permute-start.7 = (bf16[272,128]{1,0:T(8,128)(2,1)S(1)}, bf16[272,128]{1,0:T(8,128)(2,1)S(1)}, u32[]{:S(2)}, u32[]{:S(2)}) collective-permute-start(bf16[272,128]{1,0:T(8,128)(2,1)S(1)} %collective-permute-done.6), channel_id=1, source_target_pairs={{0,56},{8,0},{16,8},{24,16},{32,24},{40,32},{48,40},{56,48},{1,57}... | collective-permute-start | bytes 208904 | tf_op jit(solution)/shard_map/ppermute | solution.py:22
  25.0 3.7 %collective-permute-start.8 = (bf16[272,128]{1,0:T(8,128)(2,1)S(1)}, bf16[272,128]{1,0:T(8,128)(2,1)S(1)}, u32[]{:S(2)}, u32[]{:S(2)}) collective-permute-start(bf16[272,128]{1,0:T(8,128)(2,1)S(1)} %collective-permute-done.7), channel_id=1, source_target_pairs={{0,56},{8,0},{16,8},{24,16},{32,24},{40,32},{48,40},{56,48},{1,57}... | collective-permute-start | bytes 208904 | tf_op jit(solution)/shard_map/ppermute | solution.py:22
  28.7 23.0 %counts.1 = bf16[8,288,4096]{2,1,0:T(8,128)(2,1)S(1)} custom-call(s32[4]{0:T(128)S(1)} %pad_add_fusion.1.place, s32[8,16,512]{2,1,0:T(8,128)S(1)} %constant_dynamic-update-slice_fusion.ids_ref), custom_call_target="tpu_custom_call" | custom-call | flops 150994944 | bytes 18874368 | tf_op jit(solution)/shard_map/counts/pallas_call | solution.py:82
  51.7 6.4 %copy-done = bf16[8,288,4096]{2,1,0:T(8,128)(2,1)} copy-done((bf16[8,288,4096]{2,1,0:T(8,128)(2,1)}, bf16[8,288,4096]{2,1,0:T(8,128)(2,1)S(1)}, u32[]{:S(2)}) %copy-start) | copy-done | bytes 18874392
  58.2 3.3 %collective-permute-start.9 = (bf16[272,128]{1,0:T(8,128)(2,1)S(1)}, bf16[272,128]{1,0:T(8,128)(2,1)S(1)}, u32[]{:S(2)}, u32[]{:S(2)}) collective-permute-start(bf16[272,128]{1,0:T(8,128)(2,1)S(1)} %collective-permute-done.8), channel_id=1, source_target_pairs={{0,56},{8,0},{16,8},{24,16},{32,24},{40,32},{48,40},{56,48},{1,57}... | collective-permute-start | bytes 208904 | tf_op jit(solution)/shard_map/ppermute | solution.py:22
  63.5 7.6 %fusion.2 = f32[128,4096]{1,0:T(8,128)S(1)} fusion(bf16[8,272,128]{2,1,0:T(8,128)(2,1)S(1)} %bitcast_dynamic-update-slice_fusion, bf16[8,288,4096]{2,1,0:T(8,128)(2,1)} %copy-done), kind=kOutput, calls=%fused_computation.2 | convolution fusion | flops 2281701376 | bytes 20480000 | tf_op jit(solution)/shard_map/dot_general | solution.py:240
  75.1 3.0 %collective-permute-start.20 = (bf16[128,512]{1,0:T(8,128)(2,1)S(1)}, bf16[128,512]{1,0:T(8,128)(2,1)S(1)}, u32[]{:S(2)}, u32[]{:S(2)}) collective-permute-start(bf16[128,512]{1,0:T(8,128)(2,1)S(1)} %get-tuple-element.26), channel_id=1, source_target_pairs={{0,192},{64,128},{128,64},{192,0},{1,193},{65,129},{129,65},{193,1... | collective-permute-start | bytes 393224 | tf_op jit(solution)/shard_map/ppermute | solution.py:26
  93.5 2.4 %collective-permute-done.5.g3 = bf16[256,128]{1,0:T(8,128)(2,1)S(1)} collective-permute-done((bf16[256,128]{1,0:T(8,128)(2,1)S(1)}, bf16[256,128]{1,0:T(8,128)(2,1)S(1)}, u32[]{:S(2)}, u32[]{:S(2)}) %collective-permute-start.5) | collective-permute-done | bytes 65568 | tf_op jit(solution)/shard_map/ppermute | solution.py:26
  96.0 2.5 %dense.1 = (bf16[256,128]{1,0:T(8,128)(2,1)}, bf16[512,128]{1,0:T(8,128)(2,1)S(1)}, f32[256,128]{1,0:T(8,128)S(1)}, bf16[256,128]{1,0:T(8,128)(2,1)S(1)}) custom-call(s32[4]{0:T(128)S(1)} %pad_add_fusion.1.place, bf16[256,128]{1,0:T(8,128)(2,1)S(1)} %copy-done.1, bf16[256,128]{1,0:T(8,128)(2,1)S(1)} %collective-permute-done.f1, ...), custom_call_target="tpu_custom_call" | custom-call | tf_op jit(solution)/shard_map/dense/pallas_call | solution.py:158
  98.6 4.4 %collective-permute-start.25 = (bf16[768,128]{1,0:T(8,128)(2,1)S(1)}, bf16[768,128]{1,0:T(8,128)(2,1)S(1)}, u32[]{:S(2)}, u32[]{:S(2)}) collective-permute-start(bf16[768,128]{1,0:T(8,128)(2,1)S(1)} %constant_dynamic-update-slice_fusion.5), channel_id=1, source_target_pairs={{0,128},{64,192},{128,0},{192,64},{1,129},{65,193},{129,1},{193,65... | collective-permute-start | bytes 589832 | tf_op jit(solution)/shard_map/ppermute | solution.py:26
  103.3 3.0 %collective-permute-done.24 = bf16[768,128]{1,0:T(8,128)(2,1)S(1)} collective-permute-done((bf16[768,128]{1,0:T(8,128)(2,1)S(1)}, bf16[768,128]{1,0:T(8,128)(2,1)S(1)}, u32[]{:S(2)}, u32[]{:S(2)}) %collective-permute-start.24) | collective-permute-done | bytes 196640 | tf_op jit(solution)/shard_map/ppermute | solution.py:26
  106.3 4.5 %collective-permute-done.25 = bf16[768,128]{1,0:T(8,128)(2,1)S(1)} collective-permute-done((bf16[768,128]{1,0:T(8,128)(2,1)S(1)}, bf16[768,128]{1,0:T(8,128)(2,1)S(1)}, u32[]{:S(2)}, u32[]{:S(2)}) %collective-permute-start.25) | collective-permute-done | bytes 196640 | tf_op jit(solution)/shard_map/ppermute | solution.py:26
  122.9 2.4 %fusion.11 = bf16[288,128]{1,0:T(8,128)(2,1)S(1)} fusion(bf16[4096,128]{1,0:T(8,128)(2,1)S(1)} %slice_dynamic-update-slice_fusion, bf16[8,288,4096]{2,1,0:T(8,128)(2,1)} %copy-done), kind=kOutput, calls=%fused_computation.16 | convolution fusion | flops 301989888 | bytes 3481600 | tf_op jit(solution)/shard_map/dot_general | solution.py:268
  136.3 3.7 %collective-permute-start.32 = (bf16[528,128]{1,0:T(8,128)(2,1)S(1)}, bf16[528,128]{1,0:T(8,128)(2,1)S(1)}, u32[]{:S(2)}, u32[]{:S(2)}) collective-permute-start(bf16[528,128]{1,0:T(8,128)(2,1)S(1)} %get-tuple-element.57), channel_id=1, source_target_pairs={{0,56},{8,0},{16,8},{24,16},{32,24},{40,32},{48,40},{56,48},{1,57}... | collective-permute-start | bytes 405512 | tf_op jit(solution)/shard_map/ppermute | solution.py:22
  140.0 3.8 %collective-permute-start.35 = (bf16[16,128]{1,0:T(8,128)(2,1)S(1)}, bf16[16,128]{1,0:T(8,128)(2,1)S(1)}, u32[]{:S(2)}, u32[]{:S(2)}) collective-permute-start(bf16[16,128]{1,0:T(8,128)(2,1)S(1)} %get-tuple-element.63), channel_id=1, source_target_pairs={{0,0},{1,2},{2,1},{3,3},{8,8},{9,10},{10,9},{11,11},{16,16},{17,18... | collective-permute-start | bytes 12296 | tf_op jit(solution)/shard_map/ppermute | solution.py:280
  144.1 2.9 %collective-permute-start.33 = (bf16[528,128]{1,0:T(8,128)(2,1)S(1)}, bf16[528,128]{1,0:T(8,128)(2,1)S(1)}, u32[]{:S(2)}, u32[]{:S(2)}) collective-permute-start(bf16[528,128]{1,0:T(8,128)(2,1)S(1)} %pad_maximum_fusion.4), channel_id=1, source_target_pairs={{0,56},{8,0},{16,8},{24,16},{32,24},{40,32},{48,40},{56,48},{1,57}... | collective-permute-start | bytes 405512 | tf_op jit(solution)/shard_map/ppermute | solution.py:22
  147.0 2.5 %collective-permute-done.33 = bf16[528,128]{1,0:T(8,128)(2,1)S(1)} collective-permute-done((bf16[528,128]{1,0:T(8,128)(2,1)S(1)}, bf16[528,128]{1,0:T(8,128)(2,1)S(1)}, u32[]{:S(2)}, u32[]{:S(2)}) %collective-permute-start.33) | collective-permute-done | bytes 135200 | tf_op jit(solution)/shard_map/ppermute | solution.py:22
  149.8 3.7 %collective-permute-start.34 = (bf16[512,128]{1,0:T(8,128)(2,1)S(1)}, bf16[512,128]{1,0:T(8,128)(2,1)S(1)}, u32[]{:S(2)}, u32[]{:S(2)}) collective-permute-start(bf16[512,128]{1,0:T(8,128)(2,1)S(1)} %pad_maximum_fusion.6), channel_id=1, source_target_pairs={{0,56},{8,0},{16,8},{24,16},{32,24},{40,32},{48,40},{56,48},{1,57}... | collective-permute-start | bytes 393224 | tf_op jit(solution)/shard_map/ppermute | solution.py:22
  153.5 3.3 %collective-permute-start.37 = (bf16[16,128]{1,0:T(8,128)(2,1)S(1)}, bf16[16,128]{1,0:T(8,128)(2,1)S(1)}, u32[]{:S(2)}, u32[]{:S(2)}) collective-permute-start(bf16[16,128]{1,0:T(8,128)(2,1)S(1)} %get-tuple-element.61), channel_id=1, source_target_pairs={{0,56},{1,58},{2,57},{3,59},{8,0},{9,2},{10,1},{11,3},{16,8},{17,1... | collective-permute-start | bytes 12296 | tf_op jit(solution)/shard_map/ppermute | solution.py:280
  157.7 5.5 %collective-permute-done.30 = bf16[528,128]{1,0:T(8,128)(2,1)S(1)} collective-permute-done((bf16[528,128]{1,0:T(8,128)(2,1)S(1)}, bf16[528,128]{1,0:T(8,128)(2,1)S(1)}, u32[]{:S(2)}, u32[]{:S(2)}) %collective-permute-start.30) | collective-permute-done | bytes 135200 | tf_op jit(solution)/shard_map/ppermute | solution.py:22
  163.9 5.7 %collective-permute-done.31 = bf16[512,128]{1,0:T(8,128)(2,1)S(1)} collective-permute-done((bf16[512,128]{1,0:T(8,128)(2,1)S(1)}, bf16[512,128]{1,0:T(8,128)(2,1)S(1)}, u32[]{:S(2)}, u32[]{:S(2)}) %collective-permute-start.31) | collective-permute-done | bytes 131104 | tf_op jit(solution)/shard_map/ppermute | solution.py:22
  (165 shorter events, 61.1 us)
Async XLA Ops:
  2.4 17.2 %collective-permute-start.6 = (bf16[272,128]{1,0:T(8,128)(2,1)S(1)}, bf16[272,128]{1,0:T(8,128)(2,1)S(1)}, u32[]{:S(2)}, u32[]{:S(2)}) collective-permute-start(bf16[272,128]{1,0:T(8,128)(2,1)S(1)} %pad_maximum_fusion.7), channel_id=1, source_target_pairs={{0,56},{8,0},{16,8},{24,16},{32,24},{40,32},{48,40},{56,48},{1,57}... | collective-permute-start | bytes 208904 | tf_op jit(solution)/shard_map/ppermute | solution.py:22
  8.2 14.7 %collective-permute-start.10 = (bf16[272,128]{1,0:T(8,128)(2,1)S(1)}, bf16[272,128]{1,0:T(8,128)(2,1)S(1)}, u32[]{:S(2)}, u32[]{:S(2)}) collective-permute-start(bf16[272,128]{1,0:T(8,128)(2,1)S(1)} %pad_maximum_fusion.7), channel_id=1, source_target_pairs={{0,8},{8,16},{16,24},{24,32},{32,40},{40,48},{48,56},{56,0},{1,9},... | collective-permute-start | bytes 208904 | tf_op jit(solution)/shard_map/ppermute | solution.py:22
  19.4 9.3 %collective-permute-start.16 = (s32[4,16,512]{2,1,0:T(8,128)S(1)}, s32[4,16,512]{2,1,0:T(8,128)S(1)}, u32[]{:S(2)}, u32[]{:S(2)}) collective-permute-start(s32[4,16,512]{2,1,0:T(8,128)S(1)} %pad_add_fusion), channel_id=1, source_target_pairs={{0,4},{4,0},{1,5},{5,1},{2,6},{6,2},{3,7},{7,3},{8,12},{12,8},{9,1... | collective-permute-start | bytes 393224 | tf_op jit(solution)/shard_map/ppermute | solution.py:26
  25.0 33.1 %collective-permute-start.8 = (bf16[272,128]{1,0:T(8,128)(2,1)S(1)}, bf16[272,128]{1,0:T(8,128)(2,1)S(1)}, u32[]{:S(2)}, u32[]{:S(2)}) collective-permute-start(bf16[272,128]{1,0:T(8,128)(2,1)S(1)} %collective-permute-done.7), channel_id=1, source_target_pairs={{0,56},{8,0},{16,8},{24,16},{32,24},{40,32},{48,40},{56,48},{1,57}... | collective-permute-start | bytes 208904 | tf_op jit(solution)/shard_map/ppermute | solution.py:22
  28.7 34.7 %collective-permute-start.12 = (bf16[272,128]{1,0:T(8,128)(2,1)S(1)}, bf16[272,128]{1,0:T(8,128)(2,1)S(1)}, u32[]{:S(2)}, u32[]{:S(2)}) collective-permute-start(bf16[272,128]{1,0:T(8,128)(2,1)S(1)} %collective-permute-done.11), channel_id=1, source_target_pairs={{0,8},{8,16},{16,24},{24,32},{32,40},{40,48},{48,56},{56,0},{1,9},... | collective-permute-start | bytes 208904 | tf_op jit(solution)/shard_map/ppermute | solution.py:22
  73.3 6.8 %collective-permute-start.18 = (bf16[128,512]{1,0:T(8,128)(2,1)S(1)}, bf16[128,512]{1,0:T(8,128)(2,1)S(1)}, u32[]{:S(2)}, u32[]{:S(2)}) collective-permute-start(bf16[128,512]{1,0:T(8,128)(2,1)S(1)} %get-tuple-element.25), channel_id=1, source_target_pairs={{0,64},{64,0},{128,192},{192,128},{1,65},{65,1},{129,193},{193,129... | collective-permute-start | bytes 393224 | tf_op jit(solution)/shard_map/ppermute | solution.py:26
  73.4 8.2 %collective-permute-start.19 = (bf16[128,512]{1,0:T(8,128)(2,1)S(1)}, bf16[128,512]{1,0:T(8,128)(2,1)S(1)}, u32[]{:S(2)}, u32[]{:S(2)}) collective-permute-start(bf16[128,512]{1,0:T(8,128)(2,1)S(1)} %get-tuple-element.27), channel_id=1, source_target_pairs={{0,128},{64,192},{128,0},{192,64},{1,129},{65,193},{129,1},{193,65... | collective-permute-start | bytes 393224 | tf_op jit(solution)/shard_map/ppermute | solution.py:26
  75.1 8.9 %collective-permute-start.20 = (bf16[128,512]{1,0:T(8,128)(2,1)S(1)}, bf16[128,512]{1,0:T(8,128)(2,1)S(1)}, u32[]{:S(2)}, u32[]{:S(2)}) collective-permute-start(bf16[128,512]{1,0:T(8,128)(2,1)S(1)} %get-tuple-element.26), channel_id=1, source_target_pairs={{0,192},{64,128},{128,64},{192,0},{1,193},{65,129},{129,65},{193,1... | collective-permute-start | bytes 393224 | tf_op jit(solution)/shard_map/ppermute | solution.py:26
  78.1 7.0 %collective-permute-start = (bf16[256,128]{1,0:T(8,128)(2,1)S(1)}, bf16[256,128]{1,0:T(8,128)(2,1)S(1)}, u32[]{:S(2)}, u32[]{:S(2)}) collective-permute-start(bf16[256,128]{1,0:T(8,128)(2,1)S(1)} %copy-done.1), channel_id=1, source_target_pairs={{0,1},{1,0},{2,3},{3,2},{4,5},{5,4},{6,7},{7,6},{8,9},{9,8},{10,11... | collective-permute-start | bytes 196616 | tf_op jit(solution)/shard_map/ppermute | solution.py:26
  80.1 7.6 %collective-permute-start.2 = (bf16[256,128]{1,0:T(8,128)(2,1)S(1)}, bf16[256,128]{1,0:T(8,128)(2,1)S(1)}, u32[]{:S(2)}, u32[]{:S(2)}) collective-permute-start(bf16[256,128]{1,0:T(8,128)(2,1)S(1)} %copy-done.1), channel_id=1, source_target_pairs={{0,3},{1,2},{2,1},{3,0},{4,7},{5,6},{6,5},{7,4},{8,11},{9,10},{10,... | collective-permute-start | bytes 196616 | tf_op jit(solution)/shard_map/ppermute | solution.py:26
  81.6 7.5 %collective-permute-start.3 = (bf16[256,128]{1,0:T(8,128)(2,1)S(1)}, bf16[256,128]{1,0:T(8,128)(2,1)S(1)}, u32[]{:S(2)}, u32[]{:S(2)}) collective-permute-start(bf16[256,128]{1,0:T(8,128)(2,1)S(1)} %copy-done.5), channel_id=1, source_target_pairs={{0,1},{1,0},{2,3},{3,2},{4,5},{5,4},{6,7},{7,6},{8,9},{9,8},{10,11... | collective-permute-start | bytes 196616 | tf_op jit(solution)/shard_map/ppermute | solution.py:26
  84.1 11.9 %collective-permute-start.21 = (bf16[128,512]{1,0:T(8,128)(2,1)S(1)}, bf16[128,512]{1,0:T(8,128)(2,1)S(1)}, u32[]{:S(2)}, u32[]{:S(2)}) collective-permute-start(bf16[128,512]{1,0:T(8,128)(2,1)S(1)} %fusion.15.s0), channel_id=1, source_target_pairs={{0,1},{1,0},{2,3},{3,2},{4,5},{5,4},{6,7},{7,6},{8,9},{9,8},{10,11... | collective-permute-start | bytes 393224 | tf_op jit(solution)/shard_map/ppermute | solution.py:26
  85.1 10.8 %collective-permute-start.22 = (bf16[128,512]{1,0:T(8,128)(2,1)S(1)}, bf16[128,512]{1,0:T(8,128)(2,1)S(1)}, u32[]{:S(2)}, u32[]{:S(2)}) collective-permute-start(bf16[128,512]{1,0:T(8,128)(2,1)S(1)} %fusion.15.s0), channel_id=1, source_target_pairs={{0,2},{1,3},{2,0},{3,1},{4,6},{5,7},{6,4},{7,5},{8,10},{9,11},{10,... | collective-permute-start | bytes 393224 | tf_op jit(solution)/shard_map/ppermute | solution.py:26
  86.0 10.0 %collective-permute-start.23 = (bf16[128,512]{1,0:T(8,128)(2,1)S(1)}, bf16[128,512]{1,0:T(8,128)(2,1)S(1)}, u32[]{:S(2)}, u32[]{:S(2)}) collective-permute-start(bf16[128,512]{1,0:T(8,128)(2,1)S(1)} %fusion.15.s0), channel_id=1, source_target_pairs={{0,3},{1,2},{2,1},{3,0},{4,7},{5,6},{6,5},{7,4},{8,11},{9,10},{10,... | collective-permute-start | bytes 393224 | tf_op jit(solution)/shard_map/ppermute | solution.py:26
  98.5 7.8 %collective-permute-start.24 = (bf16[768,128]{1,0:T(8,128)(2,1)S(1)}, bf16[768,128]{1,0:T(8,128)(2,1)S(1)}, u32[]{:S(2)}, u32[]{:S(2)}) collective-permute-start(bf16[768,128]{1,0:T(8,128)(2,1)S(1)} %constant_dynamic-update-slice_fusion.5), channel_id=1, source_target_pairs={{0,64},{64,0},{128,192},{192,128},{1,65},{65,1},{129,193},{193,129... | collective-permute-start | bytes 589832 | tf_op jit(solution)/shard_map/ppermute | solution.py:26
  98.6 12.3 %collective-permute-start.25 = (bf16[768,128]{1,0:T(8,128)(2,1)S(1)}, bf16[768,128]{1,0:T(8,128)(2,1)S(1)}, u32[]{:S(2)}, u32[]{:S(2)}) collective-permute-start(bf16[768,128]{1,0:T(8,128)(2,1)S(1)} %constant_dynamic-update-slice_fusion.5), channel_id=1, source_target_pairs={{0,128},{64,192},{128,0},{192,64},{1,129},{65,193},{129,1},{193,65... | collective-permute-start | bytes 589832 | tf_op jit(solution)/shard_map/ppermute | solution.py:26
  103.0 10.1 %collective-permute-start.26 = (bf16[768,128]{1,0:T(8,128)(2,1)S(1)}, bf16[768,128]{1,0:T(8,128)(2,1)S(1)}, u32[]{:S(2)}, u32[]{:S(2)}) collective-permute-start(bf16[768,128]{1,0:T(8,128)(2,1)S(1)} %constant_dynamic-update-slice_fusion.5), channel_id=1, source_target_pairs={{0,192},{64,128},{128,64},{192,0},{1,193},{65,129},{129,65},{193,1... | collective-permute-start | bytes 589832 | tf_op jit(solution)/shard_map/ppermute | solution.py:26
  136.2 10.8 %collective-permute-start.28 = (bf16[528,128]{1,0:T(8,128)(2,1)S(1)}, bf16[528,128]{1,0:T(8,128)(2,1)S(1)}, u32[]{:S(2)}, u32[]{:S(2)}) collective-permute-start(bf16[528,128]{1,0:T(8,128)(2,1)S(1)} %get-tuple-element.58), channel_id=1, source_target_pairs={{0,8},{8,16},{16,24},{24,32},{32,40},{40,48},{48,56},{56,0},{1,9},... | collective-permute-start | bytes 405512 | tf_op jit(solution)/shard_map/ppermute | solution.py:22
  136.3 7.6 %collective-permute-start.32 = (bf16[528,128]{1,0:T(8,128)(2,1)S(1)}, bf16[528,128]{1,0:T(8,128)(2,1)S(1)}, u32[]{:S(2)}, u32[]{:S(2)}) collective-permute-start(bf16[528,128]{1,0:T(8,128)(2,1)S(1)} %get-tuple-element.57), channel_id=1, source_target_pairs={{0,56},{8,0},{16,8},{24,16},{32,24},{40,32},{48,40},{56,48},{1,57}... | collective-permute-start | bytes 405512 | tf_op jit(solution)/shard_map/ppermute | solution.py:22
  140.0 30.3 %collective-permute-start.35 = (bf16[16,128]{1,0:T(8,128)(2,1)S(1)}, bf16[16,128]{1,0:T(8,128)(2,1)S(1)}, u32[]{:S(2)}, u32[]{:S(2)}) collective-permute-start(bf16[16,128]{1,0:T(8,128)(2,1)S(1)} %get-tuple-element.63), channel_id=1, source_target_pairs={{0,0},{1,2},{2,1},{3,3},{8,8},{9,10},{10,9},{11,11},{16,16},{17,18... | collective-permute-start | bytes 12296 | tf_op jit(solution)/shard_map/ppermute | solution.py:280
  149.6 7.2 %collective-permute-start.29 = (bf16[528,128]{1,0:T(8,128)(2,1)S(1)}, bf16[528,128]{1,0:T(8,128)(2,1)S(1)}, u32[]{:S(2)}, u32[]{:S(2)}) collective-permute-start(bf16[528,128]{1,0:T(8,128)(2,1)S(1)} %pad_maximum_fusion.2), channel_id=1, source_target_pairs={{0,8},{8,16},{16,24},{24,32},{32,40},{40,48},{48,56},{56,0},{1,9},... | collective-permute-start | bytes 405512 | tf_op jit(solution)/shard_map/ppermute | solution.py:22
  149.8 7.3 %collective-permute-start.34 = (bf16[512,128]{1,0:T(8,128)(2,1)S(1)}, bf16[512,128]{1,0:T(8,128)(2,1)S(1)}, u32[]{:S(2)}, u32[]{:S(2)}) collective-permute-start(bf16[512,128]{1,0:T(8,128)(2,1)S(1)} %pad_maximum_fusion.6), channel_id=1, source_target_pairs={{0,56},{8,0},{16,8},{24,16},{32,24},{40,32},{48,40},{56,48},{1,57}... | collective-permute-start | bytes 393224 | tf_op jit(solution)/shard_map/ppermute | solution.py:22
  153.5 16.8 %collective-permute-start.37 = (bf16[16,128]{1,0:T(8,128)(2,1)S(1)}, bf16[16,128]{1,0:T(8,128)(2,1)S(1)}, u32[]{:S(2)}, u32[]{:S(2)}) collective-permute-start(bf16[16,128]{1,0:T(8,128)(2,1)S(1)} %get-tuple-element.61), channel_id=1, source_target_pairs={{0,56},{1,58},{2,57},{3,59},{8,0},{9,2},{10,1},{11,3},{16,8},{17,1... | collective-permute-start | bytes 12296 | tf_op jit(solution)/shard_map/ppermute | solution.py:280
  163.5 6.9 %collective-permute-start.36 = (bf16[16,128]{1,0:T(8,128)(2,1)S(1)}, bf16[16,128]{1,0:T(8,128)(2,1)S(1)}, u32[]{:S(2)}, u32[]{:S(2)}) collective-permute-start(bf16[16,128]{1,0:T(8,128)(2,1)S(1)} %fusion.24), channel_id=1, source_target_pairs={{0,8},{1,10},{2,9},{3,11},{8,16},{9,18},{10,17},{11,19},{16,24},{1... | collective-permute-start | bytes 12296 | tf_op jit(solution)/shard_map/ppermute | solution.py:280
  (30 other events, 422.5 us)

commit v2 on v1

v2 whole, which is shorter than its diff:
```python
import functools

import jax
import jax.numpy as jnp
from jax import lax
from jax.experimental import pallas as pl
from jax.experimental.pallas import tpu as pltpu
from jax.sharding import Mesh, PartitionSpec as P

NY, NZ, NC, NX = 4, 8, 2, 4
V = 512
HALF = 256
COLS = 128
HUB_ROWS = 16
BLOCK = HALF + HUB_ROWS
ROWS = (NZ + 1) * HALF
PARTS = NC * NY
WROWS = 256
DISTINCT = 4
BF = jnp.bfloat16
F32 = jnp.float32
VM = pl.BlockSpec(memory_space=pltpu.VMEM)
SM = pl.BlockSpec(memory_space=pltpu.SMEM)
PLAIN = (((1,), (0,)), ((), ()))
LAST = (((1,), (1,)), ((), ()))
FIRST = (((0,), (0,)), ((), ()))


def dot(a, b, dims=PLAIN, **kw):
    return lax.dot_general(a, b, dims, preferred_element_type=F32, **kw)


def shift(x, axis, size, step):
    return lax.ppermute(x, axis, [(i, (i + step) % size) for i in range(size)])


def swap(x, axis, size, mask):
    return lax.ppermute(x, axis, [(i, i ^ mask) for i in range(size)])


def call(kernel, outs, inputs, name, scratch=(), flops=0, mib=16):
    return pl.pallas_call(
        kernel,
        out_shape=outs,
        in_specs=[SM] + [VM] * (len(inputs) - 1),
        out_specs=jax.tree.map(lambda _: VM, outs),
        scratch_shapes=list(scratch),
        compiler_params=pltpu.CompilerParams(vmem_limit_bytes=mib << 20),
        cost_estimate=pl.CostEstimate(flops=flops, bytes_accessed=1 << 18, transcendentals=0),
        name=name,
    )(*inputs)


def shaped(shape, dtype):
    return jax.ShapeDtypeStruct(shape, dtype)


def prepare_kernel(place, feat_ref, cot_ref, hub_ref, owner_ref, row_ref, hub_id_ref, ids_ref, mine_ref, both_ref):
    parity, half = place[3] // 2, place[3] % 2
    ids_ref[0:8] = owner_ref[...] * V + row_ref[...]
    ids_ref[8:12] = hub_id_ref[...]
    ids_ref[12:16] = jnp.full((4, V), -1, jnp.int32)
    mine_ref[0:HALF] = feat_ref[...]
    pick = lax.broadcasted_iota(jnp.int32, (HUB_ROWS, 2 * HUB_ROWS), 1) == (
        2 * lax.broadcasted_iota(jnp.int32, (HUB_ROWS, 2 * HUB_ROWS), 0) + parity
    )
    columns = hub_ref[:, pl.ds(pl.multiple_of(half * COLS, COLS), COLS)]
    mine_ref[HALF:BLOCK] = dot(pick.astype(F32).astype(BF), columns).astype(BF)
    both_ref[0:HALF] = feat_ref[...]
    both_ref[HALF:V] = cot_ref[...]


def counts_kernel(place, ids0, ids1, ids2, ids3, out_ref):
    y, z, c, x = place[0], place[1], place[2], place[3]
    parity = x // 2
    rows = lax.broadcasted_iota(jnp.int32, (16, 16, 128), 0) * 16 + lax.broadcasted_iota(
        jnp.int32, (16, 16, 128), 1
    )
    rows = rows.astype(F32).astype(BF)
    level = lax.broadcasted_iota(jnp.int32, (8, V), 0)
    column = y * (NZ * NC) + c
    mask = (NY - 1) * (NZ * NC) + (NC - 1)

    def allmax(a):
        for s in (4, 2, 1):
            a = jnp.maximum(a, pltpu.roll(a, s, 0))
        return a

    def allsum(a):
        for s in (4, 2, 1):
            a = a + pltpu.roll(a, s, 0)
        return a

    def extract(keys):
        top = allmax(keys)
        hit = keys == top
        return jnp.where(hit, -1.0, keys), top, allsum(jnp.where(hit, 1.0, 0.0))

    def pair(a):
        return jnp.concatenate([a, a], 0).astype(BF)

    for dy, ids_ref in enumerate((ids0, ids1, ids2, ids3)):

        def part(dc, carry, dy=dy, ids_ref=ids_ref):
            index = dc * NY + dy
            ids = ids_ref[dc]
            flat, hub = ids[0:8], ids[8:16]
            here = ((flat >> 9) & mask) == column
            here = here & ((flat & 1) == parity)
            keys = jnp.where(here, (((flat >> 10) - z) & 7) * HALF + ((flat >> 1) & 255), -1).astype(F32)
            here = (((hub >> 5) & mask) == column) & (level < 4)
            hub_row = (((hub >> 6) - z) & 7) * 32 + ((hub & 1) ^ parity) * 16 + ((hub >> 1) & 15)
            hub_keys = jnp.where(here, hub_row, -1).astype(F32)
            found, hub_found = [], []
            for _ in range(DISTINCT):
                keys, top, times = extract(keys)
                found.append((top, pair(times)))
            for _ in range(4):
                hub_keys, top, times = extract(hub_keys)
                hub_found.append((pair(top), pair(times)))
            for tile in range(V // 128):
                lanes = slice(tile * 128, (tile + 1) * 128)
                for delta in range(NZ):
                    block = jnp.zeros((16, 16, 128), BF)
                    for top, times in found:
                        match = pair(top[:, lanes] - float(HALF * delta))[None] == rows
                        block = jnp.where(match, times[:, lanes][None], block)
                    out_ref[index, delta * HALF : (delta + 1) * HALF, lanes] = block.reshape(HALF, 128)
                block = jnp.zeros((16, 16, 128), BF)
                for top, times in hub_found:
                    block = jnp.where(top[:, lanes][None] == rows, times[:, lanes][None], block)
                out_ref[index, NZ * HALF : ROWS, lanes] = block.reshape(HALF, 128)

            @pl.when(jnp.max(keys) >= 0)
            def _():
                def more(_, keys):
                    keys, top, times = extract(keys)
                    for tile in range(V // 128):
                        lanes = slice(tile * 128, (tile + 1) * 128)
                        for delta in range(NZ):
                            span = slice(delta * HALF, (delta + 1) * HALF)
                            block = out_ref[index, span, lanes].reshape(16, 16, 128)
                            match = pair(top[:, lanes] - float(HALF * delta))[None] == rows
                            block = jnp.where(match, pair(times[:, lanes])[None], block)
                            out_ref[index, span, lanes] = block.reshape(HALF, 128)
                    return keys

                lax.fori_loop(0, 8 - DISTINCT, more, keys)

            return carry

        lax.fori_loop(0, NC, part, 0)


def far_sums_kernel(place, counts, t0, t1, t7, t23, t65, t4, sums_ref, turned_ref, table):
    blocks = {0: t0[...], 1: t1[...], 7: t7[...], 4: t4[...]}
    blocks[2], blocks[3] = t23[0:BLOCK], t23[BLOCK : 2 * BLOCK]
    blocks[6], blocks[5] = t65[0:BLOCK], t65[BLOCK : 2 * BLOCK]
    for delta in range(NZ):
        table[delta * HALF : (delta + 1) * HALF] = blocks[delta][0:HALF]
        start = NZ * HALF + delta * 2 * HUB_ROWS
        table[start : start + HUB_ROWS] = blocks[delta][HALF:BLOCK]
        table[start + HUB_ROWS : start + 2 * HUB_ROWS] = jnp.zeros((HUB_ROWS, COLS), BF)
    turned_ref[...] = table[...].T

    def step(dy, carry):
        sums_ref[dy] = dot(turned_ref[...], counts[NY + dy]).astype(BF)
        return carry

    lax.fori_loop(0, NY, step, 0)


def near_sums_kernel(place, counts, turned, sums_ref):
    def step(dy, carry):
        sums_ref[dy] = dot(turned[...], counts[dy])
        return carry

    lax.fori_loop(0, NY, step, 0)


def dense_kernel(
    place, fg0, fg1, fg23, s0, s1, s2, s3, ws_ref, wn_ref,
    out_ref, message_ref, self_ref,
    f_scr, g_scr, s_scr, o_scr, w_scr,
):
    x = place[3]
    parity, half = x // 2, x % 2
    sources = ((fg0, 0), (fg1, 0), (fg23, 0), (fg23, V))
    for mask, ((ref, start), sr) in enumerate(zip(sources, (s0, s1, s2, s3))):
        f_scr[x ^ mask] = ref[start : start + HALF]
        g_scr[x ^ mask] = ref[start + HALF : start + V]
        s_scr[x ^ mask] = sr[...]
    feats = jnp.concatenate(
        [jnp.concatenate([f_scr[0], f_scr[1]], 1), jnp.concatenate([f_scr[2], f_scr[3]], 1)], 0
    )
    cot = jnp.concatenate(
        [jnp.concatenate([g_scr[0], g_scr[1]], 1), jnp.concatenate([g_scr[2], g_scr[3]], 1)], 0
    ).astype(F32)
    mean_t = jnp.concatenate(
        [
            s_scr[0].astype(F32) + s_scr[2].astype(F32),
            s_scr[1].astype(F32) + s_scr[3].astype(F32),
        ],
        0,
    )
    mean_t = (mean_t / 12.0).astype(BF)
    ordered = lax.broadcasted_iota(jnp.int32, (V, V), 0)
    natural = lax.broadcasted_iota(jnp.int32, (V, V), 1)
    order = ((ordered % HALF) * 2 + ordered // HALF == natural).astype(F32).astype(BF)
    mean = dot(order, mean_t, LAST).astype(BF)
    pre = dot(feats, ws_ref[...]) + dot(mean, wn_ref[...])
    sig = jax.nn.sigmoid(pre)
    value = (pre * sig).astype(BF)
    grad_pre = (cot * sig * (1.0 + pre * (1.0 - sig))).astype(BF)
    for q in range(2):
        for h in range(2):
            o_scr[q * 2 + h] = value[q * HALF : (q + 1) * HALF, h * COLS : (h + 1) * COLS]
    out_ref[...] = o_scr[x]
    rows = pl.ds(pl.multiple_of(half * COLS, COLS), COLS)
    grad_mean = (dot(grad_pre, wn_ref[rows, :], LAST) / 12.0).astype(BF)
    message_ref[0:V] = dot(order, grad_mean, FIRST).astype(BF)
    own_self = dot(grad_pre, ws_ref[rows, :], LAST)
    self_ref[...] = jnp.where(parity == 0, own_self[0:HALF], own_self[HALF:V])
    w_scr[0] = dot(feats, grad_pre, FIRST)
    w_scr[1] = dot(mean, grad_pre, FIRST)
    quarter = pl.ds(pl.multiple_of(x * 64, 64), 64)
    for which in range(2):
        part = w_scr[which, quarter, :]
        for h in range(2):
            start = V + which * 128 + h * 64
            message_ref[start : start + 64, :] = part[:, h * COLS : (h + 1) * COLS].astype(BF)


def gather_kernel(place, m0, m1, m2, m3, out_ref):
    for dy, ref in enumerate((m0, m1, m2, m3)):
        out_ref[dy * V : (dy + 1) * V] = ref[0:V]
    tail = slice(V, V + WROWS)
    weight = (m0[tail].astype(F32) + m1[tail].astype(F32)) + (m2[tail].astype(F32) + m3[tail].astype(F32))
    high = weight.astype(BF)
    out_ref[NY * V : NY * V + WROWS] = high
    out_ref[NY * V + WROWS :] = (weight - high.astype(F32)).astype(BF)


def near_grads_kernel(place, counts, m0, m1, m2, m3, out_ref):
    for block in range(NZ + 1):
        span = slice(block * HALF, (block + 1) * HALF)
        total = jnp.zeros((HALF, COLS), F32)
        for dy, ref in enumerate((m0, m1, m2, m3)):
            total = total + dot(counts[dy, span], ref[0:V])
        out_ref[block] = total


def far_block(counts, other, near, block):
    span = slice(block * HALF, (block + 1) * HALF)
    total = near[block]
    for dy in range(NY):
        total = total + dot(counts[NY + dy, span], other[dy * V : (dy + 1) * V])
    return total


def first_grads_kernel(place, counts, own, other, near, up_ref, down_ref, hub_ref):
    parity = place[3] // 2
    hubs = far_block(counts, other, near, NZ)
    lane = lax.broadcasted_iota(jnp.int32, (HUB_ROWS, COLS), 1)
    low = (lane < 64) == (parity == 0)
    for delta in range(NZ):
        start = delta * 2 * HUB_ROWS
        mine = hubs[start : start + HUB_ROWS]
        rest = pltpu.roll(hubs[start + HUB_ROWS : start + 2 * HUB_ROWS], 64, 1)
        hub_ref[delta] = jnp.where(low, mine, rest)
    high, small = slice(NY * V, NY * V + WROWS), slice(NY * V + WROWS, NY * V + 2 * WROWS)
    weight = (own[high].astype(F32) + own[small].astype(F32)) + (
        other[high].astype(F32) + other[small].astype(F32)
    )
    weight = weight.astype(BF)
    for delta, ref in ((4, up_ref), (5, down_ref)):
        ref[0:HALF] = far_block(counts, other, near, delta).astype(BF)
        ref[HALF:BLOCK] = hub_ref[delta].astype(BF)
        ref[BLOCK:] = weight


REST = (0, 1, 2, 3, 6, 7)


def rest_grads_kernel(place, counts, other, near, out_ref):
    for index, delta in enumerate(REST):
        out_ref[index] = far_block(counts, other, near, delta)


def hop_kernel(place, up, down, rest, hubs, next_up, next_down, *, deltas):
    for delta, got, ref in zip(deltas, (up, down), (next_up, next_down)):
        ref[0:HALF] = (got[0:HALF].astype(F32) + rest[REST.index(delta)]).astype(BF)
        ref[HALF:BLOCK] = (got[HALF:BLOCK].astype(F32) + hubs[delta]).astype(BF)
        ref[BLOCK:] = got[BLOCK:]


def last_hop_kernel(place, up, down, rest, hubs, next_up, hub_up, hub_here):
    next_up[0:HALF] = (up[0:HALF].astype(F32) + rest[REST.index(1)]).astype(BF)
    next_up[HALF:] = up[BLOCK:]
    hub_up[...] = up[HALF:BLOCK].astype(F32) + hubs[1]
    hub_here[...] = down[HALF:BLOCK].astype(F32) + hubs[0]


def final_kernel(
    place, self_ref, rest, first, up1, up2, up3, up4, down1, down2, down3, hub_up, hub_here,
    feat_ref, hub_ref, gself_ref, gnbr_ref, w_scr,
):
    z = place[1]
    total = rest[0] + up4[0:HALF].astype(F32) + down3[0:HALF].astype(F32)
    feat_ref[...] = (self_ref[...] + total).astype(BF)
    hubs = hub_up[...] + hub_here[...]
    shape = (2 * HUB_ROWS, HUB_ROWS)
    target = lax.broadcasted_iota(jnp.int32, shape, 0)
    source = lax.broadcasted_iota(jnp.int32, shape, 1)
    spread = [
        dot((target == 2 * source + q).astype(F32), hubs[:, q * 64 : (q + 1) * 64], precision=lax.Precision.HIGHEST)
        for q in range(2)
    ]
    hub_ref[...] = spread[0] + spread[1]
    arrived = {0: first, 7: up1, 6: up2, 5: up3, 1: down1, 2: down2, 3: down3}
    for step in range(NZ):
        if step == 4:
            w_scr[(z + step) % NZ] = up4[HALF:]
        else:
            w_scr[(z + step) % NZ] = arrived[step][BLOCK:]
    weight = w_scr[0].astype(F32)
    for step in range(1, NZ):
        weight = weight + w_scr[step].astype(F32)
    gself_ref[...] = jnp.concatenate([weight[0:64], weight[64:128]], 1)
    gnbr_ref[...] = jnp.concatenate([weight[128:192], weight[192:256]], 1)


def body(features, hub_feats, nbr_owner, nbr_row, hub_ids, w_self, w_nbr, grad_out):
    place = jnp.stack([lax.axis_index(a) for a in ("y", "z", "c", "x")]).astype(jnp.int32)
    ids, mine, fg = call(
        prepare_kernel,
        (shaped((16, V), jnp.int32), shaped((BLOCK, COLS), BF), shaped((V, COLS), BF)),
        (place, features, grad_out, hub_feats, nbr_owner.reshape(8, V), nbr_row, hub_ids.T),
        "prepare",
    )

    t1, t7 = shift(mine, "z", NZ, -1), shift(mine, "z", NZ, 1)
    pair = jnp.stack([ids, swap(ids, "c", NC, 1)])
    fg1 = swap(fg, "x", NX, 1)
    pairs = [pair] + [swap(pair, "y", NY, m) for m in range(1, NY)]
    t23 = shift(jnp.concatenate([mine, t1], 0), "z", NZ, -2)
    t65 = shift(jnp.concatenate([mine, t7], 0), "z", NZ, 2)
    t4 = shift(t1, "z", NZ, -3)
    fg23 = swap(jnp.concatenate([fg, fg1], 0), "x", NX, 2)
    counts = call(
        counts_kernel,
        pltpu.VMEM((PARTS, ROWS, V), BF),
        (place, *pairs),
        "counts",
        flops=1 << 34,
        mib=8,
    )

    far, turned = call(
        far_sums_kernel,
        (shaped((NY, COLS, V), BF), shaped((COLS, ROWS), BF)),
        (place, counts, mine, t1, t7, t23, t65, t4),
        "far_sums",
        scratch=[pltpu.VMEM((ROWS, COLS), BF)],
        flops=1 << 31,
    )
    got = swap(far, "c", NC, 1)
    near = call(
        near_sums_kernel, shaped((NY, COLS, V), F32), (place, counts, turned), "near_sums", flops=1 << 31
    )
    both = near + got.astype(F32)
    total = both[0]
    for m in range(1, NY):
        total = total + swap(both[m].astype(BF), "y", NY, m).astype(F32)
    total = total.astype(BF)
    sums = [total] + [swap(total, "x", NX, m) for m in range(1, NX)]

    outputs, message, self_term = call(
        dense_kernel,
        (shaped((HALF, COLS), BF), shaped((V + WROWS, COLS), BF), shaped((HALF, COLS), F32)),
        (place, fg, fg1, fg23, *sums, w_self, w_nbr),
        "dense",
        scratch=[
            pltpu.VMEM((4, HALF, COLS), BF),
            pltpu.VMEM((4, HALF, COLS), BF),
            pltpu.VMEM((4, COLS, V), BF),
            pltpu.VMEM((4, HALF, COLS), BF),
            pltpu.VMEM((2, 256, 256), F32),
        ],
        flops=1 << 30,
    )

    messages = [message] + [swap(message, "y", NY, m) for m in range(1, NY)]
    own = call(
        gather_kernel, shaped((NY * V + 2 * WROWS, COLS), BF), (place, *messages), "gather_grads"
    )
    other = swap(own, "c", NC, 1)
    near_grads = call(
        near_grads_kernel,
        shaped((NZ + 1, HALF, COLS), F32),
        (place, counts, *messages),
        "near_grads",
        flops=1 << 31,
    )
    up0, down0, hubs = call(
        first_grads_kernel,
        (
            shaped((BLOCK + WROWS, COLS), BF),
            shaped((BLOCK + WROWS, COLS), BF),
            shaped((NZ, HUB_ROWS, COLS), F32),
        ),
        (place, counts, own, other, near_grads),
        "first_grads",
        flops=1 << 29,
    )
    up1, down1 = shift(up0, "z", NZ, 1), shift(down0, "z", NZ, -1)
    rest = call(
        rest_grads_kernel,
        shaped((len(REST), HALF, COLS), F32),
        (place, counts, other, near_grads),
        "rest_grads",
        flops=1 << 30,
    )
    hop_shapes = (shaped((BLOCK + WROWS, COLS), BF),) * 2
    ups, downs = [up1], [down1]
    for deltas in ((3, 6), (2, 7)):
        up, down = call(
            functools.partial(hop_kernel, deltas=deltas),
            hop_shapes,
            (place, ups[-1], downs[-1], rest, hubs),
            "hop",
        )
        ups.append(shift(up, "z", NZ, 1))
        downs.append(shift(down, "z", NZ, -1))
    up, hub_up, hub_here = call(
        last_hop_kernel,
        (
            shaped((HALF + WROWS, COLS), BF),
            shaped((HUB_ROWS, COLS), F32),
            shaped((HUB_ROWS, COLS), F32),
        ),
        (place, ups[-1], downs[-1], rest, hubs),
        "last_hop",
    )
    ups.append(shift(up, "z", NZ, 1))
    turn = (0, 2, 1, 3)
    cross = [(z * NX + x, (z + 1) % NZ * NX + turn[x]) for z in range(NZ) for x in range(NX)]
    hub_up = lax.ppermute(hub_up, ("z", "x"), cross)
    hub_here = lax.ppermute(hub_here, "x", [(x, turn[x]) for x in range(NX)])
    grad_features, hub_rows, grad_self, grad_nbr = call(
        final_kernel,
        (
            shaped((HALF, COLS), BF),
            shaped((2 * HUB_ROWS, 64), F32),
            shaped((64, 256), F32),
            shaped((64, 256), F32),
        ),
        (place, self_term, rest, up0, *ups, *downs, hub_up, hub_here),
        "last_sums",
        scratch=[pltpu.VMEM((NZ, WROWS, COLS), BF)],
    )
    return outputs, grad_features, hub_rows, grad_self, grad_nbr


def solution(mesh):
    fine = Mesh(mesh.devices.reshape(NY, NZ, NC, NX), ("y", "z", "c", "x"))
    dom = ("y", "z", "c")
    in_specs = (
        P(dom, "x"),
        P(dom, None),
        P(None, dom, None),
        P(None, dom),
        P(dom, None),
        P(),
        P(),
        P(dom, "x"),
    )
    out_specs = (P(dom, "x"), P(dom, "x"), P(dom, "x"), P("x", None), P("x", None))
    return jax.shard_map(body, mesh=fine, in_specs=in_specs, out_specs=out_specs, check_vma=False)
```

time: 176 us -> 113 us (0.64)
  matrix products: 27 us -> 0 us
  starting transfers between devices: 62.2 us -> 47.8 us
  waiting for transfers between devices: 39.4 us -> 31.1 us
  local copies, waits for them, and re-layouts: 12.2 us -> 4.57 us
  other arithmetic: 4.92 us -> 0.4 us
    dot_general x9 -> x0, matrix products: 27 us -> none  [the longest x8 19.5 us: term(): rows = jnp.dot(counts[delta], grads, preferred_element_type=F32)]
    ppermute x21 -> x17, starting transfers between devices: 27.9 us -> 19.9 us  [swap(): return lax.ppermute(x, axis, [(i, i ^ mask) for i in range(size)])]
    ppermute x14 -> x12, waiting for transfers between devices: 17.8 us -> 10.5 us  [shift(): return lax.ppermute(x, axis, [(i, (i + step) % size) for i in range(size)])]
    ppermute x14 -> x12, starting transfers between devices: 26.8 us -> 22.8 us  [shift(): return lax.ppermute(x, axis, [(i, (i + step) % size) for i in range(size)])]
    unnamed x46 -> x15, local copies, waits for them, and re-layouts: 7.25 us -> 4.54 us
    ppermute x21 -> x17, waiting for transfers between devices: 21.4 us -> 18.8 us  [swap(): return lax.ppermute(x, axis, [(i, i ^ mask) for i in range(size)])]
    slice x18 -> x0, local copies, waits for them, and re-layouts: 2.56 us -> none  [the longest x7 1.35 us: travel(): passing = arrived[-256:]]
    ppermute x3 -> x2, starting transfers between devices: 7.48 us -> 5.19 us  [the longest x1 3.73 us: body(): hub_here = lax.ppermute(hub_here, 'x', [(x, turn[x]) for x in range(NX)])]
  transfers between devices with their start and end apart: 38 -> 31, of which waited for: 15 -> 13; matrix products, arithmetic and copies ran while one was open for 3% -> 0% of each run, Pallas kernels for 13% -> 15%
where the time goes in v2:
time: 113 us; the launch traced here: 112 us
  starting transfers between devices  47.8 us (42%)
  waiting for transfers between devices  31.1 us (28%)
  Pallas kernels  27.5 us (24%)
  local copies, waits for them, and re-layouts  4.57 us (4%)
    pallas_call x13, Pallas kernels, call(): pl.pallas_call(kernel, out_shape=outs, in_specs=[SM] + [VM] * (len(inputs...  27.5 us
    ppermute x12, starting transfers between devices, shift(): return lax.ppermute(x, axis, [(i, (i + step) % size) for i in range(size)])  22.8 us
    ppermute x17, starting transfers between devices, swap(): return lax.ppermute(x, axis, [(i, i ^ mask) for i in range(size)])  19.9 us
    ppermute x17, waiting for transfers between devices, swap(): return lax.ppermute(x, axis, [(i, i ^ mask) for i in range(size)])  18.8 us
    ppermute x12, waiting for transfers between devices, shift(): return lax.ppermute(x, axis, [(i, (i + step) % size) for i in range(size)])  10.5 us
    unnamed x15, local copies, waits for them, and re-layouts  4.54 us
    ppermute x1, starting transfers between devices, body(): hub_here = lax.ppermute(hub_here, 'x', [(x, turn[x]) for x in range(NX)])  3.73 us
  transfers between devices with their start and end apart: 31, of which 13 were waited for; matrix products, arithmetic and copies ran while one was open for 0% of the time, Pallas kernels for 15%

profile of v2, /device:TPU:4, one launch (start us, length us, event | category | flops | bytes accessed | tf_op | source)
XLA Modules:
  0.0 112.2 jit_solution(4032553404278007395)
XLA Ops:
  5.9 2.0 %collective-permute-start.7 = (bf16[272,128]{1,0:T(8,128)(2,1)S(1)}, bf16[272,128]{1,0:T(8,128)(2,1)S(1)}, u32[]{:S(2)}, u32[]{:S(2)}) collective-permute-start(bf16[272,128]{1,0:T(8,128)(2,1)S(1)} %get-tuple-element.29.t0), channel_id=1, source_target_pairs={{0,8},{8,16},{16,24},{24,32},{32,40},{40,48},{48,56},{56,0},{1,9},... | collective-permute-start | bytes 208904 | tf_op jit(solution)/shard_map/ppermute | solution.py:34
  7.9 4.0 %collective-permute-start.6 = (bf16[272,128]{1,0:T(8,128)(2,1)S(1)}, bf16[272,128]{1,0:T(8,128)(2,1)S(1)}, u32[]{:S(2)}, u32[]{:S(2)}) collective-permute-start(bf16[272,128]{1,0:T(8,128)(2,1)S(1)} %get-tuple-element.29.t0), channel_id=1, source_target_pairs={{0,56},{8,0},{16,8},{24,16},{32,24},{40,32},{48,40},{56,48},{1,57}... | collective-permute-start | bytes 208904 | tf_op jit(solution)/shard_map/ppermute | solution.py:34
  12.0 3.1 %collective-permute-start.5 = (s32[2,16,512]{2,1,0:T(8,128)S(1)}, s32[2,16,512]{2,1,0:T(8,128)S(1)}, u32[]{:S(2)}, u32[]{:S(2)}) collective-permute-start(s32[2,16,512]{2,1,0:T(8,128)S(1)} %pad_add_fusion.ids0), channel_id=1, source_target_pairs={{0,192},{64,128},{128,64},{192,0},{1,193},{65,129},{129,65},{193,1... | collective-permute-start | bytes 196616 | tf_op jit(solution)/shard_map/ppermute | solution.py:38
  16.9 3.5 %collective-permute-start.8 = (bf16[544,128]{1,0:T(8,128)(2,1)S(1)}, bf16[544,128]{1,0:T(8,128)(2,1)S(1)}, u32[]{:S(2)}, u32[]{:S(2)}) collective-permute-start(bf16[544,128]{1,0:T(8,128)(2,1)S(1)} %get-tuple-element.55), channel_id=1, source_target_pairs={{0,48},{8,56},{16,0},{24,8},{32,16},{40,24},{48,32},{56,40},{1,49}... | collective-permute-start | bytes 417800 | tf_op jit(solution)/shard_map/ppermute | solution.py:34
  20.4 2.8 %collective-permute-start.10 = (bf16[272,128]{1,0:T(8,128)(2,1)S(1)}, bf16[272,128]{1,0:T(8,128)(2,1)S(1)}, u32[]{:S(2)}, u32[]{:S(2)}) collective-permute-start(bf16[272,128]{1,0:T(8,128)(2,1)S(1)} %collective-permute-done.6.t1), channel_id=1, source_target_pairs={{0,40},{8,48},{16,56},{24,0},{32,8},{40,16},{48,24},{56,32},{1,41}... | collective-permute-start | bytes 208904 | tf_op jit(solution)/shard_map/ppermute | solution.py:34
  23.2 8.9 %counts.1 = bf16[8,2304,512]{2,1,0:T(8,128)(2,1)S(1)} custom-call(s32[4]{0:T(128)S(1)} %pad_add_fusion.1.place, s32[2,16,512]{2,1,0:T(8,128)S(1)} %pad_add_fusion.ids0, s32[2,16,512]{2,1,0:T(8,128)S(1)} %collective-permute-done.3.ids1, s32[2,16,512]{2,1,0:T(8,128)S(1)} %collective-permute-done.4.ids2, s32[2,16,512]{2,1,0:T(8,128)S(1)} %collective-permute-done.5.ids3), custom_call_target="tpu_custom_call" | custom-call | flops 17179869184 | bytes 262144 | tf_op jit(solution)/shard_map/counts/pallas_call | solution.py:42
  32.1 2.7 %far_sums.1 = (bf16[4,128,512]{2,1,0:T(8,128)(2,1)S(1)}, bf16[128,2304]{1,0:T(8,128)(2,1)S(1)}) custom-call(s32[4]{0:T(128)S(1)} %pad_add_fusion.1.place, bf16[8,2304,512]{2,1,0:T(8,128)(2,1)S(1)} %counts.1, bf16[272,128]{1,0:T(8,128)(2,1)S(1)} %get-tuple-element.29.t0, bf16[272,128]{1,0:T(8,128)(2,1)S(1)} %collective-permute-done.6.t1, ...), custom_call_target="tpu_custom_call" | custom-call | flops 2147483648 | bytes 262144 | tf_op jit(solution)/shard_map/far_sums/pallas_call | solution.py:42
  36.2 2.5 %near_sums.1 = f32[4,128,512]{2,1,0:T(8,128)S(1)} custom-call(s32[4]{0:T(128)S(1)} %pad_add_fusion.1.place, bf16[8,2304,512]{2,1,0:T(8,128)(2,1)S(1)} %counts.1, bf16[128,2304]{1,0:T(8,128)(2,1)S(1)} %get-tuple-element.30.turned), custom_call_target="tpu_custom_call" | custom-call | flops 2147483648 | bytes 262144 | tf_op jit(solution)/shard_map/near_sums/pallas_call | solution.py:42
  40.6 3.7 %collective-permute-start.14 = (bf16[128,512]{1,0:T(8,128)(2,1)S(1)}, bf16[128,512]{1,0:T(8,128)(2,1)S(1)}, u32[]{:S(2)}, u32[]{:S(2)}) collective-permute-start(bf16[128,512]{1,0:T(8,128)(2,1)S(1)} %get-tuple-element.52), channel_id=1, source_target_pairs={{0,192},{64,128},{128,64},{192,0},{1,193},{65,129},{129,65},{193,1... | collective-permute-start | bytes 393224 | tf_op jit(solution)/shard_map/ppermute | solution.py:38
  44.6 5.3 %collective-permute-done.14 = bf16[128,512]{1,0:T(8,128)(2,1)S(1)} collective-permute-done((bf16[128,512]{1,0:T(8,128)(2,1)S(1)}, bf16[128,512]{1,0:T(8,128)(2,1)S(1)}, u32[]{:S(2)}, u32[]{:S(2)}) %collective-permute-start.14) | collective-permute-done | bytes 131104 | tf_op jit(solution)/shard_map/ppermute | solution.py:38
  51.0 2.9 %collective-permute-start.16 = (bf16[128,512]{1,0:T(8,128)(2,1)S(1)}, bf16[128,512]{1,0:T(8,128)(2,1)S(1)}, u32[]{:S(2)}, u32[]{:S(2)}) collective-permute-start(bf16[128,512]{1,0:T(8,128)(2,1)S(1)} %fusion.3.s0), channel_id=1, source_target_pairs={{0,2},{1,3},{2,0},{3,1},{4,6},{5,7},{6,4},{7,5},{8,10},{9,11},{10,... | collective-permute-start | bytes 393224 | tf_op jit(solution)/shard_map/ppermute | solution.py:38
  55.1 4.3 %collective-permute-done.17.s3 = bf16[128,512]{1,0:T(8,128)(2,1)S(1)} collective-permute-done((bf16[128,512]{1,0:T(8,128)(2,1)S(1)}, bf16[128,512]{1,0:T(8,128)(2,1)S(1)}, u32[]{:S(2)}, u32[]{:S(2)}) %collective-permute-start.17) | collective-permute-done | bytes 131104 | tf_op jit(solution)/shard_map/ppermute | solution.py:38
  59.8 2.0 %dense.1 = (bf16[256,128]{1,0:T(8,128)(2,1)}, bf16[768,128]{1,0:T(8,128)(2,1)S(1)}, f32[256,128]{1,0:T(8,128)S(1)}) custom-call(s32[4]{0:T(128)S(1)} %pad_add_fusion.1.place, bf16[512,128]{1,0:T(8,128)(2,1)S(1)} %get-tuple-element.27.fg0, bf16[512,128]{1,0:T(8,128)(2,1)S(1)} %collective-permute-done.fg1, bf16[1024,128]{1,0:T(8,128)(2,1)S(1)} %collective-permute-done.1.fg23, ...), custom_call_target="tpu_custom_call" | custom-call | flops 1073741824 | bytes 262144 | tf_op jit(solution)/shard_map/dense/pallas_call | solution.py:42
  61.8 3.7 %collective-permute-start.20 = (bf16[768,128]{1,0:T(8,128)(2,1)S(1)}, bf16[768,128]{1,0:T(8,128)(2,1)S(1)}, u32[]{:S(2)}, u32[]{:S(2)}) collective-permute-start(bf16[768,128]{1,0:T(8,128)(2,1)S(1)} %get-tuple-element.34.m0), channel_id=1, source_target_pairs={{0,192},{64,128},{128,64},{192,0},{1,193},{65,129},{129,65},{193,1... | collective-permute-start | bytes 589832 | tf_op jit(solution)/shard_map/ppermute | solution.py:38
  66.5 6.0 %collective-permute-done.20.m3 = bf16[768,128]{1,0:T(8,128)(2,1)S(1)} collective-permute-done((bf16[768,128]{1,0:T(8,128)(2,1)S(1)}, bf16[768,128]{1,0:T(8,128)(2,1)S(1)}, u32[]{:S(2)}, u32[]{:S(2)}) %collective-permute-start.20) | collective-permute-done | bytes 196640 | tf_op jit(solution)/shard_map/ppermute | solution.py:38
  74.8 3.1 %near_grads.1.near = f32[9,256,128]{2,1,0:T(8,128)S(1)} custom-call(s32[4]{0:T(128)S(1)} %pad_add_fusion.1.place, bf16[8,2304,512]{2,1,0:T(8,128)(2,1)S(1)} %counts.1, bf16[768,128]{1,0:T(8,128)(2,1)S(1)} %get-tuple-element.34.m0, bf16[768,128]{1,0:T(8,128)(2,1)S(1)} %collective-permute-done.18.m1, bf16[768,128]{1,0:T(8,128)(2,1)S(1)} %collective-permute-done.19.m2, ...), custom_call_target="tpu_custom_call" | custom-call | flops 2147483648 | bytes 262144 | tf_op jit(solution)/shard_map/near_grads/pallas_call | solution.py:42
  79.5 2.7 %collective-permute-start.23 = (bf16[528,128]{1,0:T(8,128)(2,1)S(1)}, bf16[528,128]{1,0:T(8,128)(2,1)S(1)}, u32[]{:S(2)}, u32[]{:S(2)}) collective-permute-start(bf16[528,128]{1,0:T(8,128)(2,1)S(1)} %get-tuple-element.36), channel_id=1, source_target_pairs={{0,56},{8,0},{16,8},{24,16},{32,24},{40,32},{48,40},{56,48},{1,57}... | collective-permute-start | bytes 405512 | tf_op jit(solution)/shard_map/ppermute | solution.py:34
  82.2 2.3 %rest_grads.1.rest = f32[6,256,128]{2,1,0:T(8,128)S(1)} custom-call(s32[4]{0:T(128)S(1)} %pad_add_fusion.1.place, bf16[8,2304,512]{2,1,0:T(8,128)(2,1)S(1)} %counts.1, bf16[2560,128]{1,0:T(8,128)(2,1)S(1)} %collective-permute-done.21.other, f32[9,256,128]{2,1,0:T(8,128)S(1)} %near_grads.1.near), custom_call_target="tpu_custom_call" | custom-call | flops 1073741824 | bytes 262144 | tf_op jit(solution)/shard_map/rest_grads/pallas_call | solution.py:42
  85.7 3.4 %collective-permute-done.22.up.up1 = bf16[528,128]{1,0:T(8,128)(2,1)S(1)} collective-permute-done((bf16[528,128]{1,0:T(8,128)(2,1)S(1)}, bf16[528,128]{1,0:T(8,128)(2,1)S(1)}, u32[]{:S(2)}, u32[]{:S(2)}) %collective-permute-start.22) | collective-permute-done | bytes 135200 | tf_op jit(solution)/shard_map/ppermute | solution.py:34
  89.8 3.2 %collective-permute-start.25 = (bf16[528,128]{1,0:T(8,128)(2,1)S(1)}, bf16[528,128]{1,0:T(8,128)(2,1)S(1)}, u32[]{:S(2)}, u32[]{:S(2)}) collective-permute-start(bf16[528,128]{1,0:T(8,128)(2,1)S(1)} %get-tuple-element.39), channel_id=1, source_target_pairs={{0,56},{8,0},{16,8},{24,16},{32,24},{40,32},{48,40},{56,48},{1,57}... | collective-permute-start | bytes 405512 | tf_op jit(solution)/shard_map/ppermute | solution.py:34
  93.0 3.0 %collective-permute-done.24.up.up2 = bf16[528,128]{1,0:T(8,128)(2,1)S(1)} collective-permute-done((bf16[528,128]{1,0:T(8,128)(2,1)S(1)}, bf16[528,128]{1,0:T(8,128)(2,1)S(1)}, u32[]{:S(2)}, u32[]{:S(2)}) %collective-permute-start.24) | collective-permute-done | bytes 135200 | tf_op jit(solution)/shard_map/ppermute | solution.py:34
  96.9 3.3 %collective-permute-start.27 = (bf16[528,128]{1,0:T(8,128)(2,1)S(1)}, bf16[528,128]{1,0:T(8,128)(2,1)S(1)}, u32[]{:S(2)}, u32[]{:S(2)}) collective-permute-start(bf16[528,128]{1,0:T(8,128)(2,1)S(1)} %get-tuple-element.41), channel_id=1, source_target_pairs={{0,56},{8,0},{16,8},{24,16},{32,24},{40,32},{48,40},{56,48},{1,57}... | collective-permute-start | bytes 405512 | tf_op jit(solution)/shard_map/ppermute | solution.py:34
  100.2 2.9 %collective-permute-done.26.up.up3 = bf16[528,128]{1,0:T(8,128)(2,1)S(1)} collective-permute-done((bf16[528,128]{1,0:T(8,128)(2,1)S(1)}, bf16[528,128]{1,0:T(8,128)(2,1)S(1)}, u32[]{:S(2)}, u32[]{:S(2)}) %collective-permute-start.26) | collective-permute-done | bytes 135200 | tf_op jit(solution)/shard_map/ppermute | solution.py:34
  105.3 3.7 %collective-permute-start.30 = (f32[16,128]{1,0:T(8,128)S(1)}, f32[16,128]{1,0:T(8,128)S(1)}, u32[]{:S(2)}, u32[]{:S(2)}) collective-permute-start(f32[16,128]{1,0:T(8,128)S(1)} %get-tuple-element.44), channel_id=1, source_target_pairs={{0,0},{1,2},{2,1},{3,3},{4,4},{5,6},{6,5},{7,7},{8,8},{9,10},{10,9... | collective-permute-start | bytes 24584 | tf_op jit(solution)/shard_map/ppermute | solution.py:449
  (73 shorter events, 26.4 us)
Async XLA Ops:
  5.9 10.2 %collective-permute-start.7 = (bf16[272,128]{1,0:T(8,128)(2,1)S(1)}, bf16[272,128]{1,0:T(8,128)(2,1)S(1)}, u32[]{:S(2)}, u32[]{:S(2)}) collective-permute-start(bf16[272,128]{1,0:T(8,128)(2,1)S(1)} %get-tuple-element.29.t0), channel_id=1, source_target_pairs={{0,8},{8,16},{16,24},{24,32},{32,40},{40,48},{48,56},{56,0},{1,9},... | collective-permute-start | bytes 208904 | tf_op jit(solution)/shard_map/ppermute | solution.py:34
  7.9 8.2 %collective-permute-start.6 = (bf16[272,128]{1,0:T(8,128)(2,1)S(1)}, bf16[272,128]{1,0:T(8,128)(2,1)S(1)}, u32[]{:S(2)}, u32[]{:S(2)}) collective-permute-start(bf16[272,128]{1,0:T(8,128)(2,1)S(1)} %get-tuple-element.29.t0), channel_id=1, source_target_pairs={{0,56},{8,0},{16,8},{24,16},{32,24},{40,32},{48,40},{56,48},{1,57}... | collective-permute-start | bytes 208904 | tf_op jit(solution)/shard_map/ppermute | solution.py:34
  12.0 8.4 %collective-permute-start.5 = (s32[2,16,512]{2,1,0:T(8,128)S(1)}, s32[2,16,512]{2,1,0:T(8,128)S(1)}, u32[]{:S(2)}, u32[]{:S(2)}) collective-permute-start(s32[2,16,512]{2,1,0:T(8,128)S(1)} %pad_add_fusion.ids0), channel_id=1, source_target_pairs={{0,192},{64,128},{128,64},{192,0},{1,193},{65,129},{129,65},{193,1... | collective-permute-start | bytes 196616 | tf_op jit(solution)/shard_map/ppermute | solution.py:38
  15.1 8.2 %collective-permute-start.4 = (s32[2,16,512]{2,1,0:T(8,128)S(1)}, s32[2,16,512]{2,1,0:T(8,128)S(1)}, u32[]{:S(2)}, u32[]{:S(2)}) collective-permute-start(s32[2,16,512]{2,1,0:T(8,128)S(1)} %pad_add_fusion.ids0), channel_id=1, source_target_pairs={{0,128},{64,192},{128,0},{192,64},{1,129},{65,193},{129,1},{193,65... | collective-permute-start | bytes 196616 | tf_op jit(solution)/shard_map/ppermute | solution.py:38
  15.7 7.5 %collective-permute-start.3 = (s32[2,16,512]{2,1,0:T(8,128)S(1)}, s32[2,16,512]{2,1,0:T(8,128)S(1)}, u32[]{:S(2)}, u32[]{:S(2)}) collective-permute-start(s32[2,16,512]{2,1,0:T(8,128)S(1)} %pad_add_fusion.ids0), channel_id=1, source_target_pairs={{0,64},{64,0},{128,192},{192,128},{1,65},{65,1},{129,193},{193,129... | collective-permute-start | bytes 196616 | tf_op jit(solution)/shard_map/ppermute | solution.py:38
  16.2 16.0 %collective-permute-start.9 = (bf16[544,128]{1,0:T(8,128)(2,1)S(1)}, bf16[544,128]{1,0:T(8,128)(2,1)S(1)}, u32[]{:S(2)}, u32[]{:S(2)}) collective-permute-start(bf16[544,128]{1,0:T(8,128)(2,1)S(1)} %get-tuple-element.54), channel_id=1, source_target_pairs={{0,16},{8,24},{16,32},{24,40},{32,48},{40,56},{48,0},{56,8},{1,17}... | collective-permute-start | bytes 417800 | tf_op jit(solution)/shard_map/ppermute | solution.py:34
  16.9 15.2 %collective-permute-start.8 = (bf16[544,128]{1,0:T(8,128)(2,1)S(1)}, bf16[544,128]{1,0:T(8,128)(2,1)S(1)}, u32[]{:S(2)}, u32[]{:S(2)}) collective-permute-start(bf16[544,128]{1,0:T(8,128)(2,1)S(1)} %get-tuple-element.55), channel_id=1, source_target_pairs={{0,48},{8,56},{16,0},{24,8},{32,16},{40,24},{48,32},{56,40},{1,49}... | collective-permute-start | bytes 417800 | tf_op jit(solution)/shard_map/ppermute | solution.py:34
  20.4 11.7 %collective-permute-start.10 = (bf16[272,128]{1,0:T(8,128)(2,1)S(1)}, bf16[272,128]{1,0:T(8,128)(2,1)S(1)}, u32[]{:S(2)}, u32[]{:S(2)}) collective-permute-start(bf16[272,128]{1,0:T(8,128)(2,1)S(1)} %collective-permute-done.6.t1), channel_id=1, source_target_pairs={{0,40},{8,48},{16,56},{24,0},{32,8},{40,16},{48,24},{56,32},{1,41}... | collective-permute-start | bytes 208904 | tf_op jit(solution)/shard_map/ppermute | solution.py:34
  34.9 9.4 %collective-permute-start = (bf16[512,128]{1,0:T(8,128)(2,1)S(1)}, bf16[512,128]{1,0:T(8,128)(2,1)S(1)}, u32[]{:S(2)}, u32[]{:S(2)}) collective-permute-start(bf16[512,128]{1,0:T(8,128)(2,1)S(1)} %get-tuple-element.27.fg0), channel_id=1, source_target_pairs={{0,1},{1,0},{2,3},{3,2},{4,5},{5,4},{6,7},{7,6},{8,9},{9,8},{10,11... | collective-permute-start | bytes 393224 | tf_op jit(solution)/shard_map/ppermute | solution.py:38
  40.6 9.3 %collective-permute-start.14 = (bf16[128,512]{1,0:T(8,128)(2,1)S(1)}, bf16[128,512]{1,0:T(8,128)(2,1)S(1)}, u32[]{:S(2)}, u32[]{:S(2)}) collective-permute-start(bf16[128,512]{1,0:T(8,128)(2,1)S(1)} %get-tuple-element.52), channel_id=1, source_target_pairs={{0,192},{64,128},{128,64},{192,0},{1,193},{65,129},{129,65},{193,1... | collective-permute-start | bytes 393224 | tf_op jit(solution)/shard_map/ppermute | solution.py:38
  44.3 6.5 %collective-permute-start.13 = (bf16[128,512]{1,0:T(8,128)(2,1)S(1)}, bf16[128,512]{1,0:T(8,128)(2,1)S(1)}, u32[]{:S(2)}, u32[]{:S(2)}) collective-permute-start(bf16[128,512]{1,0:T(8,128)(2,1)S(1)} %get-tuple-element.53), channel_id=1, source_target_pairs={{0,128},{64,192},{128,0},{192,64},{1,129},{65,193},{129,1},{193,65... | collective-permute-start | bytes 393224 | tf_op jit(solution)/shard_map/ppermute | solution.py:38
  44.3 10.7 %collective-permute-start.1 = (bf16[1024,128]{1,0:T(8,128)(2,1)S(1)}, bf16[1024,128]{1,0:T(8,128)(2,1)S(1)}, u32[]{:S(2)}, u32[]{:S(2)}) collective-permute-start(bf16[1024,128]{1,0:T(8,128)(2,1)S(1)} %pad_maximum_fusion), channel_id=1, source_target_pairs={{0,2},{1,3},{2,0},{3,1},{4,6},{5,7},{6,4},{7,5},{8,10},{9,11},{10,... | collective-permute-start | bytes 786440 | tf_op jit(solution)/shard_map/ppermute | solution.py:38
  50.9 8.5 %collective-permute-start.17 = (bf16[128,512]{1,0:T(8,128)(2,1)S(1)}, bf16[128,512]{1,0:T(8,128)(2,1)S(1)}, u32[]{:S(2)}, u32[]{:S(2)}) collective-permute-start(bf16[128,512]{1,0:T(8,128)(2,1)S(1)} %fusion.3.s0), channel_id=1, source_target_pairs={{0,3},{1,2},{2,1},{3,0},{4,7},{5,6},{6,5},{7,4},{8,11},{9,10},{10,... | collective-permute-start | bytes 393224 | tf_op jit(solution)/shard_map/ppermute | solution.py:38
  51.0 8.4 %collective-permute-start.16 = (bf16[128,512]{1,0:T(8,128)(2,1)S(1)}, bf16[128,512]{1,0:T(8,128)(2,1)S(1)}, u32[]{:S(2)}, u32[]{:S(2)}) collective-permute-start(bf16[128,512]{1,0:T(8,128)(2,1)S(1)} %fusion.3.s0), channel_id=1, source_target_pairs={{0,2},{1,3},{2,0},{3,1},{4,6},{5,7},{6,4},{7,5},{8,10},{9,11},{10,... | collective-permute-start | bytes 393224 | tf_op jit(solution)/shard_map/ppermute | solution.py:38
  61.8 10.6 %collective-permute-start.20 = (bf16[768,128]{1,0:T(8,128)(2,1)S(1)}, bf16[768,128]{1,0:T(8,128)(2,1)S(1)}, u32[]{:S(2)}, u32[]{:S(2)}) collective-permute-start(bf16[768,128]{1,0:T(8,128)(2,1)S(1)} %get-tuple-element.34.m0), channel_id=1, source_target_pairs={{0,192},{64,128},{128,64},{192,0},{1,193},{65,129},{129,65},{193,1... | collective-permute-start | bytes 589832 | tf_op jit(solution)/shard_map/ppermute | solution.py:38
  65.5 8.6 %collective-permute-start.19 = (bf16[768,128]{1,0:T(8,128)(2,1)S(1)}, bf16[768,128]{1,0:T(8,128)(2,1)S(1)}, u32[]{:S(2)}, u32[]{:S(2)}) collective-permute-start(bf16[768,128]{1,0:T(8,128)(2,1)S(1)} %get-tuple-element.34.m0), channel_id=1, source_target_pairs={{0,128},{64,192},{128,0},{192,64},{1,129},{65,193},{129,1},{193,65... | collective-permute-start | bytes 589832 | tf_op jit(solution)/shard_map/ppermute | solution.py:38
  65.5 8.6 %collective-permute-start.18 = (bf16[768,128]{1,0:T(8,128)(2,1)S(1)}, bf16[768,128]{1,0:T(8,128)(2,1)S(1)}, u32[]{:S(2)}, u32[]{:S(2)}) collective-permute-start(bf16[768,128]{1,0:T(8,128)(2,1)S(1)} %get-tuple-element.34.m0), channel_id=1, source_target_pairs={{0,64},{64,0},{128,192},{192,128},{1,65},{65,1},{129,193},{193,129... | collective-permute-start | bytes 589832 | tf_op jit(solution)/shard_map/ppermute | solution.py:38
  82.2 6.9 %collective-permute-start.22 = (bf16[528,128]{1,0:T(8,128)(2,1)S(1)}, bf16[528,128]{1,0:T(8,128)(2,1)S(1)}, u32[]{:S(2)}, u32[]{:S(2)}) collective-permute-start(bf16[528,128]{1,0:T(8,128)(2,1)S(1)} %get-tuple-element.35.first), channel_id=1, source_target_pairs={{0,8},{8,16},{16,24},{24,32},{32,40},{40,48},{48,56},{56,0},{1,9},... | collective-permute-start | bytes 405512 | tf_op jit(solution)/shard_map/ppermute | solution.py:34
  89.7 6.3 %collective-permute-start.24 = (bf16[528,128]{1,0:T(8,128)(2,1)S(1)}, bf16[528,128]{1,0:T(8,128)(2,1)S(1)}, u32[]{:S(2)}, u32[]{:S(2)}) collective-permute-start(bf16[528,128]{1,0:T(8,128)(2,1)S(1)} %get-tuple-element.38), channel_id=1, source_target_pairs={{0,8},{8,16},{16,24},{24,32},{32,40},{40,48},{48,56},{56,0},{1,9},... | collective-permute-start | bytes 405512 | tf_op jit(solution)/shard_map/ppermute | solution.py:34
  89.8 6.2 %collective-permute-start.25 = (bf16[528,128]{1,0:T(8,128)(2,1)S(1)}, bf16[528,128]{1,0:T(8,128)(2,1)S(1)}, u32[]{:S(2)}, u32[]{:S(2)}) collective-permute-start(bf16[528,128]{1,0:T(8,128)(2,1)S(1)} %get-tuple-element.39), channel_id=1, source_target_pairs={{0,56},{8,0},{16,8},{24,16},{32,24},{40,32},{48,40},{56,48},{1,57}... | collective-permute-start | bytes 405512 | tf_op jit(solution)/shard_map/ppermute | solution.py:34
  96.6 6.6 %collective-permute-start.26 = (bf16[528,128]{1,0:T(8,128)(2,1)S(1)}, bf16[528,128]{1,0:T(8,128)(2,1)S(1)}, u32[]{:S(2)}, u32[]{:S(2)}) collective-permute-start(bf16[528,128]{1,0:T(8,128)(2,1)S(1)} %get-tuple-element.40), channel_id=1, source_target_pairs={{0,8},{8,16},{16,24},{24,32},{32,40},{40,48},{48,56},{56,0},{1,9},... | collective-permute-start | bytes 405512 | tf_op jit(solution)/shard_map/ppermute | solution.py:34
  96.9 6.2 %collective-permute-start.27 = (bf16[528,128]{1,0:T(8,128)(2,1)S(1)}, bf16[528,128]{1,0:T(8,128)(2,1)S(1)}, u32[]{:S(2)}, u32[]{:S(2)}) collective-permute-start(bf16[528,128]{1,0:T(8,128)(2,1)S(1)} %get-tuple-element.41), channel_id=1, source_target_pairs={{0,56},{8,0},{16,8},{24,16},{32,24},{40,32},{48,40},{56,48},{1,57}... | collective-permute-start | bytes 405512 | tf_op jit(solution)/shard_map/ppermute | solution.py:34
  103.7 7.1 %collective-permute-start.28 = (bf16[512,128]{1,0:T(8,128)(2,1)S(1)}, bf16[512,128]{1,0:T(8,128)(2,1)S(1)}, u32[]{:S(2)}, u32[]{:S(2)}) collective-permute-start(bf16[512,128]{1,0:T(8,128)(2,1)S(1)} %get-tuple-element.42), channel_id=1, source_target_pairs={{0,8},{8,16},{16,24},{24,32},{32,40},{40,48},{48,56},{56,0},{1,9},... | collective-permute-start | bytes 393224 | tf_op jit(solution)/shard_map/ppermute | solution.py:34
  103.8 6.3 %collective-permute-start.29 = (f32[16,128]{1,0:T(8,128)S(1)}, f32[16,128]{1,0:T(8,128)S(1)}, u32[]{:S(2)}, u32[]{:S(2)}) collective-permute-start(f32[16,128]{1,0:T(8,128)S(1)} %get-tuple-element.43), channel_id=1, source_target_pairs={{0,8},{1,10},{2,9},{3,11},{8,16},{9,18},{10,17},{11,19},{16,24},{1... | collective-permute-start | bytes 24584 | tf_op jit(solution)/shard_map/ppermute | solution.py:448
  (14 other events, 95.7 us)

commit v3 on v2

--- a/solution.py
+++ b/solution.py
@@ -38,11 +38,11 @@
     return lax.ppermute(x, axis, [(i, i ^ mask) for i in range(size)])
 
 
-def call(kernel, outs, inputs, name, scratch=(), flops=0, mib=16):
+def call(kernel, outs, inputs, name, scratch=(), flops=0, mib=16, far=0):
     return pl.pallas_call(
         kernel,
         out_shape=outs,
-        in_specs=[SM] + [VM] * (len(inputs) - 1),
+        in_specs=[SM] + [VM] * (len(inputs) - 1 - far) + [pl.BlockSpec(memory_space=pl.ANY)] * far,
         out_specs=jax.tree.map(lambda _: VM, outs),
         scratch_shapes=list(scratch),
         compiler_params=pltpu.CompilerParams(vmem_limit_bytes=mib << 20),
@@ -55,22 +55,41 @@
     return jax.ShapeDtypeStruct(shape, dtype)
 
 
-def prepare_kernel(place, feat_ref, cot_ref, hub_ref, owner_ref, row_ref, hub_id_ref, ids_ref, mine_ref, both_ref):
+def prepare_kernel(
+    place, feat, cot, hub, owner, row, hub_id, ids_ref, mine_ref, both_ref,
+    owner_scr, row_scr, hub_id_scr, hub_scr, sems,
+):
     parity, half = place[3] // 2, place[3] % 2
-    ids_ref[0:8] = owner_ref[...] * V + row_ref[...]
-    ids_ref[8:12] = hub_id_ref[...]
+    copies = [
+        pltpu.make_async_copy(source, target, sems.at[index])
+        for index, (source, target) in enumerate(
+            (
+                (owner, owner_scr),
+                (row, row_scr),
+                (hub_id, hub_id_scr),
+                (hub, hub_scr),
+                (feat, mine_ref.at[pl.ds(0, HALF)]),
+                (feat, both_ref.at[pl.ds(0, HALF)]),
+                (cot, both_ref.at[pl.ds(HALF, HALF)]),
+            )
+        )
+    ]
+    for copy in copies:
+        copy.start()
+    for copy in copies:
+        copy.wait()
+    ids_ref[0:8] = owner_scr[...].reshape(8, V) * V + row_scr[...]
+    ids_ref[8:12] = hub_id_scr[...]
     ids_ref[12:16] = jnp.full((4, V), -1, jnp.int32)
-    mine_ref[0:HALF] = feat_ref[...]
     pick = lax.broadcasted_iota(jnp.int32, (HUB_ROWS, 2 * HUB_ROWS), 1) == (
         2 * lax.broadcasted_iota(jnp.int32, (HUB_ROWS, 2 * HUB_ROWS), 0) + parity
     )
-    columns = hub_ref[:, pl.ds(pl.multiple_of(half * COLS, COLS), COLS)]
+    columns = hub_scr[:, pl.ds(pl.multiple_of(half * COLS, COLS), COLS)]
     mine_ref[HALF:BLOCK] = dot(pick.astype(F32).astype(BF), columns).astype(BF)
-    both_ref[0:HALF] = feat_ref[...]
-    both_ref[HALF:V] = cot_ref[...]
-
-
-def counts_kernel(place, ids0, ids1, ids2, ids3, out_ref):
+
+
+def counts_kernel(place, *refs, number):
+    out_ref = refs[-1]
     y, z, c, x = place[0], place[1], place[2], place[3]
     parity = x // 2
     rows = lax.broadcasted_iota(jnp.int32, (16, 16, 128), 0) * 16 + lax.broadcasted_iota(
@@ -99,10 +118,10 @@
     def pair(a):
         return jnp.concatenate([a, a], 0).astype(BF)
 
-    for dy, ids_ref in enumerate((ids0, ids1, ids2, ids3)):
+    for dy, ids_ref in enumerate(refs[:number]):
 
         def part(dc, carry, dy=dy, ids_ref=ids_ref):
-            index = dc * NY + dy
+            index = dc * number + dy
             ids = ids_ref[dc]
             flat, hub = ids[0:8], ids[8:16]
             here = ((flat >> 9) & mask) == column
@@ -152,7 +171,23 @@
         lax.fori_loop(0, NC, part, 0)
 
 
-def far_sums_kernel(place, counts, t0, t1, t7, t23, t65, t4, sums_ref, turned_ref, table):
+def near_counts_kernel(place, ids, t0, t1, t7, fg0, fg1, out_ref, ahead, behind, skip, both, token):
+    ahead[0:BLOCK] = t0[...]
+    ahead[BLOCK:] = t1[...]
+    behind[0:BLOCK] = t0[...]
+    behind[BLOCK:] = t7[...]
+    skip[...] = t1[...]
+    both[0:V] = fg0[...]
+    both[V:] = fg1[...]
+    token[...] = place[0] + jnp.zeros_like(token)
+    counts_kernel(place, ids, out_ref, number=1)
+
+
+def far_counts_kernel(place, token, ids1, ids2, ids3, out_ref):
+    counts_kernel(place, ids1, ids2, ids3, out_ref, number=NY - 1)
+
+
+def far_sums_kernel(place, counts0, counts, t0, t1, t7, t23, t65, t4, sums_ref, turned_ref, table):
     blocks = {0: t0[...], 1: t1[...], 7: t7[...], 4: t4[...]}
     blocks[2], blocks[3] = t23[0:BLOCK], t23[BLOCK : 2 * BLOCK]
     blocks[6], blocks[5] = t65[0:BLOCK], t65[BLOCK : 2 * BLOCK]
@@ -162,20 +197,23 @@
         table[start : start + HUB_ROWS] = blocks[delta][HALF:BLOCK]
         table[start + HUB_ROWS : start + 2 * HUB_ROWS] = jnp.zeros((HUB_ROWS, COLS), BF)
     turned_ref[...] = table[...].T
+    sums_ref[0] = dot(turned_ref[...], counts0[1]).astype(BF)
 
     def step(dy, carry):
-        sums_ref[dy] = dot(turned_ref[...], counts[NY + dy]).astype(BF)
+        sums_ref[dy] = dot(turned_ref[...], counts[NY - 2 + dy]).astype(BF)
         return carry
 
-    lax.fori_loop(0, NY, step, 0)
-
-
-def near_sums_kernel(place, counts, turned, sums_ref):
+    lax.fori_loop(1, NY, step, 0)
+
+
+def near_sums_kernel(place, counts0, counts, turned, sums_ref):
+    sums_ref[0] = dot(turned[...], counts0[0])
+
     def step(dy, carry):
-        sums_ref[dy] = dot(turned[...], counts[dy])
+        sums_ref[dy] = dot(turned[...], counts[dy - 1])
         return carry
 
-    lax.fori_loop(0, NY, step, 0)
+    lax.fori_loop(1, NY, step, 0)
 
 
 def dense_kernel(
@@ -231,36 +269,34 @@
             message_ref[start : start + 64, :] = part[:, h * COLS : (h + 1) * COLS].astype(BF)
 
 
-def gather_kernel(place, m0, m1, m2, m3, out_ref):
-    for dy, ref in enumerate((m0, m1, m2, m3)):
-        out_ref[dy * V : (dy + 1) * V] = ref[0:V]
-    tail = slice(V, V + WROWS)
-    weight = (m0[tail].astype(F32) + m1[tail].astype(F32)) + (m2[tail].astype(F32) + m3[tail].astype(F32))
-    high = weight.astype(BF)
-    out_ref[NY * V : NY * V + WROWS] = high
-    out_ref[NY * V + WROWS :] = (weight - high.astype(F32)).astype(BF)
-
-
-def near_grads_kernel(place, counts, m0, m1, m2, m3, out_ref):
+def own_grads_kernel(place, counts0, m0, out_ref):
+    for block in range(NZ + 1):
+        out_ref[block] = dot(counts0[0, block * HALF : (block + 1) * HALF], m0[0:V])
+
+
+def near_grads_kernel(place, counts, m1, m2, m3, start, out_ref):
     for block in range(NZ + 1):
         span = slice(block * HALF, (block + 1) * HALF)
-        total = jnp.zeros((HALF, COLS), F32)
-        for dy, ref in enumerate((m0, m1, m2, m3)):
+        total = start[block]
+        for dy, ref in enumerate((m1, m2, m3)):
             total = total + dot(counts[dy, span], ref[0:V])
         out_ref[block] = total
 
 
-def far_block(counts, other, near, block):
+def far_block(counts0, counts, others, near, block):
     span = slice(block * HALF, (block + 1) * HALF)
-    total = near[block]
-    for dy in range(NY):
-        total = total + dot(counts[NY + dy, span], other[dy * V : (dy + 1) * V])
+    total = near[block] + dot(counts0[1, span], others[0][0:V])
+    for dy in range(1, NY):
+        total = total + dot(counts[NY - 2 + dy, span], others[dy][0:V])
     return total
 
 
-def first_grads_kernel(place, counts, own, other, near, up_ref, down_ref, hub_ref):
+def first_grads_kernel(
+    place, counts0, counts, m0, m1, m2, m3, o0, o1, o2, o3, near, up_ref, down_ref, hub_ref, hub4_ref
+):
     parity = place[3] // 2
-    hubs = far_block(counts, other, near, NZ)
+    others = (o0, o1, o2, o3)
+    hubs = far_block(counts0, counts, others, near, NZ)
     lane = lax.broadcasted_iota(jnp.int32, (HUB_ROWS, COLS), 1)
     low = (lane < 64) == (parity == 0)
     for delta in range(NZ):
@@ -268,47 +304,49 @@
         mine = hubs[start : start + HUB_ROWS]
         rest = pltpu.roll(hubs[start + HUB_ROWS : start + 2 * HUB_ROWS], 64, 1)
         hub_ref[delta] = jnp.where(low, mine, rest)
-    high, small = slice(NY * V, NY * V + WROWS), slice(NY * V + WROWS, NY * V + 2 * WROWS)
-    weight = (own[high].astype(F32) + own[small].astype(F32)) + (
-        other[high].astype(F32) + other[small].astype(F32)
-    )
-    weight = weight.astype(BF)
-    for delta, ref in ((4, up_ref), (5, down_ref)):
-        ref[0:HALF] = far_block(counts, other, near, delta).astype(BF)
-        ref[HALF:BLOCK] = hub_ref[delta].astype(BF)
+    hub4_ref[...] = hub_ref[4]
+    tail = slice(V, V + WROWS)
+    sums = [
+        (a[tail].astype(F32) + b[tail].astype(F32)) + (c[tail].astype(F32) + d[tail].astype(F32))
+        for a, b, c, d in ((m0, m1, m2, m3), others)
+    ]
+    weight = (sums[0] + sums[1]).astype(BF)
+    for delta, hub_delta, ref in ((4, 3, up_ref), (5, 5, down_ref)):
+        ref[0:HALF] = far_block(counts0, counts, others, near, delta).astype(BF)
+        ref[HALF:BLOCK] = hub_ref[hub_delta].astype(BF)
         ref[BLOCK:] = weight
 
 
 REST = (0, 1, 2, 3, 6, 7)
 
 
-def rest_grads_kernel(place, counts, other, near, out_ref):
+def rest_grads_kernel(place, counts0, counts, o0, o1, o2, o3, near, out_ref):
     for index, delta in enumerate(REST):
-        out_ref[index] = far_block(counts, other, near, delta)
+        out_ref[index] = far_block(counts0, counts, (o0, o1, o2, o3), near, delta)
 
 
 def hop_kernel(place, up, down, rest, hubs, next_up, next_down, *, deltas):
-    for delta, got, ref in zip(deltas, (up, down), (next_up, next_down)):
+    for (delta, hub_delta), got, ref in zip(deltas, (up, down), (next_up, next_down)):
         ref[0:HALF] = (got[0:HALF].astype(F32) + rest[REST.index(delta)]).astype(BF)
-        ref[HALF:BLOCK] = (got[HALF:BLOCK].astype(F32) + hubs[delta]).astype(BF)
+        ref[HALF:BLOCK] = (got[HALF:BLOCK].astype(F32) + hubs[hub_delta]).astype(BF)
         ref[BLOCK:] = got[BLOCK:]
 
 
-def last_hop_kernel(place, up, down, rest, hubs, next_up, hub_up, hub_here):
+def last_hop_kernel(place, up, down, rest, hubs, hub4, next_up, hub_sum):
     next_up[0:HALF] = (up[0:HALF].astype(F32) + rest[REST.index(1)]).astype(BF)
     next_up[HALF:] = up[BLOCK:]
-    hub_up[...] = up[HALF:BLOCK].astype(F32) + hubs[1]
-    hub_here[...] = down[HALF:BLOCK].astype(F32) + hubs[0]
+    arrived = up[HALF:BLOCK].astype(F32) + down[HALF:BLOCK].astype(F32)
+    hub_sum[...] = arrived + hubs[0] + hub4[...]
 
 
 def final_kernel(
-    place, self_ref, rest, first, up1, up2, up3, up4, down1, down2, down3, hub_up, hub_here,
+    place, self_ref, rest, first, up1, up2, up3, up4, down1, down2, down3, hub_sum,
     feat_ref, hub_ref, gself_ref, gnbr_ref, w_scr,
 ):
     z = place[1]
     total = rest[0] + up4[0:HALF].astype(F32) + down3[0:HALF].astype(F32)
     feat_ref[...] = (self_ref[...] + total).astype(BF)
-    hubs = hub_up[...] + hub_here[...]
+    hubs = hub_sum[...]
     shape = (2 * HUB_ROWS, HUB_ROWS)
     target = lax.broadcasted_iota(jnp.int32, shape, 0)
     source = lax.broadcasted_iota(jnp.int32, shape, 1)
@@ -334,39 +372,66 @@
     place = jnp.stack([lax.axis_index(a) for a in ("y", "z", "c", "x")]).astype(jnp.int32)
     ids, mine, fg = call(
         prepare_kernel,
-        (shaped((16, V), jnp.int32), shaped((BLOCK, COLS), BF), shaped((V, COLS), BF)),
-        (place, features, grad_out, hub_feats, nbr_owner.reshape(8, V), nbr_row, hub_ids.T),
+        (pltpu.VMEM((16, V), jnp.int32), pltpu.VMEM((BLOCK, COLS), BF), pltpu.VMEM((V, COLS), BF)),
+        (place, features, grad_out, hub_feats, nbr_owner.reshape(8, 1, V), nbr_row, hub_ids.T),
         "prepare",
-    )
-
+        scratch=[
+            pltpu.VMEM((8, 1, V), jnp.int32),
+            pltpu.VMEM((8, V), jnp.int32),
+            pltpu.VMEM((4, V), jnp.int32),
+            pltpu.VMEM((2 * HUB_ROWS, 256), BF),
+            pltpu.SemaphoreType.DMA((7,)),
+        ],
+        far=6,
+        mib=56,
+    )
+
+    pair = jnp.stack([ids, swap(ids, "c", NC, 1)])
     t1, t7 = shift(mine, "z", NZ, -1), shift(mine, "z", NZ, 1)
-    pair = jnp.stack([ids, swap(ids, "c", NC, 1)])
     fg1 = swap(fg, "x", NX, 1)
-    pairs = [pair] + [swap(pair, "y", NY, m) for m in range(1, NY)]
-    t23 = shift(jnp.concatenate([mine, t1], 0), "z", NZ, -2)
-    t65 = shift(jnp.concatenate([mine, t7], 0), "z", NZ, 2)
-    t4 = shift(t1, "z", NZ, -3)
-    fg23 = swap(jnp.concatenate([fg, fg1], 0), "x", NX, 2)
+    pairs = [swap(pair, "y", NY, m) for m in range(1, NY)]
+    counts0, ahead, behind, skip, both, token = call(
+        near_counts_kernel,
+        (
+            pltpu.VMEM((NC, ROWS, V), BF),
+            shaped((2 * BLOCK, COLS), BF),
+            shaped((2 * BLOCK, COLS), BF),
+            shaped((BLOCK, COLS), BF),
+            shaped((2 * V, COLS), BF),
+            shaped((8, 128), jnp.int32),
+        ),
+        (place, pair, mine, t1, t7, fg, fg1),
+        "near_counts",
+        flops=1 << 32,
+        mib=8,
+    )
+    t23, t65, t4 = shift(ahead, "z", NZ, -2), shift(behind, "z", NZ, 2), shift(skip, "z", NZ, -3)
+    fg23 = swap(both, "x", NX, 2)
     counts = call(
-        counts_kernel,
-        pltpu.VMEM((PARTS, ROWS, V), BF),
-        (place, *pairs),
-        "counts",
-        flops=1 << 34,
+        far_counts_kernel,
+        pltpu.VMEM((NC * (NY - 1), ROWS, V), BF),
+        (place, token, *pairs),
+        "far_counts",
+        flops=3 << 32,
         mib=8,
     )
+    t23, t65, t4, fg23 = lax.optimization_barrier((t23, t65, t4, fg23))
 
     far, turned = call(
         far_sums_kernel,
         (shaped((NY, COLS, V), BF), shaped((COLS, ROWS), BF)),
-        (place, counts, mine, t1, t7, t23, t65, t4),
+        (place, counts0, counts, mine, t1, t7, t23, t65, t4),
         "far_sums",
         scratch=[pltpu.VMEM((ROWS, COLS), BF)],
         flops=1 << 31,
     )
     got = swap(far, "c", NC, 1)
     near = call(
-        near_sums_kernel, shaped((NY, COLS, V), F32), (place, counts, turned), "near_sums", flops=1 << 31
+        near_sums_kernel,
+        shaped((NY, COLS, V), F32),
+        (place, counts0, counts, turned),
+        "near_sums",
+        flops=1 << 31,
     )
     both = near + got.astype(F32)
     total = both[0]
@@ -391,39 +456,39 @@
     )
 
     messages = [message] + [swap(message, "y", NY, m) for m in range(1, NY)]
-    own = call(
-        gather_kernel, shaped((NY * V + 2 * WROWS, COLS), BF), (place, *messages), "gather_grads"
-    )
-    other = swap(own, "c", NC, 1)
+    other = swap(message, "c", NC, 1)
+    grads_shape = shaped((NZ + 1, HALF, COLS), F32)
+    own_grads = call(own_grads_kernel, grads_shape, (place, counts0, message), "own_grads", flops=1 << 29)
+    *arrived, own_grads = lax.optimization_barrier((*messages[1:], own_grads))
+    messages = [message, *arrived]
+    others = [other] + [swap(m, "c", NC, 1) for m in arrived]
     near_grads = call(
         near_grads_kernel,
-        shaped((NZ + 1, HALF, COLS), F32),
-        (place, counts, *messages),
+        grads_shape,
+        (place, counts, *messages[1:], own_grads),
         "near_grads",
-        flops=1 << 31,
-    )
-    up0, down0, hubs = call(
+        flops=3 << 29,
+    )
+    hop_shapes = (shaped((BLOCK + WROWS, COLS), BF),) * 2
+    hub_shape = shaped((HUB_ROWS, COLS), F32)
+    up0, down0, hubs, hub4 = call(
         first_grads_kernel,
-        (
-            shaped((BLOCK + WROWS, COLS), BF),
-            shaped((BLOCK + WROWS, COLS), BF),
-            shaped((NZ, HUB_ROWS, COLS), F32),
-        ),
-        (place, counts, own, other, near_grads),
+        (*hop_shapes, shaped((NZ, HUB_ROWS, COLS), F32), hub_shape),
+        (place, counts0, counts, *messages, *others, near_grads),
         "first_grads",
         flops=1 << 29,
     )
     up1, down1 = shift(up0, "z", NZ, 1), shift(down0, "z", NZ, -1)
+    hub4 = shift(hub4, "z", NZ, 4)
     rest = call(
         rest_grads_kernel,
         shaped((len(REST), HALF, COLS), F32),
-        (place, counts, other, near_grads),
+        (place, counts0, counts, *others, near_grads),
         "rest_grads",
         flops=1 << 30,
     )
-    hop_shapes = (shaped((BLOCK + WROWS, COLS), BF),) * 2
     ups, downs = [up1], [down1]
-    for deltas in ((3, 6), (2, 7)):
+    for deltas in (((3, 2), (6, 6)), ((2, 1), (7, 7))):
         up, down = call(
             functools.partial(hop_kernel, deltas=deltas),
             hop_shapes,
@@ -432,21 +497,16 @@
         )
         ups.append(shift(up, "z", NZ, 1))
         downs.append(shift(down, "z", NZ, -1))
-    up, hub_up, hub_here = call(
+        if len(ups) == 2:
+            ups[1], downs[1], hub4 = lax.optimization_barrier((ups[1], downs[1], hub4))
+    up, hub_sum = call(
         last_hop_kernel,
-        (
-            shaped((HALF + WROWS, COLS), BF),
-            shaped((HUB_ROWS, COLS), F32),
-            shaped((HUB_ROWS, COLS), F32),
-        ),
-        (place, ups[-1], downs[-1], rest, hubs),
+        (shaped((HALF + WROWS, COLS), BF), hub_shape),
+        (place, ups[-1], downs[-1], rest, hubs, hub4),
         "last_hop",
     )
     ups.append(shift(up, "z", NZ, 1))
-    turn = (0, 2, 1, 3)
-    cross = [(z * NX + x, (z + 1) % NZ * NX + turn[x]) for z in range(NZ) for x in range(NX)]
-    hub_up = lax.ppermute(hub_up, ("z", "x"), cross)
-    hub_here = lax.ppermute(hub_here, "x", [(x, turn[x]) for x in range(NX)])
+    hub_sum = lax.ppermute(hub_sum, "x", [(0, 0), (1, 2), (2, 1), (3, 3)])
     grad_features, hub_rows, grad_self, grad_nbr = call(
         final_kernel,
         (
@@ -455,7 +515,7 @@
             shaped((64, 256), F32),
             shaped((64, 256), F32),
         ),
-        (place, self_term, rest, up0, *ups, *downs, hub_up, hub_here),
+        (place, self_term, rest, up0, *ups, *downs, hub_sum),
         "last_sums",
         scratch=[pltpu.VMEM((NZ, WROWS, COLS), BF)],
     )

time: 113 us -> 120 us (1.062); the launches traced: 112 us -> 118 us
  waiting for transfers between devices: 31.1 us -> 36.8 us
  local copies, waits for them, and re-layouts: 4.57 us -> 0.7 us
  Pallas kernels: 27.5 us -> 29.1 us
  starting transfers between devices: 47.8 us -> 49.3 us
    ppermute x17 -> x20, waiting for transfers between devices: 18.8 us -> 23.3 us  [swap(): return lax.ppermute(x, axis, [(i, i ^ mask) for i in range(size)])]
    unnamed x15 -> x8, local copies, waits for them, and re-layouts: 4.54 us -> 0.67 us
    ppermute x2 -> x1, starting transfers between devices: 5.19 us -> 1.92 us  [body(): hub_sum = lax.ppermute(hub_sum, 'x', [(0, 0), (1, 2), (2, 1), (3, 3)])]
    ppermute x17 -> x20, starting transfers between devices: 19.9 us -> 22.4 us  [swap(): return lax.ppermute(x, axis, [(i, i ^ mask) for i in range(size)])]
    ppermute x12 -> x13, starting transfers between devices: 22.8 us -> 25 us  [shift(): return lax.ppermute(x, axis, [(i, (i + step) % size) for i in range(size)])]
    ppermute x2 -> x1, waiting for transfers between devices: 1.8 us -> 3.62 us  [body(): hub_sum = lax.ppermute(hub_sum, 'x', [(0, 0), (1, 2), (2, 1), (3, 3)])]
    pallas_call x13 -> x14, Pallas kernels: 27.5 us -> 29.1 us  [call(): pl.pallas_call(kernel, out_shape=outs, in_specs=[SM] + [VM] * (len(inputs...]
    ppermute x12 -> x13, waiting for transfers between devices: 10.5 us -> 9.93 us  [shift(): return lax.ppermute(x, axis, [(i, (i + step) % size) for i in range(size)])]
  transfers between devices with their start and end apart: 31 -> 34, of which waited for: 13 -> 15; matrix products, arithmetic and copies ran while one was open for 0% -> 0% of each run, Pallas kernels for 15% -> 15%
where the time goes in v3:
time: 120 us; the launch traced here: 118 us
  starting transfers between devices  49.3 us (41%)
  waiting for transfers between devices  36.8 us (31%)
  Pallas kernels  29.1 us (24%)
    pallas_call x14, Pallas kernels, call(): pl.pallas_call(kernel, out_shape=outs, in_specs=[SM] + [VM] * (len(inputs...  29.1 us
    ppermute x13, starting transfers between devices, shift(): return lax.ppermute(x, axis, [(i, (i + step) % size) for i in range(size)])  25 us
    ppermute x20, waiting for transfers between devices, swap(): return lax.ppermute(x, axis, [(i, i ^ mask) for i in range(size)])  23.3 us
    ppermute x20, starting transfers between devices, swap(): return lax.ppermute(x, axis, [(i, i ^ mask) for i in range(size)])  22.4 us
    ppermute x13, waiting for transfers between devices, shift(): return lax.ppermute(x, axis, [(i, (i + step) % size) for i in range(size)])  9.93 us
    ppermute x1, waiting for transfers between devices, body(): hub_sum = lax.ppermute(hub_sum, 'x', [(0, 0), (1, 2), (2, 1), (3, 3)])  3.62 us
  transfers between devices with their start and end apart: 34, of which 15 were waited for; matrix products, arithmetic and copies ran while one was open for 0% of the time, Pallas kernels for 15%

profile of v3, /device:TPU:4, one launch (start us, length us, event | category | flops | bytes accessed | tf_op | source)
XLA Modules:
  0.0 117.8 jit_solution(18434073045012622479)
XLA Ops:
  4.4 5.9 %collective-permute-start.2 = (bf16[272,128]{1,0:T(8,128)(2,1)S(1)}, bf16[272,128]{1,0:T(8,128)(2,1)S(1)}, u32[]{:S(2)}, u32[]{:S(2)}) collective-permute-start(bf16[272,128]{1,0:T(8,128)(2,1)S(1)} %get-tuple-element.46.t0), channel_id=1, source_target_pairs={{0,56},{8,0},{16,8},{24,16},{32,24},{40,32},{48,40},{56,48},{1,57}... | collective-permute-start | bytes 208904 | tf_op jit(solution)/shard_map/ppermute | solution.py:34
  10.3 3.1 %collective-permute-start.10 = (s32[2,16,512]{2,1,0:T(8,128)S(1)}, s32[2,16,512]{2,1,0:T(8,128)S(1)}, u32[]{:S(2)}, u32[]{:S(2)}) collective-permute-start(s32[2,16,512]{2,1,0:T(8,128)S(1)} %pad_add_fusion.ids), channel_id=1, source_target_pairs={{0,192},{64,128},{128,64},{192,0},{1,193},{65,129},{129,65},{193,1... | collective-permute-start | bytes 196616 | tf_op jit(solution)/shard_map/ppermute | solution.py:38
  16.5 2.7 %near_counts.1 = (bf16[2,2304,512]{2,1,0:T(8,128)(2,1)S(1)}, bf16[544,128]{1,0:T(8,128)(2,1)S(1)}, bf16[544,128]{1,0:T(8,128)(2,1)S(1)}, bf16[272,128]{1,0:T(8,1...) custom-call(s32[4]{0:T(128)S(1)} %copy-done, s32[2,16,512]{2,1,0:T(8,128)S(1)} %pad_add_fusion.ids, ...), custom_call_target="tpu_custom_call" | custom-call | flops 4294967296 | bytes 262144 | tf_op jit(solution)/shard_map/near_counts/pallas_call | solution.py:42
  20.0 2.4 %collective-permute-start.4 = (bf16[544,128]{1,0:T(8,128)(2,1)S(1)}, bf16[544,128]{1,0:T(8,128)(2,1)S(1)}, u32[]{:S(2)}, u32[]{:S(2)}) collective-permute-start(bf16[544,128]{1,0:T(8,128)(2,1)S(1)} %get-tuple-element.47), channel_id=1, source_target_pairs={{0,48},{8,56},{16,0},{24,8},{32,16},{40,24},{48,32},{56,40},{1,49}... | collective-permute-start | bytes 417800 | tf_op jit(solution)/shard_map/ppermute | solution.py:34
  23.0 2.9 %collective-permute-start.6 = (bf16[272,128]{1,0:T(8,128)(2,1)S(1)}, bf16[272,128]{1,0:T(8,128)(2,1)S(1)}, u32[]{:S(2)}, u32[]{:S(2)}) collective-permute-start(bf16[272,128]{1,0:T(8,128)(2,1)S(1)} %get-tuple-element.49), channel_id=1, source_target_pairs={{0,40},{8,48},{16,56},{24,0},{32,8},{40,16},{48,24},{56,32},{1,41}... | collective-permute-start | bytes 208904 | tf_op jit(solution)/shard_map/ppermute | solution.py:34
  25.9 6.8 %far_counts.1.counts = bf16[6,2304,512]{2,1,0:T(8,128)(2,1)S(1)} custom-call(s32[4]{0:T(128)S(1)} %copy-done, s32[8,128]{1,0:T(8,128)S(1)} %get-tuple-element.53.token, s32[2,16,512]{2,1,0:T(8,128)S(1)} %collective-permute-done.8.ids1, s32[2,16,512]{2,1,0:T(8,128)S(1)} %collective-permute-done.9.ids2, s32[2,16,512]{2,1,0:T(8,128)S(1)} %collective-permute-done.10.ids3), custom_call_target="tpu_custom_call" | custom-call | flops 12884901888 | bytes 262144 | tf_op jit(solution)/shard_map/far_counts/pallas_call | solution.py:42
  32.7 2.5 %far_sums.1 = (bf16[4,128,512]{2,1,0:T(8,128)(2,1)S(1)}, bf16[128,2304]{1,0:T(8,128)(2,1)S(1)}) custom-call(s32[4]{0:T(128)S(1)} %copy-done.1, bf16[2,2304,512]{2,1,0:T(8,128)(2,1)S(1)} %get-tuple-element.52.counts0, bf16[6,2304,512]{2,1,0:T(8,128)(2,1)S(1)} %far_counts.1.counts, bf16[272,128]{1,0:T(8,128)(2,1)S(1)} %get-tuple-element.46.t0, ...), custom_call_target="tpu_custom_call" | custom-call | flops 2147483648 | bytes 262144 | tf_op jit(solution)/shard_map/far_sums/pallas_call | solution.py:42
  35.3 2.5 %near_sums.1 = f32[4,128,512]{2,1,0:T(8,128)S(1)} custom-call(s32[4]{0:T(128)S(1)} %copy-done.1, bf16[2,2304,512]{2,1,0:T(8,128)(2,1)S(1)} %get-tuple-element.52.counts0, bf16[6,2304,512]{2,1,0:T(8,128)(2,1)S(1)} %far_counts.1.counts, bf16[128,2304]{1,0:T(8,128)(2,1)S(1)} %get-tuple-element.57.turned), custom_call_target="tpu_custom_call" | custom-call | flops 2147483648 | bytes 262144 | tf_op jit(solution)/shard_map/near_sums/pallas_call | solution.py:42
  39.7 3.0 %collective-permute-start.13 = (bf16[128,512]{1,0:T(8,128)(2,1)S(1)}, bf16[128,512]{1,0:T(8,128)(2,1)S(1)}, u32[]{:S(2)}, u32[]{:S(2)}) collective-permute-start(bf16[128,512]{1,0:T(8,128)(2,1)S(1)} %get-tuple-element.87), channel_id=1, source_target_pairs={{0,128},{64,192},{128,0},{192,64},{1,129},{65,193},{129,1},{193,65... | collective-permute-start | bytes 393224 | tf_op jit(solution)/shard_map/ppermute | solution.py:38
  44.5 4.5 %collective-permute-done.13 = bf16[128,512]{1,0:T(8,128)(2,1)S(1)} collective-permute-done((bf16[128,512]{1,0:T(8,128)(2,1)S(1)}, bf16[128,512]{1,0:T(8,128)(2,1)S(1)}, u32[]{:S(2)}, u32[]{:S(2)}) %collective-permute-start.13) | collective-permute-done | bytes 131104 | tf_op jit(solution)/shard_map/ppermute | solution.py:38
  49.0 2.2 %collective-permute-done.14 = bf16[128,512]{1,0:T(8,128)(2,1)S(1)} collective-permute-done((bf16[128,512]{1,0:T(8,128)(2,1)S(1)}, bf16[128,512]{1,0:T(8,128)(2,1)S(1)}, u32[]{:S(2)}, u32[]{:S(2)}) %collective-permute-start.14) | collective-permute-done | bytes 131104 | tf_op jit(solution)/shard_map/ppermute | solution.py:38
  52.4 3.4 %collective-permute-start.16 = (bf16[128,512]{1,0:T(8,128)(2,1)S(1)}, bf16[128,512]{1,0:T(8,128)(2,1)S(1)}, u32[]{:S(2)}, u32[]{:S(2)}) collective-permute-start(bf16[128,512]{1,0:T(8,128)(2,1)S(1)} %fusion.3.s0), channel_id=1, source_target_pairs={{0,2},{1,3},{2,0},{3,1},{4,6},{5,7},{6,4},{7,5},{8,10},{9,11},{10,... | collective-permute-start | bytes 393224 | tf_op jit(solution)/shard_map/ppermute | solution.py:38
  56.3 5.7 %collective-permute-done.16.s2 = bf16[128,512]{1,0:T(8,128)(2,1)S(1)} collective-permute-done((bf16[128,512]{1,0:T(8,128)(2,1)S(1)}, bf16[128,512]{1,0:T(8,128)(2,1)S(1)}, u32[]{:S(2)}, u32[]{:S(2)}) %collective-permute-start.16) | collective-permute-done | bytes 131104 | tf_op jit(solution)/shard_map/ppermute | solution.py:38
  65.4 3.1 %collective-permute-start.20 = (bf16[768,128]{1,0:T(8,128)(2,1)S(1)}, bf16[768,128]{1,0:T(8,128)(2,1)S(1)}, u32[]{:S(2)}, u32[]{:S(2)}) collective-permute-start(bf16[768,128]{1,0:T(8,128)(2,1)S(1)} %get-tuple-element.61.m0), channel_id=1, source_target_pairs={{0,128},{64,192},{128,0},{192,64},{1,129},{65,193},{129,1},{193,65... | collective-permute-start | bytes 589832 | tf_op jit(solution)/shard_map/ppermute | solution.py:38
  73.3 3.5 %collective-permute-done.20.m2 = bf16[768,128]{1,0:T(8,128)(2,1)S(1)} collective-permute-done((bf16[768,128]{1,0:T(8,128)(2,1)S(1)}, bf16[768,128]{1,0:T(8,128)(2,1)S(1)}, u32[]{:S(2)}, u32[]{:S(2)}) %collective-permute-start.20) | collective-permute-done | bytes 196640 | tf_op jit(solution)/shard_map/ppermute | solution.py:38
  76.8 2.4 %collective-permute-done.21.m3 = bf16[768,128]{1,0:T(8,128)(2,1)S(1)} collective-permute-done((bf16[768,128]{1,0:T(8,128)(2,1)S(1)}, bf16[768,128]{1,0:T(8,128)(2,1)S(1)}, u32[]{:S(2)}, u32[]{:S(2)}) %collective-permute-start.21) | collective-permute-done | bytes 196640 | tf_op jit(solution)/shard_map/ppermute | solution.py:38
  79.7 2.5 %near_grads.1.near = f32[9,256,128]{2,1,0:T(8,128)S(1)} custom-call(s32[4]{0:T(128)S(1)} %copy-done.1, bf16[6,2304,512]{2,1,0:T(8,128)(2,1)S(1)} %far_counts.1.counts, bf16[768,128]{1,0:T(8,128)(2,1)S(1)} %collective-permute-done.19.m1, bf16[768,128]{1,0:T(8,128)(2,1)S(1)} %collective-permute-done.20.m2, bf16[768,128]{1,0:T(8,128)(2,1)S(1)} %collective-permute-done.21.m3, ...), custom_call_target="tpu_custom_call" | custom-call | flops 1610612736 | bytes 262144 | tf_op jit(solution)/shard_map/near_grads/pallas_call | solution.py:42
  87.2 2.3 %rest_grads.1.rest = f32[6,256,128]{2,1,0:T(8,128)S(1)} custom-call(s32[4]{0:T(128)S(1)} %copy-done.1, bf16[2,2304,512]{2,1,0:T(8,128)(2,1)S(1)} %get-tuple-element.52.counts0, bf16[6,2304,512]{2,1,0:T(8,128)(2,1)S(1)} %far_counts.1.counts, bf16[768,128]{1,0:T(8,128)(2,1)S(1)} %collective-permute-done.18.o0, ...), custom_call_target="tpu_custom_call" | custom-call | flops 1073741824 | bytes 262144 | tf_op jit(solution)/shard_map/rest_grads/pallas_call | solution.py:42
  92.5 2.6 %collective-permute-start.28 = (bf16[528,128]{1,0:T(8,128)(2,1)S(1)}, bf16[528,128]{1,0:T(8,128)(2,1)S(1)}, u32[]{:S(2)}, u32[]{:S(2)}) collective-permute-start(bf16[528,128]{1,0:T(8,128)(2,1)S(1)} %get-tuple-element.70), channel_id=1, source_target_pairs={{0,56},{8,0},{16,8},{24,16},{32,24},{40,32},{48,40},{56,48},{1,57}... | collective-permute-start | bytes 405512 | tf_op jit(solution)/shard_map/ppermute | solution.py:34
  95.1 3.3 %collective-permute-start.29 = (f32[16,128]{1,0:T(8,128)S(1)}, f32[16,128]{1,0:T(8,128)S(1)}, u32[]{:S(2)}, u32[]{:S(2)}) collective-permute-start(f32[16,128]{1,0:T(8,128)S(1)} %get-tuple-element.71), channel_id=1, source_target_pairs={{0,32},{8,40},{16,48},{24,56},{32,0},{40,8},{48,16},{56,24},{1,33}... | collective-permute-start | bytes 24584 | tf_op jit(solution)/shard_map/ppermute | solution.py:34
  98.4 4.3 %collective-permute-done.29.hub4 = f32[16,128]{1,0:T(8,128)S(1)} collective-permute-done((f32[16,128]{1,0:T(8,128)S(1)}, f32[16,128]{1,0:T(8,128)S(1)}, u32[]{:S(2)}, u32[]{:S(2)}) %collective-permute-start.29) | collective-permute-done | bytes 8224 | tf_op jit(solution)/shard_map/ppermute | solution.py:34
  103.3 3.2 %collective-permute-start.31 = (bf16[528,128]{1,0:T(8,128)(2,1)S(1)}, bf16[528,128]{1,0:T(8,128)(2,1)S(1)}, u32[]{:S(2)}, u32[]{:S(2)}) collective-permute-start(bf16[528,128]{1,0:T(8,128)(2,1)S(1)} %get-tuple-element.75), channel_id=1, source_target_pairs={{0,56},{8,0},{16,8},{24,16},{32,24},{40,32},{48,40},{56,48},{1,57}... | collective-permute-start | bytes 405512 | tf_op jit(solution)/shard_map/ppermute | solution.py:34
  106.6 3.0 %collective-permute-done.30.up.up3 = bf16[528,128]{1,0:T(8,128)(2,1)S(1)} collective-permute-done((bf16[528,128]{1,0:T(8,128)(2,1)S(1)}, bf16[528,128]{1,0:T(8,128)(2,1)S(1)}, u32[]{:S(2)}, u32[]{:S(2)}) %collective-permute-start.30) | collective-permute-done | bytes 135200 | tf_op jit(solution)/shard_map/ppermute | solution.py:34
  112.1 3.6 %collective-permute-done.33.hub_sum = f32[16,128]{1,0:T(8,128)S(1)} collective-permute-done((f32[16,128]{1,0:T(8,128)S(1)}, f32[16,128]{1,0:T(8,128)S(1)}, u32[]{:S(2)}, u32[]{:S(2)}) %collective-permute-start.33) | collective-permute-done | bytes 8224 | tf_op jit(solution)/shard_map/ppermute | solution.py:509
  (71 shorter events, 35.7 us)
Async XLA Ops:
  3.0 7.2 %collective-permute-start.1 = (s32[16,512]{1,0:T(8,128)S(1)}, s32[16,512]{1,0:T(8,128)S(1)}, u32[]{:S(2)}, u32[]{:S(2)}) collective-permute-start(s32[16,512]{1,0:T(8,128)S(1)} %get-tuple-element.45), channel_id=1, source_target_pairs={{0,4},{4,0},{1,5},{5,1},{2,6},{6,2},{3,7},{7,3},{8,12},{12,8},{9,1... | collective-permute-start | bytes 98312 | tf_op jit(solution)/shard_map/ppermute | solution.py:38
  3.2 12.7 %collective-permute-start = (bf16[512,128]{1,0:T(8,128)(2,1)S(1)}, bf16[512,128]{1,0:T(8,128)(2,1)S(1)}, u32[]{:S(2)}, u32[]{:S(2)}) collective-permute-start(bf16[512,128]{1,0:T(8,128)(2,1)S(1)} %get-tuple-element.44.fg0), channel_id=1, source_target_pairs={{0,1},{1,0},{2,3},{3,2},{4,5},{5,4},{6,7},{7,6},{8,9},{9,8},{10,11... | collective-permute-start | bytes 393224 | tf_op jit(solution)/shard_map/ppermute | solution.py:38
  4.4 9.1 %collective-permute-start.2 = (bf16[272,128]{1,0:T(8,128)(2,1)S(1)}, bf16[272,128]{1,0:T(8,128)(2,1)S(1)}, u32[]{:S(2)}, u32[]{:S(2)}) collective-permute-start(bf16[272,128]{1,0:T(8,128)(2,1)S(1)} %get-tuple-element.46.t0), channel_id=1, source_target_pairs={{0,56},{8,0},{16,8},{24,16},{32,24},{40,32},{48,40},{56,48},{1,57}... | collective-permute-start | bytes 208904 | tf_op jit(solution)/shard_map/ppermute | solution.py:34
  10.3 12.2 %collective-permute-start.10 = (s32[2,16,512]{2,1,0:T(8,128)S(1)}, s32[2,16,512]{2,1,0:T(8,128)S(1)}, u32[]{:S(2)}, u32[]{:S(2)}) collective-permute-start(s32[2,16,512]{2,1,0:T(8,128)S(1)} %pad_add_fusion.ids), channel_id=1, source_target_pairs={{0,192},{64,128},{128,64},{192,0},{1,193},{65,129},{129,65},{193,1... | collective-permute-start | bytes 196616 | tf_op jit(solution)/shard_map/ppermute | solution.py:38
  13.4 9.6 %collective-permute-start.8 = (s32[2,16,512]{2,1,0:T(8,128)S(1)}, s32[2,16,512]{2,1,0:T(8,128)S(1)}, u32[]{:S(2)}, u32[]{:S(2)}) collective-permute-start(s32[2,16,512]{2,1,0:T(8,128)S(1)} %pad_add_fusion.ids), channel_id=1, source_target_pairs={{0,64},{64,0},{128,192},{192,128},{1,65},{65,1},{129,193},{193,129... | collective-permute-start | bytes 196616 | tf_op jit(solution)/shard_map/ppermute | solution.py:38
  13.6 12.3 %collective-permute-start.9 = (s32[2,16,512]{2,1,0:T(8,128)S(1)}, s32[2,16,512]{2,1,0:T(8,128)S(1)}, u32[]{:S(2)}, u32[]{:S(2)}) collective-permute-start(s32[2,16,512]{2,1,0:T(8,128)S(1)} %pad_add_fusion.ids), channel_id=1, source_target_pairs={{0,128},{64,192},{128,0},{192,64},{1,129},{65,193},{129,1},{193,65... | collective-permute-start | bytes 196616 | tf_op jit(solution)/shard_map/ppermute | solution.py:38
  19.2 13.5 %collective-permute-start.7 = (bf16[1024,128]{1,0:T(8,128)(2,1)S(1)}, bf16[1024,128]{1,0:T(8,128)(2,1)S(1)}, u32[]{:S(2)}, u32[]{:S(2)}) collective-permute-start(bf16[1024,128]{1,0:T(8,128)(2,1)S(1)} %get-tuple-element.50), channel_id=1, source_target_pairs={{0,2},{1,3},{2,0},{3,1},{4,6},{5,7},{6,4},{7,5},{8,10},{9,11},{10,... | collective-permute-start | bytes 786440 | tf_op jit(solution)/shard_map/ppermute | solution.py:38
  20.0 12.6 %collective-permute-start.4 = (bf16[544,128]{1,0:T(8,128)(2,1)S(1)}, bf16[544,128]{1,0:T(8,128)(2,1)S(1)}, u32[]{:S(2)}, u32[]{:S(2)}) collective-permute-start(bf16[544,128]{1,0:T(8,128)(2,1)S(1)} %get-tuple-element.47), channel_id=1, source_target_pairs={{0,48},{8,56},{16,0},{24,8},{32,16},{40,24},{48,32},{56,40},{1,49}... | collective-permute-start | bytes 417800 | tf_op jit(solution)/shard_map/ppermute | solution.py:34
  22.5 10.2 %collective-permute-start.5 = (bf16[544,128]{1,0:T(8,128)(2,1)S(1)}, bf16[544,128]{1,0:T(8,128)(2,1)S(1)}, u32[]{:S(2)}, u32[]{:S(2)}) collective-permute-start(bf16[544,128]{1,0:T(8,128)(2,1)S(1)} %get-tuple-element.48), channel_id=1, source_target_pairs={{0,16},{8,24},{16,32},{24,40},{32,48},{40,56},{48,0},{56,8},{1,17}... | collective-permute-start | bytes 417800 | tf_op jit(solution)/shard_map/ppermute | solution.py:34
  23.0 9.7 %collective-permute-start.6 = (bf16[272,128]{1,0:T(8,128)(2,1)S(1)}, bf16[272,128]{1,0:T(8,128)(2,1)S(1)}, u32[]{:S(2)}, u32[]{:S(2)}) collective-permute-start(bf16[272,128]{1,0:T(8,128)(2,1)S(1)} %get-tuple-element.49), channel_id=1, source_target_pairs={{0,40},{8,48},{16,56},{24,0},{32,8},{40,16},{48,24},{56,32},{1,41}... | collective-permute-start | bytes 208904 | tf_op jit(solution)/shard_map/ppermute | solution.py:34
  38.1 6.4 %collective-permute-start.12 = (bf16[128,512]{1,0:T(8,128)(2,1)S(1)}, bf16[128,512]{1,0:T(8,128)(2,1)S(1)}, u32[]{:S(2)}, u32[]{:S(2)}) collective-permute-start(bf16[128,512]{1,0:T(8,128)(2,1)S(1)} %get-tuple-element.85), channel_id=1, source_target_pairs={{0,64},{64,0},{128,192},{192,128},{1,65},{65,1},{129,193},{193,129... | collective-permute-start | bytes 393224 | tf_op jit(solution)/shard_map/ppermute | solution.py:38
  39.7 9.3 %collective-permute-start.13 = (bf16[128,512]{1,0:T(8,128)(2,1)S(1)}, bf16[128,512]{1,0:T(8,128)(2,1)S(1)}, u32[]{:S(2)}, u32[]{:S(2)}) collective-permute-start(bf16[128,512]{1,0:T(8,128)(2,1)S(1)} %get-tuple-element.87), channel_id=1, source_target_pairs={{0,128},{64,192},{128,0},{192,64},{1,129},{65,193},{129,1},{193,65... | collective-permute-start | bytes 393224 | tf_op jit(solution)/shard_map/ppermute | solution.py:38
  42.7 8.5 %collective-permute-start.14 = (bf16[128,512]{1,0:T(8,128)(2,1)S(1)}, bf16[128,512]{1,0:T(8,128)(2,1)S(1)}, u32[]{:S(2)}, u32[]{:S(2)}) collective-permute-start(bf16[128,512]{1,0:T(8,128)(2,1)S(1)} %get-tuple-element.86), channel_id=1, source_target_pairs={{0,192},{64,128},{128,64},{192,0},{1,193},{65,129},{129,65},{193,1... | collective-permute-start | bytes 393224 | tf_op jit(solution)/shard_map/ppermute | solution.py:38
  52.4 9.5 %collective-permute-start.16 = (bf16[128,512]{1,0:T(8,128)(2,1)S(1)}, bf16[128,512]{1,0:T(8,128)(2,1)S(1)}, u32[]{:S(2)}, u32[]{:S(2)}) collective-permute-start(bf16[128,512]{1,0:T(8,128)(2,1)S(1)} %fusion.3.s0), channel_id=1, source_target_pairs={{0,2},{1,3},{2,0},{3,1},{4,6},{5,7},{6,4},{7,5},{8,10},{9,11},{10,... | collective-permute-start | bytes 393224 | tf_op jit(solution)/shard_map/ppermute | solution.py:38
  55.8 7.6 %collective-permute-start.17 = (bf16[128,512]{1,0:T(8,128)(2,1)S(1)}, bf16[128,512]{1,0:T(8,128)(2,1)S(1)}, u32[]{:S(2)}, u32[]{:S(2)}) collective-permute-start(bf16[128,512]{1,0:T(8,128)(2,1)S(1)} %fusion.3.s0), channel_id=1, source_target_pairs={{0,3},{1,2},{2,1},{3,0},{4,7},{5,6},{6,5},{7,4},{8,11},{9,10},{10,... | collective-permute-start | bytes 393224 | tf_op jit(solution)/shard_map/ppermute | solution.py:38
  65.4 7.9 %collective-permute-start.19 = (bf16[768,128]{1,0:T(8,128)(2,1)S(1)}, bf16[768,128]{1,0:T(8,128)(2,1)S(1)}, u32[]{:S(2)}, u32[]{:S(2)}) collective-permute-start(bf16[768,128]{1,0:T(8,128)(2,1)S(1)} %get-tuple-element.61.m0), channel_id=1, source_target_pairs={{0,64},{64,0},{128,192},{192,128},{1,65},{65,1},{129,193},{193,129... | collective-permute-start | bytes 589832 | tf_op jit(solution)/shard_map/ppermute | solution.py:38
  65.4 11.4 %collective-permute-start.20 = (bf16[768,128]{1,0:T(8,128)(2,1)S(1)}, bf16[768,128]{1,0:T(8,128)(2,1)S(1)}, u32[]{:S(2)}, u32[]{:S(2)}) collective-permute-start(bf16[768,128]{1,0:T(8,128)(2,1)S(1)} %get-tuple-element.61.m0), channel_id=1, source_target_pairs={{0,128},{64,192},{128,0},{192,64},{1,129},{65,193},{129,1},{193,65... | collective-permute-start | bytes 589832 | tf_op jit(solution)/shard_map/ppermute | solution.py:38
  68.5 10.7 %collective-permute-start.21 = (bf16[768,128]{1,0:T(8,128)(2,1)S(1)}, bf16[768,128]{1,0:T(8,128)(2,1)S(1)}, u32[]{:S(2)}, u32[]{:S(2)}) collective-permute-start(bf16[768,128]{1,0:T(8,128)(2,1)S(1)} %get-tuple-element.61.m0), channel_id=1, source_target_pairs={{0,192},{64,128},{128,64},{192,0},{1,193},{65,129},{129,65},{193,1... | collective-permute-start | bytes 589832 | tf_op jit(solution)/shard_map/ppermute | solution.py:38
  70.1 12.1 %collective-permute-start.18 = (bf16[768,128]{1,0:T(8,128)(2,1)S(1)}, bf16[768,128]{1,0:T(8,128)(2,1)S(1)}, u32[]{:S(2)}, u32[]{:S(2)}) collective-permute-start(bf16[768,128]{1,0:T(8,128)(2,1)S(1)} %get-tuple-element.61.m0), channel_id=1, source_target_pairs={{0,4},{4,0},{1,5},{5,1},{2,6},{6,2},{3,7},{7,3},{8,12},{12,8},{9,1... | collective-permute-start | bytes 589832 | tf_op jit(solution)/shard_map/ppermute | solution.py:38
  83.9 7.3 %collective-permute-start.25 = (bf16[528,128]{1,0:T(8,128)(2,1)S(1)}, bf16[528,128]{1,0:T(8,128)(2,1)S(1)}, u32[]{:S(2)}, u32[]{:S(2)}) collective-permute-start(bf16[528,128]{1,0:T(8,128)(2,1)S(1)} %get-tuple-element.66.first), channel_id=1, source_target_pairs={{0,8},{8,16},{16,24},{24,32},{32,40},{40,48},{48,56},{56,0},{1,9},... | collective-permute-start | bytes 405512 | tf_op jit(solution)/shard_map/ppermute | solution.py:34
  91.8 10.9 %collective-permute-start.27 = (bf16[528,128]{1,0:T(8,128)(2,1)S(1)}, bf16[528,128]{1,0:T(8,128)(2,1)S(1)}, u32[]{:S(2)}, u32[]{:S(2)}) collective-permute-start(bf16[528,128]{1,0:T(8,128)(2,1)S(1)} %get-tuple-element.69), channel_id=1, source_target_pairs={{0,8},{8,16},{16,24},{24,32},{32,40},{40,48},{48,56},{56,0},{1,9},... | collective-permute-start | bytes 405512 | tf_op jit(solution)/shard_map/ppermute | solution.py:34
  92.5 10.1 %collective-permute-start.28 = (bf16[528,128]{1,0:T(8,128)(2,1)S(1)}, bf16[528,128]{1,0:T(8,128)(2,1)S(1)}, u32[]{:S(2)}, u32[]{:S(2)}) collective-permute-start(bf16[528,128]{1,0:T(8,128)(2,1)S(1)} %get-tuple-element.70), channel_id=1, source_target_pairs={{0,56},{8,0},{16,8},{24,16},{32,24},{40,32},{48,40},{56,48},{1,57}... | collective-permute-start | bytes 405512 | tf_op jit(solution)/shard_map/ppermute | solution.py:34
  95.1 7.6 %collective-permute-start.29 = (f32[16,128]{1,0:T(8,128)S(1)}, f32[16,128]{1,0:T(8,128)S(1)}, u32[]{:S(2)}, u32[]{:S(2)}) collective-permute-start(f32[16,128]{1,0:T(8,128)S(1)} %get-tuple-element.71), channel_id=1, source_target_pairs={{0,32},{8,40},{16,48},{24,56},{32,0},{40,8},{48,16},{56,24},{1,33}... | collective-permute-start | bytes 24584 | tf_op jit(solution)/shard_map/ppermute | solution.py:34
  103.2 6.3 %collective-permute-start.30 = (bf16[528,128]{1,0:T(8,128)(2,1)S(1)}, bf16[528,128]{1,0:T(8,128)(2,1)S(1)}, u32[]{:S(2)}, u32[]{:S(2)}) collective-permute-start(bf16[528,128]{1,0:T(8,128)(2,1)S(1)} %get-tuple-element.74), channel_id=1, source_target_pairs={{0,8},{8,16},{16,24},{24,32},{32,40},{40,48},{48,56},{56,0},{1,9},... | collective-permute-start | bytes 405512 | tf_op jit(solution)/shard_map/ppermute | solution.py:34
  (14 other events, 104.2 us)

commit v4 on v2

--- a/solution.py
+++ b/solution.py
@@ -20,7 +20,6 @@
 BF = jnp.bfloat16
 F32 = jnp.float32
 VM = pl.BlockSpec(memory_space=pltpu.VMEM)
-SM = pl.BlockSpec(memory_space=pltpu.SMEM)
 PLAIN = (((1,), (0,)), ((), ()))
 LAST = (((1,), (1,)), ((), ()))
 FIRST = (((0,), (0,)), ((), ()))
@@ -38,12 +37,15 @@
     return lax.ppermute(x, axis, [(i, i ^ mask) for i in range(size)])
 
 
-def call(kernel, outs, inputs, name, scratch=(), flops=0, mib=16):
+def call(kernel, outs, inputs, name, scratch=(), flops=0, mib=16, far=0, far_outs=0):
+    out_specs = jax.tree.map(lambda _: VM, outs)
+    if far_outs:
+        out_specs = (*out_specs[:-far_outs], *[pl.BlockSpec(memory_space=pl.ANY)] * far_outs)
     return pl.pallas_call(
         kernel,
         out_shape=outs,
-        in_specs=[SM] + [VM] * (len(inputs) - 1),
-        out_specs=jax.tree.map(lambda _: VM, outs),
+        in_specs=[VM] * (len(inputs) - far) + [pl.BlockSpec(memory_space=pl.ANY)] * far,
+        out_specs=out_specs,
         scratch_shapes=list(scratch),
         compiler_params=pltpu.CompilerParams(vmem_limit_bytes=mib << 20),
         cost_estimate=pl.CostEstimate(flops=flops, bytes_accessed=1 << 18, transcendentals=0),
@@ -55,23 +57,45 @@
     return jax.ShapeDtypeStruct(shape, dtype)
 
 
-def prepare_kernel(place, feat_ref, cot_ref, hub_ref, owner_ref, row_ref, hub_id_ref, ids_ref, mine_ref, both_ref):
-    parity, half = place[3] // 2, place[3] % 2
-    ids_ref[0:8] = owner_ref[...] * V + row_ref[...]
-    ids_ref[8:12] = hub_id_ref[...]
+def prepare_kernel(
+    feat, cot, hub, owner, row, hub_id, ids_ref, mine_ref, both,
+    owner_scr, row_scr, hub_id_scr, hub_scr, sems,
+):
+    parity, half = lax.axis_index("x") // 2, lax.axis_index("x") % 2
+    copies = [
+        pltpu.make_async_copy(source, target, sems.at[index])
+        for index, (source, target) in enumerate(
+            (
+                (owner, owner_scr),
+                (row, row_scr),
+                (hub_id, hub_id_scr),
+                (hub, hub_scr),
+                (feat, mine_ref.at[pl.ds(0, HALF)]),
+                (feat, both.at[pl.ds(0, HALF)]),
+                (cot, both.at[pl.ds(HALF, HALF)]),
+                (feat, both.at[pl.ds(V, HALF)]),
+                (cot, both.at[pl.ds(V + HALF, HALF)]),
+            )
+        )
+    ]
+    for copy in copies:
+        copy.start()
+    for copy in copies[:5]:
+        copy.wait()
+    ids_ref[0:8] = owner_scr[...].reshape(8, V) * V + row_scr[...]
+    ids_ref[8:12] = hub_id_scr[...]
     ids_ref[12:16] = jnp.full((4, V), -1, jnp.int32)
-    mine_ref[0:HALF] = feat_ref[...]
     pick = lax.broadcasted_iota(jnp.int32, (HUB_ROWS, 2 * HUB_ROWS), 1) == (
         2 * lax.broadcasted_iota(jnp.int32, (HUB_ROWS, 2 * HUB_ROWS), 0) + parity
     )
-    columns = hub_ref[:, pl.ds(pl.multiple_of(half * COLS, COLS), COLS)]
+    columns = hub_scr[:, pl.ds(pl.multiple_of(half * COLS, COLS), COLS)]
     mine_ref[HALF:BLOCK] = dot(pick.astype(F32).astype(BF), columns).astype(BF)
-    both_ref[0:HALF] = feat_ref[...]
-    both_ref[HALF:V] = cot_ref[...]
-
-
-def counts_kernel(place, ids0, ids1, ids2, ids3, out_ref):
-    y, z, c, x = place[0], place[1], place[2], place[3]
+    for copy in copies[5:]:
+        copy.wait()
+
+
+def counts_kernel(ids0, ids1, ids2, ids3, out_ref):
+    y, z, c, x = (lax.axis_index(a) for a in ("y", "z", "c", "x"))
     parity = x // 2
     rows = lax.broadcasted_iota(jnp.int32, (16, 16, 128), 0) * 16 + lax.broadcasted_iota(
         jnp.int32, (16, 16, 128), 1
@@ -152,9 +176,9 @@
         lax.fori_loop(0, NC, part, 0)
 
 
-def far_sums_kernel(place, counts, t0, t1, t7, t23, t65, t4, sums_ref, turned_ref, table):
-    blocks = {0: t0[...], 1: t1[...], 7: t7[...], 4: t4[...]}
-    blocks[2], blocks[3] = t23[0:BLOCK], t23[BLOCK : 2 * BLOCK]
+def far_sums_kernel(counts, t0, t1, t2, t7, t34, t65, sums_ref, turned_ref, table):
+    blocks = {0: t0[...], 1: t1[...], 2: t2[...], 7: t7[...]}
+    blocks[3], blocks[4] = t34[0:BLOCK], t34[BLOCK : 2 * BLOCK]
     blocks[6], blocks[5] = t65[0:BLOCK], t65[BLOCK : 2 * BLOCK]
     for delta in range(NZ):
         table[delta * HALF : (delta + 1) * HALF] = blocks[delta][0:HALF]
@@ -170,7 +194,7 @@
     lax.fori_loop(0, NY, step, 0)
 
 
-def near_sums_kernel(place, counts, turned, sums_ref):
+def near_sums_kernel(counts, turned, sums_ref):
     def step(dy, carry):
         sums_ref[dy] = dot(turned[...], counts[dy])
         return carry
@@ -178,24 +202,24 @@
     lax.fori_loop(0, NY, step, 0)
 
 
+def arrange_kernel(fg, ws_ref, feat_ref, cot_ref, pre_ref):
+    for start, ref in ((0, feat_ref), (HALF, cot_ref)):
+        quarters = [fg[q, start : start + HALF] for q in range(NX)]
+        ref[...] = jnp.concatenate(
+            [jnp.concatenate(quarters[0:2], 1), jnp.concatenate(quarters[2:4], 1)], 0
+        )
+    pre_ref[...] = dot(feat_ref[...], ws_ref[...])
+
+
 def dense_kernel(
-    place, fg0, fg1, fg23, s0, s1, s2, s3, ws_ref, wn_ref,
+    feat_ref, cot_ref, pre_ref, s0, s1, s2, s3, ws_ref, wn_ref,
     out_ref, message_ref, self_ref,
-    f_scr, g_scr, s_scr, o_scr, w_scr,
+    s_scr, o_scr, w_scr,
 ):
-    x = place[3]
+    x = lax.axis_index("x")
     parity, half = x // 2, x % 2
-    sources = ((fg0, 0), (fg1, 0), (fg23, 0), (fg23, V))
-    for mask, ((ref, start), sr) in enumerate(zip(sources, (s0, s1, s2, s3))):
-        f_scr[x ^ mask] = ref[start : start + HALF]
-        g_scr[x ^ mask] = ref[start + HALF : start + V]
-        s_scr[x ^ mask] = sr[...]
-    feats = jnp.concatenate(
-        [jnp.concatenate([f_scr[0], f_scr[1]], 1), jnp.concatenate([f_scr[2], f_scr[3]], 1)], 0
-    )
-    cot = jnp.concatenate(
-        [jnp.concatenate([g_scr[0], g_scr[1]], 1), jnp.concatenate([g_scr[2], g_scr[3]], 1)], 0
-    ).astype(F32)
+    for mask, ref in enumerate((s0, s1, s2, s3)):
+        s_scr[x ^ mask] = ref[...]
     mean_t = jnp.concatenate(
         [
             s_scr[0].astype(F32) + s_scr[2].astype(F32),
@@ -208,10 +232,10 @@
     natural = lax.broadcasted_iota(jnp.int32, (V, V), 1)
     order = ((ordered % HALF) * 2 + ordered // HALF == natural).astype(F32).astype(BF)
     mean = dot(order, mean_t, LAST).astype(BF)
-    pre = dot(feats, ws_ref[...]) + dot(mean, wn_ref[...])
+    pre = pre_ref[...] + dot(mean, wn_ref[...])
     sig = jax.nn.sigmoid(pre)
     value = (pre * sig).astype(BF)
-    grad_pre = (cot * sig * (1.0 + pre * (1.0 - sig))).astype(BF)
+    grad_pre = (cot_ref[...].astype(F32) * sig * (1.0 + pre * (1.0 - sig))).astype(BF)
     for q in range(2):
         for h in range(2):
             o_scr[q * 2 + h] = value[q * HALF : (q + 1) * HALF, h * COLS : (h + 1) * COLS]
@@ -221,7 +245,7 @@
     message_ref[0:V] = dot(order, grad_mean, FIRST).astype(BF)
     own_self = dot(grad_pre, ws_ref[rows, :], LAST)
     self_ref[...] = jnp.where(parity == 0, own_self[0:HALF], own_self[HALF:V])
-    w_scr[0] = dot(feats, grad_pre, FIRST)
+    w_scr[0] = dot(feat_ref[...], grad_pre, FIRST)
     w_scr[1] = dot(mean, grad_pre, FIRST)
     quarter = pl.ds(pl.multiple_of(x * 64, 64), 64)
     for which in range(2):
@@ -231,36 +255,30 @@
             message_ref[start : start + 64, :] = part[:, h * COLS : (h + 1) * COLS].astype(BF)
 
 
-def gather_kernel(place, m0, m1, m2, m3, out_ref):
-    for dy, ref in enumerate((m0, m1, m2, m3)):
-        out_ref[dy * V : (dy + 1) * V] = ref[0:V]
-    tail = slice(V, V + WROWS)
-    weight = (m0[tail].astype(F32) + m1[tail].astype(F32)) + (m2[tail].astype(F32) + m3[tail].astype(F32))
-    high = weight.astype(BF)
-    out_ref[NY * V : NY * V + WROWS] = high
-    out_ref[NY * V + WROWS :] = (weight - high.astype(F32)).astype(BF)
-
-
-def near_grads_kernel(place, counts, m0, m1, m2, m3, out_ref):
-    for block in range(NZ + 1):
-        span = slice(block * HALF, (block + 1) * HALF)
-        total = jnp.zeros((HALF, COLS), F32)
-        for dy, ref in enumerate((m0, m1, m2, m3)):
-            total = total + dot(counts[dy, span], ref[0:V])
-        out_ref[block] = total
-
-
-def far_block(counts, other, near, block):
+def block_sum(counts, base, messages, block, total=None):
     span = slice(block * HALF, (block + 1) * HALF)
-    total = near[block]
-    for dy in range(NY):
-        total = total + dot(counts[NY + dy, span], other[dy * V : (dy + 1) * V])
+    for dy, ref in enumerate(messages):
+        term = dot(counts[base + dy, span], ref[0:V])
+        total = term if total is None else total + term
     return total
 
 
-def first_grads_kernel(place, counts, own, other, near, up_ref, down_ref, hub_ref):
-    parity = place[3] // 2
-    hubs = far_block(counts, other, near, NZ)
+FIRST_BLOCKS = (4, 5, NZ)
+REST = (0, 1, 2, 3, 6, 7)
+
+
+def near_grads_kernel(counts, m0, m1, m2, m3, out_ref):
+    for index, block in enumerate(FIRST_BLOCKS):
+        out_ref[index] = block_sum(counts, 0, (m0, m1, m2, m3), block)
+
+
+def first_grads_kernel(
+    counts, m0, m1, m2, m3, o0, o1, o2, o3, near, up_ref, down_ref, hub_ref
+):
+    parity = lax.axis_index("x") // 2
+    others = (o0, o1, o2, o3)
+    blocks = [block_sum(counts, NY, others, block, near[index]) for index, block in enumerate(FIRST_BLOCKS)]
+    hubs = blocks[2]
     lane = lax.broadcasted_iota(jnp.int32, (HUB_ROWS, COLS), 1)
     low = (lane < 64) == (parity == 0)
     for delta in range(NZ):
@@ -268,33 +286,31 @@
         mine = hubs[start : start + HUB_ROWS]
         rest = pltpu.roll(hubs[start + HUB_ROWS : start + 2 * HUB_ROWS], 64, 1)
         hub_ref[delta] = jnp.where(low, mine, rest)
-    high, small = slice(NY * V, NY * V + WROWS), slice(NY * V + WROWS, NY * V + 2 * WROWS)
-    weight = (own[high].astype(F32) + own[small].astype(F32)) + (
-        other[high].astype(F32) + other[small].astype(F32)
-    )
-    weight = weight.astype(BF)
-    for delta, ref in ((4, up_ref), (5, down_ref)):
-        ref[0:HALF] = far_block(counts, other, near, delta).astype(BF)
-        ref[HALF:BLOCK] = hub_ref[delta].astype(BF)
+    tail = slice(V, V + WROWS)
+    sums = [
+        (a[tail].astype(F32) + b[tail].astype(F32)) + (c[tail].astype(F32) + d[tail].astype(F32))
+        for a, b, c, d in ((m0, m1, m2, m3), others)
+    ]
+    weight = (sums[0] + sums[1]).astype(BF)
+    for index, ref in enumerate((up_ref, down_ref)):
+        ref[0:HALF] = blocks[index].astype(BF)
+        ref[HALF:BLOCK] = hub_ref[FIRST_BLOCKS[index]].astype(BF)
         ref[BLOCK:] = weight
 
 
-REST = (0, 1, 2, 3, 6, 7)
-
-
-def rest_grads_kernel(place, counts, other, near, out_ref):
-    for index, delta in enumerate(REST):
-        out_ref[index] = far_block(counts, other, near, delta)
-
-
-def hop_kernel(place, up, down, rest, hubs, next_up, next_down, *, deltas):
+def rest_grads_kernel(counts, m0, m1, m2, m3, o0, o1, o2, o3, out_ref):
+    for index, block in enumerate(REST):
+        out_ref[index] = block_sum(counts, 0, (m0, m1, m2, m3, o0, o1, o2, o3), block)
+
+
+def hop_kernel(up, down, rest, hubs, next_up, next_down, *, deltas):
     for delta, got, ref in zip(deltas, (up, down), (next_up, next_down)):
         ref[0:HALF] = (got[0:HALF].astype(F32) + rest[REST.index(delta)]).astype(BF)
         ref[HALF:BLOCK] = (got[HALF:BLOCK].astype(F32) + hubs[delta]).astype(BF)
         ref[BLOCK:] = got[BLOCK:]
 
 
-def last_hop_kernel(place, up, down, rest, hubs, next_up, hub_up, hub_here):
+def last_hop_kernel(up, down, rest, hubs, next_up, hub_up, hub_here):
     next_up[0:HALF] = (up[0:HALF].astype(F32) + rest[REST.index(1)]).astype(BF)
     next_up[HALF:] = up[BLOCK:]
     hub_up[...] = up[HALF:BLOCK].astype(F32) + hubs[1]
@@ -302,10 +318,10 @@
 
 
 def final_kernel(
-    place, self_ref, rest, first, up1, up2, up3, up4, down1, down2, down3, hub_up, hub_here,
+    self_ref, rest, first, up1, up2, up3, up4, down1, down2, down3, hub_up, hub_here,
     feat_ref, hub_ref, gself_ref, gnbr_ref, w_scr,
 ):
-    z = place[1]
+    z = lax.axis_index("z")
     total = rest[0] + up4[0:HALF].astype(F32) + down3[0:HALF].astype(F32)
     feat_ref[...] = (self_ref[...] + total).astype(BF)
     hubs = hub_up[...] + hub_here[...]
@@ -331,26 +347,34 @@
 
 
 def body(features, hub_feats, nbr_owner, nbr_row, hub_ids, w_self, w_nbr, grad_out):
-    place = jnp.stack([lax.axis_index(a) for a in ("y", "z", "c", "x")]).astype(jnp.int32)
     ids, mine, fg = call(
         prepare_kernel,
-        (shaped((16, V), jnp.int32), shaped((BLOCK, COLS), BF), shaped((V, COLS), BF)),
-        (place, features, grad_out, hub_feats, nbr_owner.reshape(8, V), nbr_row, hub_ids.T),
+        (pltpu.VMEM((16, V), jnp.int32), pltpu.VMEM((BLOCK, COLS), BF), shaped((2 * V, COLS), BF)),
+        (features, grad_out, hub_feats, nbr_owner.reshape(8, 1, V), nbr_row, hub_ids.T),
         "prepare",
-    )
-
-    t1, t7 = shift(mine, "z", NZ, -1), shift(mine, "z", NZ, 1)
+        scratch=[
+            pltpu.VMEM((8, 1, V), jnp.int32),
+            pltpu.VMEM((8, V), jnp.int32),
+            pltpu.VMEM((4, V), jnp.int32),
+            pltpu.VMEM((2 * HUB_ROWS, 256), BF),
+            pltpu.SemaphoreType.DMA((9,)),
+        ],
+        far=6,
+        far_outs=1,
+        mib=56,
+    )
+
+    everything = lax.all_gather(fg, "x", axis=0)
+
     pair = jnp.stack([ids, swap(ids, "c", NC, 1)])
-    fg1 = swap(fg, "x", NX, 1)
+    t1, t7, t2 = shift(mine, "z", NZ, -1), shift(mine, "z", NZ, 1), shift(mine, "z", NZ, -2)
     pairs = [pair] + [swap(pair, "y", NY, m) for m in range(1, NY)]
-    t23 = shift(jnp.concatenate([mine, t1], 0), "z", NZ, -2)
+    t34 = shift(jnp.concatenate([t1, t2], 0), "z", NZ, -2)
     t65 = shift(jnp.concatenate([mine, t7], 0), "z", NZ, 2)
-    t4 = shift(t1, "z", NZ, -3)
-    fg23 = swap(jnp.concatenate([fg, fg1], 0), "x", NX, 2)
     counts = call(
         counts_kernel,
         pltpu.VMEM((PARTS, ROWS, V), BF),
-        (place, *pairs),
+        (*pairs,),
         "counts",
         flops=1 << 34,
         mib=8,
@@ -359,14 +383,14 @@
     far, turned = call(
         far_sums_kernel,
         (shaped((NY, COLS, V), BF), shaped((COLS, ROWS), BF)),
-        (place, counts, mine, t1, t7, t23, t65, t4),
+        (counts, mine, t1, t2, t7, t34, t65),
         "far_sums",
         scratch=[pltpu.VMEM((ROWS, COLS), BF)],
         flops=1 << 31,
     )
     got = swap(far, "c", NC, 1)
     near = call(
-        near_sums_kernel, shaped((NY, COLS, V), F32), (place, counts, turned), "near_sums", flops=1 << 31
+        near_sums_kernel, shaped((NY, COLS, V), F32), (counts, turned), "near_sums", flops=1 << 31
     )
     both = near + got.astype(F32)
     total = both[0]
@@ -375,14 +399,19 @@
     total = total.astype(BF)
     sums = [total] + [swap(total, "x", NX, m) for m in range(1, NX)]
 
+    feats, cots, base = call(
+        arrange_kernel,
+        (shaped((V, 256), BF), shaped((V, 256), BF), shaped((V, 256), F32)),
+        (everything, w_self),
+        "arrange",
+        flops=1 << 28,
+    )
     outputs, message, self_term = call(
         dense_kernel,
         (shaped((HALF, COLS), BF), shaped((V + WROWS, COLS), BF), shaped((HALF, COLS), F32)),
-        (place, fg, fg1, fg23, *sums, w_self, w_nbr),
+        (feats, cots, base, *sums, w_self, w_nbr),
         "dense",
         scratch=[
-            pltpu.VMEM((4, HALF, COLS), BF),
-            pltpu.VMEM((4, HALF, COLS), BF),
             pltpu.VMEM((4, COLS, V), BF),
             pltpu.VMEM((4, HALF, COLS), BF),
             pltpu.VMEM((2, 256, 256), F32),
@@ -391,43 +420,36 @@
     )
 
     messages = [message] + [swap(message, "y", NY, m) for m in range(1, NY)]
-    own = call(
-        gather_kernel, shaped((NY * V + 2 * WROWS, COLS), BF), (place, *messages), "gather_grads"
-    )
-    other = swap(own, "c", NC, 1)
+    others = [swap(m, "c", NC, 1) for m in messages]
     near_grads = call(
         near_grads_kernel,
-        shaped((NZ + 1, HALF, COLS), F32),
-        (place, counts, *messages),
+        shaped((len(FIRST_BLOCKS), HALF, COLS), F32),
+        (counts, *messages),
         "near_grads",
-        flops=1 << 31,
-    )
+        flops=1 << 30,
+    )
+    hop_shapes = (shaped((BLOCK + WROWS, COLS), BF),) * 2
     up0, down0, hubs = call(
         first_grads_kernel,
-        (
-            shaped((BLOCK + WROWS, COLS), BF),
-            shaped((BLOCK + WROWS, COLS), BF),
-            shaped((NZ, HUB_ROWS, COLS), F32),
-        ),
-        (place, counts, own, other, near_grads),
+        (*hop_shapes, shaped((NZ, HUB_ROWS, COLS), F32)),
+        (counts, *messages, *others, near_grads),
         "first_grads",
-        flops=1 << 29,
+        flops=1 << 30,
     )
     up1, down1 = shift(up0, "z", NZ, 1), shift(down0, "z", NZ, -1)
     rest = call(
         rest_grads_kernel,
         shaped((len(REST), HALF, COLS), F32),
-        (place, counts, other, near_grads),
+        (counts, *messages, *others),
         "rest_grads",
-        flops=1 << 30,
-    )
-    hop_shapes = (shaped((BLOCK + WROWS, COLS), BF),) * 2
+        flops=1 << 31,
+    )
     ups, downs = [up1], [down1]
     for deltas in ((3, 6), (2, 7)):
         up, down = call(
             functools.partial(hop_kernel, deltas=deltas),
             hop_shapes,
-            (place, ups[-1], downs[-1], rest, hubs),
+            (ups[-1], downs[-1], rest, hubs),
             "hop",
         )
         ups.append(shift(up, "z", NZ, 1))
@@ -439,7 +461,7 @@
             shaped((HUB_ROWS, COLS), F32),
             shaped((HUB_ROWS, COLS), F32),
         ),
-        (place, ups[-1], downs[-1], rest, hubs),
+        (ups[-1], downs[-1], rest, hubs),
         "last_hop",
     )
     ups.append(shift(up, "z", NZ, 1))
@@ -455,7 +477,7 @@
             shaped((64, 256), F32),
             shaped((64, 256), F32),
         ),
-        (place, self_term, rest, up0, *ups, *downs, hub_up, hub_here),
+        (self_term, rest, up0, *ups, *downs, hub_up, hub_here),
         "last_sums",
         scratch=[pltpu.VMEM((NZ, WROWS, COLS), BF)],
     )

time: 113 us -> 131 us (1.16)
  between operations: 0.88 us -> 14.3 us
  local copies, waits for them, and re-layouts: 4.57 us -> 9.89 us
  Pallas kernels: 27.5 us -> 29.8 us
  starting transfers between devices: 47.8 us -> 45.6 us
    unnamed x15 -> x10, local copies, waits for them, and re-layouts: 4.54 us -> 9.87 us
    ppermute x12, waiting for transfers between devices: 10.5 us -> 7.14 us  [shift(): return lax.ppermute(x, axis, [(i, (i + step) % size) for i in range(size)])]
    pallas_call x13, Pallas kernels: 27.5 us -> 29.8 us  [call(): pl.pallas_call(kernel, out_shape=outs, in_specs=[VM] * (len(inputs) - far...]
    ppermute x1, starting transfers between devices: 3.73 us -> 1.91 us  [body(): hub_here = lax.ppermute(hub_here, 'x', [(x, turn[x]) for x in range(NX)])]
    ppermute x17 -> x18, starting transfers between devices: 19.9 us -> 18.1 us  [swap(): return lax.ppermute(x, axis, [(i, i ^ mask) for i in range(size)])]
    ppermute x17 -> x18, waiting for transfers between devices: 18.8 us -> 20.6 us  [swap(): return lax.ppermute(x, axis, [(i, i ^ mask) for i in range(size)])]
    ppermute x1, waiting for transfers between devices: 0.74 us -> 2.16 us  [body(): hub_here = lax.ppermute(hub_here, 'x', [(x, turn[x]) for x in range(NX)])]
  transfers between devices with their start and end apart: 31 -> 33, of which waited for: 13 -> 15; matrix products, arithmetic and copies ran while one was open for 0% -> 0% of each run, Pallas kernels for 15% -> 13%
where the time goes in v4:
time: 131 us
  starting transfers between devices  45.6 us (35%)
  waiting for transfers between devices  31.3 us (24%)
  Pallas kernels  29.8 us (23%)
  between operations  14.3 us (11%)
  local copies, waits for them, and re-layouts  9.89 us (8%)
    pallas_call x13, Pallas kernels, call(): pl.pallas_call(kernel, out_shape=outs, in_specs=[VM] * (len(inputs) - far...  29.8 us
    ppermute x12, starting transfers between devices, shift(): return lax.ppermute(x, axis, [(i, (i + step) % size) for i in range(size)])  23 us
    ppermute x18, waiting for transfers between devices, swap(): return lax.ppermute(x, axis, [(i, i ^ mask) for i in range(size)])  20.6 us
    ppermute x18, starting transfers between devices, swap(): return lax.ppermute(x, axis, [(i, i ^ mask) for i in range(size)])  18.1 us
    unnamed x10, local copies, waits for them, and re-layouts  9.87 us
    ppermute x12, waiting for transfers between devices, shift(): return lax.ppermute(x, axis, [(i, (i + step) % size) for i in range(size)])  7.14 us
  transfers between devices with their start and end apart: 33, of which 15 were waited for; matrix products, arithmetic and copies ran while one was open for 0% of the time, Pallas kernels for 13%

profile of v4, /device:TPU:4, one launch (start us, length us, event | category | flops | bytes accessed | tf_op | source)
XLA Modules:
  0.0 131.2 jit_solution(815732119814076399)
XLA Ops:
  7.2 9.1 %prepare.1 = (s32[16,512]{1,0:T(8,128)S(1)}, bf16[272,128]{1,0:T(8,128)(2,1)S(1)}, bf16[1024,128]{1,0:T(8,128)(2,1)}) custom-call(bf16[256,128]{1,0:T(8,128)(2,1)} %feat.1, bf16[256,128]{1,0:T(8,128)(2,1)} %cot.1, bf16[32,256]{1,0:T(8,128)(2,1)} %hub.1, s32[8,1,512]{2,1,0:T(1,128)} %bitcast.24, s32[8,512]{1,0:T(8,128)} %row.1, s32[4,512]{1,0:T(4,128)} %bitcast.25), custom_call_target="tpu_custom_call" | custom-call | bytes 262144 | tf_op jit(solution)/shard_map/prepare/pallas_call | solution.py:44
  16.4 5.9 %collective-permute-start.4 = (bf16[272,128]{1,0:T(8,128)(2,1)S(1)}, bf16[272,128]{1,0:T(8,128)(2,1)S(1)}, u32[]{:S(2)}, u32[]{:S(2)}) collective-permute-start(bf16[272,128]{1,0:T(8,128)(2,1)S(1)} %get-tuple-element.35.t0), channel_id=1, source_target_pairs={{0,56},{8,0},{16,8},{24,16},{32,24},{40,32},{48,40},{56,48},{1,57}... | collective-permute-start | bytes 208904 | tf_op jit(solution)/shard_map/ppermute | solution.py:33
  26.6 2.9 %collective-permute-start.2 = (s32[2,16,512]{2,1,0:T(8,128)S(1)}, s32[2,16,512]{2,1,0:T(8,128)S(1)}, u32[]{:S(2)}, u32[]{:S(2)}) collective-permute-start(s32[2,16,512]{2,1,0:T(8,128)S(1)} %pad_add_fusion.ids0), channel_id=1, source_target_pairs={{0,128},{64,192},{128,0},{192,64},{1,129},{65,193},{129,1},{193,65... | collective-permute-start | bytes 196616 | tf_op jit(solution)/shard_map/ppermute | solution.py:37
  33.0 2.0 %collective-permute-done.3.ids3 = s32[2,16,512]{2,1,0:T(8,128)S(1)} collective-permute-done((s32[2,16,512]{2,1,0:T(8,128)S(1)}, s32[2,16,512]{2,1,0:T(8,128)S(1)}, u32[]{:S(2)}, u32[]{:S(2)}) %collective-permute-start.3) | collective-permute-done | bytes 65568 | tf_op jit(solution)/shard_map/ppermute | solution.py:37
  34.9 8.3 %counts.1 = bf16[8,2304,512]{2,1,0:T(8,128)(2,1)S(1)} custom-call(s32[2,16,512]{2,1,0:T(8,128)S(1)} %pad_add_fusion.ids0, s32[2,16,512]{2,1,0:T(8,128)S(1)} %collective-permute-done.1.ids1, s32[2,16,512]{2,1,0:T(8,128)S(1)} %collective-permute-done.2.ids2, s32[2,16,512]{2,1,0:T(8,128)S(1)} %collective-permute-done.3.ids3), custom_call_target="tpu_custom_call" | custom-call | flops 17179869184 | bytes 262144 | tf_op jit(solution)/shard_map/counts/pallas_call | solution.py:44
  43.3 2.1 %far_sums.1 = (bf16[4,128,512]{2,1,0:T(8,128)(2,1)S(1)}, bf16[128,2304]{1,0:T(8,128)(2,1)S(1)}) custom-call(bf16[8,2304,512]{2,1,0:T(8,128)(2,1)S(1)} %counts.1, bf16[272,128]{1,0:T(8,128)(2,1)S(1)} %get-tuple-element.35.t0, bf16[272,128]{1,0:T(8,128)(2,1)S(1)} %collective-permute-done.4.t1, bf16[272,128]{1,0:T(8,128)(2,1)S(1)} %collective-permute-done.5.t2, ...), custom_call_target="tpu_custom_call" | custom-call | flops 2147483648 | bytes 262144 | tf_op jit(solution)/shard_map/far_sums/pallas_call | solution.py:44
  45.6 1.9 %near_sums.1 = f32[4,128,512]{2,1,0:T(8,128)S(1)} custom-call(bf16[8,2304,512]{2,1,0:T(8,128)(2,1)S(1)} %counts.1, bf16[128,2304]{1,0:T(8,128)(2,1)S(1)} %get-tuple-element.36.turned), custom_call_target="tpu_custom_call" | custom-call | flops 2147483648 | bytes 262144 | tf_op jit(solution)/shard_map/near_sums/pallas_call | solution.py:44
  47.5 2.3 %copy-done = bf16[8,2304,512]{2,1,0:T(8,128)(2,1)} copy-done((bf16[8,2304,512]{2,1,0:T(8,128)(2,1)}, bf16[8,2304,512]{2,1,0:T(8,128)(2,1)S(1)}, u32[]{:S(2)}) %copy-start) | copy-done | bytes 18874392
  50.5 2.1 %collective-permute-start.11 = (bf16[128,512]{1,0:T(8,128)(2,1)S(1)}, bf16[128,512]{1,0:T(8,128)(2,1)S(1)}, u32[]{:S(2)}, u32[]{:S(2)}) collective-permute-start(bf16[128,512]{1,0:T(8,128)(2,1)S(1)} %get-tuple-element.59), channel_id=1, source_target_pairs={{0,128},{64,192},{128,0},{192,64},{1,129},{65,193},{129,1},{193,65... | collective-permute-start | bytes 393224 | tf_op jit(solution)/shard_map/ppermute | solution.py:37
  52.6 2.2 %collective-permute-start.12 = (bf16[128,512]{1,0:T(8,128)(2,1)S(1)}, bf16[128,512]{1,0:T(8,128)(2,1)S(1)}, u32[]{:S(2)}, u32[]{:S(2)}) collective-permute-start(bf16[128,512]{1,0:T(8,128)(2,1)S(1)} %get-tuple-element.58), channel_id=1, source_target_pairs={{0,192},{64,128},{128,64},{192,0},{1,193},{65,129},{129,65},{193,1... | collective-permute-start | bytes 393224 | tf_op jit(solution)/shard_map/ppermute | solution.py:37
  64.9 2.1 %collective-permute-done.14.s2 = bf16[128,512]{1,0:T(8,128)(2,1)S(1)} collective-permute-done((bf16[128,512]{1,0:T(8,128)(2,1)S(1)}, bf16[128,512]{1,0:T(8,128)(2,1)S(1)}, u32[]{:S(2)}, u32[]{:S(2)}) %collective-permute-start.14) | collective-permute-done | bytes 131104 | tf_op jit(solution)/shard_map/ppermute | solution.py:37
  69.9 4.6 %collective-permute-start.17 = (bf16[768,128]{1,0:T(8,128)(2,1)S(1)}, bf16[768,128]{1,0:T(8,128)(2,1)S(1)}, u32[]{:S(2)}, u32[]{:S(2)}) collective-permute-start(bf16[768,128]{1,0:T(8,128)(2,1)S(1)} %get-tuple-element.40.m0), channel_id=1, source_target_pairs={{0,128},{64,192},{128,0},{192,64},{1,129},{65,193},{129,1},{193,65... | collective-permute-start | bytes 589832 | tf_op jit(solution)/shard_map/ppermute | solution.py:37
  74.6 3.0 %collective-permute-done.16.m1 = bf16[768,128]{1,0:T(8,128)(2,1)S(1)} collective-permute-done((bf16[768,128]{1,0:T(8,128)(2,1)S(1)}, bf16[768,128]{1,0:T(8,128)(2,1)S(1)}, u32[]{:S(2)}, u32[]{:S(2)}) %collective-permute-start.16) | collective-permute-done | bytes 196640 | tf_op jit(solution)/shard_map/ppermute | solution.py:37
  77.6 4.9 %collective-permute-done.17.m2 = bf16[768,128]{1,0:T(8,128)(2,1)S(1)} collective-permute-done((bf16[768,128]{1,0:T(8,128)(2,1)S(1)}, bf16[768,128]{1,0:T(8,128)(2,1)S(1)}, u32[]{:S(2)}, u32[]{:S(2)}) %collective-permute-start.17) | collective-permute-done | bytes 196640 | tf_op jit(solution)/shard_map/ppermute | solution.py:37
  82.6 2.3 %collective-permute-done.18.m3 = bf16[768,128]{1,0:T(8,128)(2,1)S(1)} collective-permute-done((bf16[768,128]{1,0:T(8,128)(2,1)S(1)}, bf16[768,128]{1,0:T(8,128)(2,1)S(1)}, u32[]{:S(2)}, u32[]{:S(2)}) %collective-permute-start.18) | collective-permute-done | bytes 196640 | tf_op jit(solution)/shard_map/ppermute | solution.py:37
  84.9 6.4 %copy-done.1 = bf16[8,2304,512]{2,1,0:T(8,128)(2,1)S(1)} copy-done((bf16[8,2304,512]{2,1,0:T(8,128)(2,1)S(1)}, bf16[8,2304,512]{2,1,0:T(8,128)(2,1)}, u32[]{:S(2)}) %copy-start.1) | copy-done | bytes 18874392
  94.4 3.3 %collective-permute-start.24 = (bf16[528,128]{1,0:T(8,128)(2,1)S(1)}, bf16[528,128]{1,0:T(8,128)(2,1)S(1)}, u32[]{:S(2)}, u32[]{:S(2)}) collective-permute-start(bf16[528,128]{1,0:T(8,128)(2,1)S(1)} %get-tuple-element.42), channel_id=1, source_target_pairs={{0,56},{8,0},{16,8},{24,16},{32,24},{40,32},{48,40},{56,48},{1,57}... | collective-permute-start | bytes 405512 | tf_op jit(solution)/shard_map/ppermute | solution.py:33
  97.7 3.4 %rest_grads.1.rest = f32[6,256,128]{2,1,0:T(8,128)S(1)} custom-call(bf16[8,2304,512]{2,1,0:T(8,128)(2,1)S(1)} %copy-done.1, bf16[768,128]{1,0:T(8,128)(2,1)S(1)} %get-tuple-element.40.m0, bf16[768,128]{1,0:T(8,128)(2,1)S(1)} %collective-permute-done.16.m1, bf16[768,128]{1,0:T(8,128)(2,1)S(1)} %collective-permute-done.17.m2, ...), custom_call_target="tpu_custom_call" | custom-call | flops 2147483648 | bytes 262144 | tf_op jit(solution)/shard_map/rest_grads/pallas_call | solution.py:44
  102.0 3.2 %collective-permute-start.26 = (bf16[528,128]{1,0:T(8,128)(2,1)S(1)}, bf16[528,128]{1,0:T(8,128)(2,1)S(1)}, u32[]{:S(2)}, u32[]{:S(2)}) collective-permute-start(bf16[528,128]{1,0:T(8,128)(2,1)S(1)} %get-tuple-element.45), channel_id=1, source_target_pairs={{0,56},{8,0},{16,8},{24,16},{32,24},{40,32},{48,40},{56,48},{1,57}... | collective-permute-start | bytes 405512 | tf_op jit(solution)/shard_map/ppermute | solution.py:33
  105.2 3.4 %collective-permute-done.25.up.up2 = bf16[528,128]{1,0:T(8,128)(2,1)S(1)} collective-permute-done((bf16[528,128]{1,0:T(8,128)(2,1)S(1)}, bf16[528,128]{1,0:T(8,128)(2,1)S(1)}, u32[]{:S(2)}, u32[]{:S(2)}) %collective-permute-start.25) | collective-permute-done | bytes 135200 | tf_op jit(solution)/shard_map/ppermute | solution.py:33
  109.0 3.2 %collective-permute-start.28 = (bf16[528,128]{1,0:T(8,128)(2,1)S(1)}, bf16[528,128]{1,0:T(8,128)(2,1)S(1)}, u32[]{:S(2)}, u32[]{:S(2)}) collective-permute-start(bf16[528,128]{1,0:T(8,128)(2,1)S(1)} %get-tuple-element.47), channel_id=1, source_target_pairs={{0,56},{8,0},{16,8},{24,16},{32,24},{40,32},{48,40},{56,48},{1,57}... | collective-permute-start | bytes 405512 | tf_op jit(solution)/shard_map/ppermute | solution.py:33
  112.2 3.0 %collective-permute-done.27.up.up3 = bf16[528,128]{1,0:T(8,128)(2,1)S(1)} collective-permute-done((bf16[528,128]{1,0:T(8,128)(2,1)S(1)}, bf16[528,128]{1,0:T(8,128)(2,1)S(1)}, u32[]{:S(2)}, u32[]{:S(2)}) %collective-permute-start.27) | collective-permute-done | bytes 135200 | tf_op jit(solution)/shard_map/ppermute | solution.py:33
  115.3 2.6 %collective-permute-start.30 = (f32[16,128]{1,0:T(8,128)S(1)}, f32[16,128]{1,0:T(8,128)S(1)}, u32[]{:S(2)}, u32[]{:S(2)}) collective-permute-start(f32[16,128]{1,0:T(8,128)S(1)} %get-tuple-element.49), channel_id=1, source_target_pairs={{0,8},{1,10},{2,9},{3,11},{8,16},{9,18},{10,17},{11,19},{16,24},{1... | collective-permute-start | bytes 24584 | tf_op jit(solution)/shard_map/ppermute | solution.py:470
  121.3 2.2 %collective-permute-done.31.hub_here = f32[16,128]{1,0:T(8,128)S(1)} collective-permute-done((f32[16,128]{1,0:T(8,128)S(1)}, f32[16,128]{1,0:T(8,128)S(1)}, u32[]{:S(2)}, u32[]{:S(2)}) %collective-permute-start.31) | collective-permute-done | bytes 8224 | tf_op jit(solution)/shard_map/ppermute | solution.py:471
  (72 shorter events, 30.6 us)
Async XLA Ops:
  7.2 55.3 %all-gather.3.cloned.1.call-start = ((), (), s32[]{:S(2)}) async-start(), calls=%async_computation | async-start | bytes 1310720 | tf_op jit(solution)/shard_map/all_gather | solution.py:367
  16.3 8.5 %collective-permute-start = (s32[16,512]{1,0:T(8,128)S(1)}, s32[16,512]{1,0:T(8,128)S(1)}, u32[]{:S(2)}, u32[]{:S(2)}) collective-permute-start(s32[16,512]{1,0:T(8,128)S(1)} %get-tuple-element.34), channel_id=1, source_target_pairs={{0,4},{4,0},{1,5},{5,1},{2,6},{6,2},{3,7},{7,3},{8,12},{12,8},{9,1... | collective-permute-start | bytes 98312 | tf_op jit(solution)/shard_map/ppermute | solution.py:37
  16.4 13.0 %collective-permute-start.4 = (bf16[272,128]{1,0:T(8,128)(2,1)S(1)}, bf16[272,128]{1,0:T(8,128)(2,1)S(1)}, u32[]{:S(2)}, u32[]{:S(2)}) collective-permute-start(bf16[272,128]{1,0:T(8,128)(2,1)S(1)} %get-tuple-element.35.t0), channel_id=1, source_target_pairs={{0,56},{8,0},{16,8},{24,16},{32,24},{40,32},{48,40},{56,48},{1,57}... | collective-permute-start | bytes 208904 | tf_op jit(solution)/shard_map/ppermute | solution.py:33
  22.4 7.3 %collective-permute-start.5 = (bf16[272,128]{1,0:T(8,128)(2,1)S(1)}, bf16[272,128]{1,0:T(8,128)(2,1)S(1)}, u32[]{:S(2)}, u32[]{:S(2)}) collective-permute-start(bf16[272,128]{1,0:T(8,128)(2,1)S(1)} %get-tuple-element.35.t0), channel_id=1, source_target_pairs={{0,48},{8,56},{16,0},{24,8},{32,16},{40,24},{48,32},{56,40},{1,49}... | collective-permute-start | bytes 208904 | tf_op jit(solution)/shard_map/ppermute | solution.py:33
  23.8 7.4 %collective-permute-start.6 = (bf16[272,128]{1,0:T(8,128)(2,1)S(1)}, bf16[272,128]{1,0:T(8,128)(2,1)S(1)}, u32[]{:S(2)}, u32[]{:S(2)}) collective-permute-start(bf16[272,128]{1,0:T(8,128)(2,1)S(1)} %get-tuple-element.35.t0), channel_id=1, source_target_pairs={{0,8},{8,16},{16,24},{24,32},{32,40},{40,48},{48,56},{56,0},{1,9},... | collective-permute-start | bytes 208904 | tf_op jit(solution)/shard_map/ppermute | solution.py:33
  24.9 8.1 %collective-permute-start.1 = (s32[2,16,512]{2,1,0:T(8,128)S(1)}, s32[2,16,512]{2,1,0:T(8,128)S(1)}, u32[]{:S(2)}, u32[]{:S(2)}) collective-permute-start(s32[2,16,512]{2,1,0:T(8,128)S(1)} %pad_add_fusion.ids0), channel_id=1, source_target_pairs={{0,64},{64,0},{128,192},{192,128},{1,65},{65,1},{129,193},{193,129... | collective-permute-start | bytes 196616 | tf_op jit(solution)/shard_map/ppermute | solution.py:37
  26.6 6.4 %collective-permute-start.2 = (s32[2,16,512]{2,1,0:T(8,128)S(1)}, s32[2,16,512]{2,1,0:T(8,128)S(1)}, u32[]{:S(2)}, u32[]{:S(2)}) collective-permute-start(s32[2,16,512]{2,1,0:T(8,128)S(1)} %pad_add_fusion.ids0), channel_id=1, source_target_pairs={{0,128},{64,192},{128,0},{192,64},{1,129},{65,193},{129,1},{193,65... | collective-permute-start | bytes 196616 | tf_op jit(solution)/shard_map/ppermute | solution.py:37
  29.7 13.6 %collective-permute-start.7 = (bf16[544,128]{1,0:T(8,128)(2,1)S(1)}, bf16[544,128]{1,0:T(8,128)(2,1)S(1)}, u32[]{:S(2)}, u32[]{:S(2)}) collective-permute-start(bf16[544,128]{1,0:T(8,128)(2,1)S(1)} %pad_maximum_fusion), channel_id=1, source_target_pairs={{0,48},{8,56},{16,0},{24,8},{32,16},{40,24},{48,32},{56,40},{1,49}... | collective-permute-start | bytes 417800 | tf_op jit(solution)/shard_map/ppermute | solution.py:33
  31.3 12.1 %collective-permute-start.8 = (bf16[544,128]{1,0:T(8,128)(2,1)S(1)}, bf16[544,128]{1,0:T(8,128)(2,1)S(1)}, u32[]{:S(2)}, u32[]{:S(2)}) collective-permute-start(bf16[544,128]{1,0:T(8,128)(2,1)S(1)} %pad_maximum_fusion.1), channel_id=1, source_target_pairs={{0,16},{8,24},{16,32},{24,40},{32,48},{40,56},{48,0},{56,8},{1,17}... | collective-permute-start | bytes 417800 | tf_op jit(solution)/shard_map/ppermute | solution.py:33
  50.5 6.5 %collective-permute-start.11 = (bf16[128,512]{1,0:T(8,128)(2,1)S(1)}, bf16[128,512]{1,0:T(8,128)(2,1)S(1)}, u32[]{:S(2)}, u32[]{:S(2)}) collective-permute-start(bf16[128,512]{1,0:T(8,128)(2,1)S(1)} %get-tuple-element.59), channel_id=1, source_target_pairs={{0,128},{64,192},{128,0},{192,64},{1,129},{65,193},{129,1},{193,65... | collective-permute-start | bytes 393224 | tf_op jit(solution)/shard_map/ppermute | solution.py:37
  60.2 6.8 %collective-permute-start.14 = (bf16[128,512]{1,0:T(8,128)(2,1)S(1)}, bf16[128,512]{1,0:T(8,128)(2,1)S(1)}, u32[]{:S(2)}, u32[]{:S(2)}) collective-permute-start(bf16[128,512]{1,0:T(8,128)(2,1)S(1)} %fusion.3.s0), channel_id=1, source_target_pairs={{0,2},{1,3},{2,0},{3,1},{4,6},{5,7},{6,4},{7,5},{8,10},{9,11},{10,... | collective-permute-start | bytes 393224 | tf_op jit(solution)/shard_map/ppermute | solution.py:37
  69.9 7.8 %collective-permute-start.16 = (bf16[768,128]{1,0:T(8,128)(2,1)S(1)}, bf16[768,128]{1,0:T(8,128)(2,1)S(1)}, u32[]{:S(2)}, u32[]{:S(2)}) collective-permute-start(bf16[768,128]{1,0:T(8,128)(2,1)S(1)} %get-tuple-element.40.m0), channel_id=1, source_target_pairs={{0,64},{64,0},{128,192},{192,128},{1,65},{65,1},{129,193},{193,129... | collective-permute-start | bytes 589832 | tf_op jit(solution)/shard_map/ppermute | solution.py:37
  69.9 12.6 %collective-permute-start.17 = (bf16[768,128]{1,0:T(8,128)(2,1)S(1)}, bf16[768,128]{1,0:T(8,128)(2,1)S(1)}, u32[]{:S(2)}, u32[]{:S(2)}) collective-permute-start(bf16[768,128]{1,0:T(8,128)(2,1)S(1)} %get-tuple-element.40.m0), channel_id=1, source_target_pairs={{0,128},{64,192},{128,0},{192,64},{1,129},{65,193},{129,1},{193,65... | collective-permute-start | bytes 589832 | tf_op jit(solution)/shard_map/ppermute | solution.py:37
  74.5 10.4 %collective-permute-start.18 = (bf16[768,128]{1,0:T(8,128)(2,1)S(1)}, bf16[768,128]{1,0:T(8,128)(2,1)S(1)}, u32[]{:S(2)}, u32[]{:S(2)}) collective-permute-start(bf16[768,128]{1,0:T(8,128)(2,1)S(1)} %get-tuple-element.40.m0), channel_id=1, source_target_pairs={{0,192},{64,128},{128,64},{192,0},{1,193},{65,129},{129,65},{193,1... | collective-permute-start | bytes 589832 | tf_op jit(solution)/shard_map/ppermute | solution.py:37
  74.6 17.6 %collective-permute-start.19 = (bf16[768,128]{1,0:T(8,128)(2,1)S(1)}, bf16[768,128]{1,0:T(8,128)(2,1)S(1)}, u32[]{:S(2)}, u32[]{:S(2)}) collective-permute-start(bf16[768,128]{1,0:T(8,128)(2,1)S(1)} %get-tuple-element.40.m0), channel_id=1, source_target_pairs={{0,4},{4,0},{1,5},{5,1},{2,6},{6,2},{3,7},{7,3},{8,12},{12,8},{9,1... | collective-permute-start | bytes 589832 | tf_op jit(solution)/shard_map/ppermute | solution.py:37
  77.6 14.6 %collective-permute-start.20 = (bf16[768,128]{1,0:T(8,128)(2,1)S(1)}, bf16[768,128]{1,0:T(8,128)(2,1)S(1)}, u32[]{:S(2)}, u32[]{:S(2)}) collective-permute-start(bf16[768,128]{1,0:T(8,128)(2,1)S(1)} %collective-permute-done.16.m1), channel_id=1, source_target_pairs={{0,4},{4,0},{1,5},{5,1},{2,6},{6,2},{3,7},{7,3},{8,12},{12,8},{9,1... | collective-permute-start | bytes 589832 | tf_op jit(solution)/shard_map/ppermute | solution.py:37
  82.6 9.7 %collective-permute-start.21 = (bf16[768,128]{1,0:T(8,128)(2,1)S(1)}, bf16[768,128]{1,0:T(8,128)(2,1)S(1)}, u32[]{:S(2)}, u32[]{:S(2)}) collective-permute-start(bf16[768,128]{1,0:T(8,128)(2,1)S(1)} %collective-permute-done.17.m2), channel_id=1, source_target_pairs={{0,4},{4,0},{1,5},{5,1},{2,6},{6,2},{3,7},{7,3},{8,12},{12,8},{9,1... | collective-permute-start | bytes 589832 | tf_op jit(solution)/shard_map/ppermute | solution.py:37
  84.9 7.4 %collective-permute-start.22 = (bf16[768,128]{1,0:T(8,128)(2,1)S(1)}, bf16[768,128]{1,0:T(8,128)(2,1)S(1)}, u32[]{:S(2)}, u32[]{:S(2)}) collective-permute-start(bf16[768,128]{1,0:T(8,128)(2,1)S(1)} %collective-permute-done.18.m3), channel_id=1, source_target_pairs={{0,4},{4,0},{1,5},{5,1},{2,6},{6,2},{3,7},{7,3},{8,12},{12,8},{9,1... | collective-permute-start | bytes 589832 | tf_op jit(solution)/shard_map/ppermute | solution.py:37
  93.3 8.5 %collective-permute-start.23 = (bf16[528,128]{1,0:T(8,128)(2,1)S(1)}, bf16[528,128]{1,0:T(8,128)(2,1)S(1)}, u32[]{:S(2)}, u32[]{:S(2)}) collective-permute-start(bf16[528,128]{1,0:T(8,128)(2,1)S(1)} %get-tuple-element.41.first), channel_id=1, source_target_pairs={{0,8},{8,16},{16,24},{24,32},{32,40},{40,48},{48,56},{56,0},{1,9},... | collective-permute-start | bytes 405512 | tf_op jit(solution)/shard_map/ppermute | solution.py:33
  94.4 7.4 %collective-permute-start.24 = (bf16[528,128]{1,0:T(8,128)(2,1)S(1)}, bf16[528,128]{1,0:T(8,128)(2,1)S(1)}, u32[]{:S(2)}, u32[]{:S(2)}) collective-permute-start(bf16[528,128]{1,0:T(8,128)(2,1)S(1)} %get-tuple-element.42), channel_id=1, source_target_pairs={{0,56},{8,0},{16,8},{24,16},{32,24},{40,32},{48,40},{56,48},{1,57}... | collective-permute-start | bytes 405512 | tf_op jit(solution)/shard_map/ppermute | solution.py:33
  101.9 6.7 %collective-permute-start.25 = (bf16[528,128]{1,0:T(8,128)(2,1)S(1)}, bf16[528,128]{1,0:T(8,128)(2,1)S(1)}, u32[]{:S(2)}, u32[]{:S(2)}) collective-permute-start(bf16[528,128]{1,0:T(8,128)(2,1)S(1)} %get-tuple-element.44), channel_id=1, source_target_pairs={{0,8},{8,16},{16,24},{24,32},{32,40},{40,48},{48,56},{56,0},{1,9},... | collective-permute-start | bytes 405512 | tf_op jit(solution)/shard_map/ppermute | solution.py:33
  102.0 6.6 %collective-permute-start.26 = (bf16[528,128]{1,0:T(8,128)(2,1)S(1)}, bf16[528,128]{1,0:T(8,128)(2,1)S(1)}, u32[]{:S(2)}, u32[]{:S(2)}) collective-permute-start(bf16[528,128]{1,0:T(8,128)(2,1)S(1)} %get-tuple-element.45), channel_id=1, source_target_pairs={{0,56},{8,0},{16,8},{24,16},{32,24},{40,32},{48,40},{56,48},{1,57}... | collective-permute-start | bytes 405512 | tf_op jit(solution)/shard_map/ppermute | solution.py:33
  108.6 6.6 %collective-permute-start.27 = (bf16[528,128]{1,0:T(8,128)(2,1)S(1)}, bf16[528,128]{1,0:T(8,128)(2,1)S(1)}, u32[]{:S(2)}, u32[]{:S(2)}) collective-permute-start(bf16[528,128]{1,0:T(8,128)(2,1)S(1)} %get-tuple-element.46), channel_id=1, source_target_pairs={{0,8},{8,16},{16,24},{24,32},{32,40},{40,48},{48,56},{56,0},{1,9},... | collective-permute-start | bytes 405512 | tf_op jit(solution)/shard_map/ppermute | solution.py:33
  115.2 8.2 %collective-permute-start.29 = (bf16[512,128]{1,0:T(8,128)(2,1)S(1)}, bf16[512,128]{1,0:T(8,128)(2,1)S(1)}, u32[]{:S(2)}, u32[]{:S(2)}) collective-permute-start(bf16[512,128]{1,0:T(8,128)(2,1)S(1)} %get-tuple-element.48), channel_id=1, source_target_pairs={{0,8},{8,16},{16,24},{24,32},{32,40},{40,48},{48,56},{56,0},{1,9},... | collective-permute-start | bytes 393224 | tf_op jit(solution)/shard_map/ppermute | solution.py:33
  (14 other events, 109.4 us)
Sparse Core Ops, SparseCore 0:
  25.0 23.5 all-gather.2

commit v5 on v4

--- a/solution.py
+++ b/solution.py
@@ -37,15 +37,12 @@
     return lax.ppermute(x, axis, [(i, i ^ mask) for i in range(size)])
 
 
-def call(kernel, outs, inputs, name, scratch=(), flops=0, mib=16, far=0, far_outs=0):
-    out_specs = jax.tree.map(lambda _: VM, outs)
-    if far_outs:
-        out_specs = (*out_specs[:-far_outs], *[pl.BlockSpec(memory_space=pl.ANY)] * far_outs)
+def call(kernel, outs, inputs, name, scratch=(), flops=0, mib=16, far=0):
     return pl.pallas_call(
         kernel,
         out_shape=outs,
         in_specs=[VM] * (len(inputs) - far) + [pl.BlockSpec(memory_space=pl.ANY)] * far,
-        out_specs=out_specs,
+        out_specs=jax.tree.map(lambda _: VM, outs),
         scratch_shapes=list(scratch),
         compiler_params=pltpu.CompilerParams(vmem_limit_bytes=mib << 20),
         cost_estimate=pl.CostEstimate(flops=flops, bytes_accessed=1 << 18, transcendentals=0),
@@ -62,25 +59,19 @@
     owner_scr, row_scr, hub_id_scr, hub_scr, sems,
 ):
     parity, half = lax.axis_index("x") // 2, lax.axis_index("x") % 2
-    copies = [
-        pltpu.make_async_copy(source, target, sems.at[index])
-        for index, (source, target) in enumerate(
-            (
-                (owner, owner_scr),
-                (row, row_scr),
-                (hub_id, hub_id_scr),
-                (hub, hub_scr),
-                (feat, mine_ref.at[pl.ds(0, HALF)]),
-                (feat, both.at[pl.ds(0, HALF)]),
-                (cot, both.at[pl.ds(HALF, HALF)]),
-                (feat, both.at[pl.ds(V, HALF)]),
-                (cot, both.at[pl.ds(V + HALF, HALF)]),
-            )
-        )
-    ]
+    pairs = (
+        (owner, owner_scr),
+        (row, row_scr),
+        (hub_id, hub_id_scr),
+        (hub, hub_scr),
+        (feat, mine_ref.at[pl.ds(0, HALF)]),
+        (feat, both.at[pl.ds(0, HALF)]),
+        (cot, both.at[pl.ds(HALF, HALF)]),
+    )
+    copies = [pltpu.make_async_copy(a, b, sems.at[i]) for i, (a, b) in enumerate(pairs)]
     for copy in copies:
         copy.start()
-    for copy in copies[:5]:
+    for copy in copies:
         copy.wait()
     ids_ref[0:8] = owner_scr[...].reshape(8, V) * V + row_scr[...]
     ids_ref[8:12] = hub_id_scr[...]
@@ -90,8 +81,6 @@
     )
     columns = hub_scr[:, pl.ds(pl.multiple_of(half * COLS, COLS), COLS)]
     mine_ref[HALF:BLOCK] = dot(pick.astype(F32).astype(BF), columns).astype(BF)
-    for copy in copies[5:]:
-        copy.wait()
 
 
 def counts_kernel(ids0, ids1, ids2, ids3, out_ref):
@@ -202,9 +191,12 @@
     lax.fori_loop(0, NY, step, 0)
 
 
-def arrange_kernel(fg, ws_ref, feat_ref, cot_ref, pre_ref):
+def arrange_kernel(fg0, fg1, fg23, ws_ref, feat_ref, cot_ref, pre_ref, scr):
+    x = lax.axis_index("x")
+    for mask, (ref, start) in enumerate(((fg0, 0), (fg1, 0), (fg23, 0), (fg23, V))):
+        scr[x ^ mask] = ref[start : start + V]
     for start, ref in ((0, feat_ref), (HALF, cot_ref)):
-        quarters = [fg[q, start : start + HALF] for q in range(NX)]
+        quarters = [scr[q, start : start + HALF] for q in range(NX)]
         ref[...] = jnp.concatenate(
             [jnp.concatenate(quarters[0:2], 1), jnp.concatenate(quarters[2:4], 1)], 0
         )
@@ -349,7 +341,7 @@
 def body(features, hub_feats, nbr_owner, nbr_row, hub_ids, w_self, w_nbr, grad_out):
     ids, mine, fg = call(
         prepare_kernel,
-        (pltpu.VMEM((16, V), jnp.int32), pltpu.VMEM((BLOCK, COLS), BF), shaped((2 * V, COLS), BF)),
+        (pltpu.VMEM((16, V), jnp.int32), pltpu.VMEM((BLOCK, COLS), BF), pltpu.VMEM((V, COLS), BF)),
         (features, grad_out, hub_feats, nbr_owner.reshape(8, 1, V), nbr_row, hub_ids.T),
         "prepare",
         scratch=[
@@ -357,14 +349,14 @@
             pltpu.VMEM((8, V), jnp.int32),
             pltpu.VMEM((4, V), jnp.int32),
             pltpu.VMEM((2 * HUB_ROWS, 256), BF),
-            pltpu.SemaphoreType.DMA((9,)),
+            pltpu.SemaphoreType.DMA((7,)),
         ],
         far=6,
-        far_outs=1,
         mib=56,
     )
 
-    everything = lax.all_gather(fg, "x", axis=0)
+    fg1 = swap(fg, "x", NX, 1)
+    fg23 = swap(jnp.concatenate([fg, fg1], 0), "x", NX, 2)
 
     pair = jnp.stack([ids, swap(ids, "c", NC, 1)])
     t1, t7, t2 = shift(mine, "z", NZ, -1), shift(mine, "z", NZ, 1), shift(mine, "z", NZ, -2)
@@ -402,8 +394,9 @@
     feats, cots, base = call(
         arrange_kernel,
         (shaped((V, 256), BF), shaped((V, 256), BF), shaped((V, 256), F32)),
-        (everything, w_self),
+        (fg, fg1, fg23, w_self),
         "arrange",
+        scratch=[pltpu.VMEM((NX, V, COLS), BF)],
         flops=1 << 28,
     )
     outputs, message, self_term = call(

time: 131 us -> 105 us (0.80)
  between operations: 14.3 us -> 0.85 us
  local copies, waits for them, and re-layouts: 9.89 us -> 0.04 us
  Pallas kernels: 29.8 us -> 23.3 us
  starting transfers between devices: 45.6 us -> 47.9 us
    unnamed x10 -> x4, local copies, waits for them, and re-layouts: 9.87 us -> 0.01 us
    pallas_call x13, Pallas kernels: 29.8 us -> 23.3 us  [call(): pl.pallas_call(kernel, out_shape=outs, in_specs=[VM] * (len(inputs) - far...]
    ppermute x18 -> x20, starting transfers between devices: 18.1 us -> 20.2 us  [swap(): return lax.ppermute(x, axis, [(i, i ^ mask) for i in range(size)])]
    ppermute x18 -> x20, waiting for transfers between devices: 20.6 us -> 22.4 us  [swap(): return lax.ppermute(x, axis, [(i, i ^ mask) for i in range(size)])]
  transfers between devices with their start and end apart: 33 -> 34, of which waited for: 15 -> 17; matrix products, arithmetic and copies ran while one was open for 0% -> 0% of each run, Pallas kernels for 13% -> 16%
where the time goes in v5:
time: 105 us; the launch traced here: 104 us
  starting transfers between devices  47.9 us (46%)
  waiting for transfers between devices  31.5 us (30%)
  Pallas kernels  23.3 us (22%)
    pallas_call x13, Pallas kernels, call(): pl.pallas_call(kernel, out_shape=outs, in_specs=[VM] * (len(inputs) - far...  23.3 us
    ppermute x12, starting transfers between devices, shift(): return lax.ppermute(x, axis, [(i, (i + step) % size) for i in range(size)])  22.8 us
    ppermute x20, waiting for transfers between devices, swap(): return lax.ppermute(x, axis, [(i, i ^ mask) for i in range(size)])  22.4 us
    ppermute x20, starting transfers between devices, swap(): return lax.ppermute(x, axis, [(i, i ^ mask) for i in range(size)])  20.2 us
    ppermute x12, waiting for transfers between devices, shift(): return lax.ppermute(x, axis, [(i, (i + step) % size) for i in range(size)])  6.08 us
    ppermute x1, starting transfers between devices, body(): hub_here = lax.ppermute(hub_here, 'x', [(x, turn[x]) for x in range(NX)])  2.57 us
    ppermute x1, starting transfers between devices, body(): hub_up = lax.ppermute(hub_up, ('z', 'x'), cross)  2.29 us
  transfers between devices with their start and end apart: 34, of which 17 were waited for; matrix products, arithmetic and copies ran while one was open for 0% of the time, Pallas kernels for 16%

profile of v5, /device:TPU:4, one launch (start us, length us, event | category | flops | bytes accessed | tf_op | source)
XLA Modules:
  0.0 103.9 jit_solution(12980473153534500537)
XLA Ops:
  1.9 5.9 %collective-permute-start.6 = (bf16[272,128]{1,0:T(8,128)(2,1)S(1)}, bf16[272,128]{1,0:T(8,128)(2,1)S(1)}, u32[]{:S(2)}, u32[]{:S(2)}) collective-permute-start(bf16[272,128]{1,0:T(8,128)(2,1)S(1)} %get-tuple-element.35.t0), channel_id=1, source_target_pairs={{0,56},{8,0},{16,8},{24,16},{32,24},{40,32},{48,40},{56,48},{1,57}... | collective-permute-start | bytes 208904 | tf_op jit(solution)/shard_map/ppermute | solution.py:33
  12.0 2.9 %collective-permute-start.4 = (s32[2,16,512]{2,1,0:T(8,128)S(1)}, s32[2,16,512]{2,1,0:T(8,128)S(1)}, u32[]{:S(2)}, u32[]{:S(2)}) collective-permute-start(s32[2,16,512]{2,1,0:T(8,128)S(1)} %pad_add_fusion.ids0), channel_id=1, source_target_pairs={{0,128},{64,192},{128,0},{192,64},{1,129},{65,193},{129,1},{193,65... | collective-permute-start | bytes 196616 | tf_op jit(solution)/shard_map/ppermute | solution.py:37
  16.7 1.7 %collective-permute-start.10 = (bf16[544,128]{1,0:T(8,128)(2,1)S(1)}, bf16[544,128]{1,0:T(8,128)(2,1)S(1)}, u32[]{:S(2)}, u32[]{:S(2)}) collective-permute-start(bf16[544,128]{1,0:T(8,128)(2,1)S(1)} %pad_maximum_fusion.2), channel_id=1, source_target_pairs={{0,16},{8,24},{16,32},{24,40},{32,48},{40,56},{48,0},{56,8},{1,17}... | collective-permute-start | bytes 417800 | tf_op jit(solution)/shard_map/ppermute | solution.py:33
  18.4 2.0 %collective-permute-done.5.ids3 = s32[2,16,512]{2,1,0:T(8,128)S(1)} collective-permute-done((s32[2,16,512]{2,1,0:T(8,128)S(1)}, s32[2,16,512]{2,1,0:T(8,128)S(1)}, u32[]{:S(2)}, u32[]{:S(2)}) %collective-permute-start.5) | collective-permute-done | bytes 65568 | tf_op jit(solution)/shard_map/ppermute | solution.py:37
  20.4 9.8 %counts.1 = bf16[8,2304,512]{2,1,0:T(8,128)(2,1)S(1)} custom-call(s32[2,16,512]{2,1,0:T(8,128)S(1)} %pad_add_fusion.ids0, s32[2,16,512]{2,1,0:T(8,128)S(1)} %collective-permute-done.3.ids1, s32[2,16,512]{2,1,0:T(8,128)S(1)} %collective-permute-done.4.ids2, s32[2,16,512]{2,1,0:T(8,128)S(1)} %collective-permute-done.5.ids3), custom_call_target="tpu_custom_call" | custom-call | flops 17179869184 | bytes 262144 | tf_op jit(solution)/shard_map/counts/pallas_call | solution.py:41
  30.2 2.1 %far_sums.1 = (bf16[4,128,512]{2,1,0:T(8,128)(2,1)S(1)}, bf16[128,2304]{1,0:T(8,128)(2,1)S(1)}) custom-call(bf16[8,2304,512]{2,1,0:T(8,128)(2,1)S(1)} %counts.1, bf16[272,128]{1,0:T(8,128)(2,1)S(1)} %get-tuple-element.35.t0, bf16[272,128]{1,0:T(8,128)(2,1)S(1)} %collective-permute-done.6.t1, bf16[272,128]{1,0:T(8,128)(2,1)S(1)} %collective-permute-done.7.t2, ...), custom_call_target="tpu_custom_call" | custom-call | flops 2147483648 | bytes 262144 | tf_op jit(solution)/shard_map/far_sums/pallas_call | solution.py:41
  33.8 1.9 %near_sums.1 = f32[4,128,512]{2,1,0:T(8,128)S(1)} custom-call(bf16[8,2304,512]{2,1,0:T(8,128)(2,1)S(1)} %counts.1, bf16[128,2304]{1,0:T(8,128)(2,1)S(1)} %get-tuple-element.36.turned), custom_call_target="tpu_custom_call" | custom-call | flops 2147483648 | bytes 262144 | tf_op jit(solution)/shard_map/near_sums/pallas_call | solution.py:41
  37.1 3.7 %collective-permute-start.14 = (bf16[128,512]{1,0:T(8,128)(2,1)S(1)}, bf16[128,512]{1,0:T(8,128)(2,1)S(1)}, u32[]{:S(2)}, u32[]{:S(2)}) collective-permute-start(bf16[128,512]{1,0:T(8,128)(2,1)S(1)} %get-tuple-element.58), channel_id=1, source_target_pairs={{0,192},{64,128},{128,64},{192,0},{1,193},{65,129},{129,65},{193,1... | collective-permute-start | bytes 393224 | tf_op jit(solution)/shard_map/ppermute | solution.py:37
  43.5 2.7 %collective-permute-done.14 = bf16[128,512]{1,0:T(8,128)(2,1)S(1)} collective-permute-done((bf16[128,512]{1,0:T(8,128)(2,1)S(1)}, bf16[128,512]{1,0:T(8,128)(2,1)S(1)}, u32[]{:S(2)}, u32[]{:S(2)}) %collective-permute-start.14) | collective-permute-done | bytes 131104 | tf_op jit(solution)/shard_map/ppermute | solution.py:37
  47.7 2.2 %collective-permute-start.17 = (bf16[128,512]{1,0:T(8,128)(2,1)S(1)}, bf16[128,512]{1,0:T(8,128)(2,1)S(1)}, u32[]{:S(2)}, u32[]{:S(2)}) collective-permute-start(bf16[128,512]{1,0:T(8,128)(2,1)S(1)} %fusion.3.s0), channel_id=1, source_target_pairs={{0,3},{1,2},{2,1},{3,0},{4,7},{5,6},{6,5},{7,4},{8,11},{9,10},{10,... | collective-permute-start | bytes 393224 | tf_op jit(solution)/shard_map/ppermute | solution.py:37
  52.7 2.8 %collective-permute-done.16.s2 = bf16[128,512]{1,0:T(8,128)(2,1)S(1)} collective-permute-done((bf16[128,512]{1,0:T(8,128)(2,1)S(1)}, bf16[128,512]{1,0:T(8,128)(2,1)S(1)}, u32[]{:S(2)}, u32[]{:S(2)}) %collective-permute-start.16) | collective-permute-done | bytes 131104 | tf_op jit(solution)/shard_map/ppermute | solution.py:37
  58.0 3.5 %collective-permute-start.19 = (bf16[768,128]{1,0:T(8,128)(2,1)S(1)}, bf16[768,128]{1,0:T(8,128)(2,1)S(1)}, u32[]{:S(2)}, u32[]{:S(2)}) collective-permute-start(bf16[768,128]{1,0:T(8,128)(2,1)S(1)} %get-tuple-element.40.m0), channel_id=1, source_target_pairs={{0,128},{64,192},{128,0},{192,64},{1,129},{65,193},{129,1},{193,65... | collective-permute-start | bytes 589832 | tf_op jit(solution)/shard_map/ppermute | solution.py:37
  62.7 3.1 %collective-permute-done.18.m1 = bf16[768,128]{1,0:T(8,128)(2,1)S(1)} collective-permute-done((bf16[768,128]{1,0:T(8,128)(2,1)S(1)}, bf16[768,128]{1,0:T(8,128)(2,1)S(1)}, u32[]{:S(2)}, u32[]{:S(2)}) %collective-permute-start.18) | collective-permute-done | bytes 196640 | tf_op jit(solution)/shard_map/ppermute | solution.py:37
  65.9 3.8 %collective-permute-done.19.m2 = bf16[768,128]{1,0:T(8,128)(2,1)S(1)} collective-permute-done((bf16[768,128]{1,0:T(8,128)(2,1)S(1)}, bf16[768,128]{1,0:T(8,128)(2,1)S(1)}, u32[]{:S(2)}, u32[]{:S(2)}) %collective-permute-start.19) | collective-permute-done | bytes 196640 | tf_op jit(solution)/shard_map/ppermute | solution.py:37
  69.6 2.3 %collective-permute-done.20.m3 = bf16[768,128]{1,0:T(8,128)(2,1)S(1)} collective-permute-done((bf16[768,128]{1,0:T(8,128)(2,1)S(1)}, bf16[768,128]{1,0:T(8,128)(2,1)S(1)}, u32[]{:S(2)}, u32[]{:S(2)}) %collective-permute-start.20) | collective-permute-done | bytes 196640 | tf_op jit(solution)/shard_map/ppermute | solution.py:37
  75.5 2.2 %collective-permute-start.26 = (bf16[528,128]{1,0:T(8,128)(2,1)S(1)}, bf16[528,128]{1,0:T(8,128)(2,1)S(1)}, u32[]{:S(2)}, u32[]{:S(2)}) collective-permute-start(bf16[528,128]{1,0:T(8,128)(2,1)S(1)} %get-tuple-element.42), channel_id=1, source_target_pairs={{0,56},{8,0},{16,8},{24,16},{32,24},{40,32},{48,40},{56,48},{1,57}... | collective-permute-start | bytes 405512 | tf_op jit(solution)/shard_map/ppermute | solution.py:33
  77.8 3.4 %rest_grads.1.rest = f32[6,256,128]{2,1,0:T(8,128)S(1)} custom-call(bf16[8,2304,512]{2,1,0:T(8,128)(2,1)S(1)} %counts.1, bf16[768,128]{1,0:T(8,128)(2,1)S(1)} %get-tuple-element.40.m0, bf16[768,128]{1,0:T(8,128)(2,1)S(1)} %collective-permute-done.18.m1, bf16[768,128]{1,0:T(8,128)(2,1)S(1)} %collective-permute-done.19.m2, ...), custom_call_target="tpu_custom_call" | custom-call | flops 2147483648 | bytes 262144 | tf_op jit(solution)/shard_map/rest_grads/pallas_call | solution.py:41
  81.6 3.1 %collective-permute-start.28 = (bf16[528,128]{1,0:T(8,128)(2,1)S(1)}, bf16[528,128]{1,0:T(8,128)(2,1)S(1)}, u32[]{:S(2)}, u32[]{:S(2)}) collective-permute-start(bf16[528,128]{1,0:T(8,128)(2,1)S(1)} %get-tuple-element.45), channel_id=1, source_target_pairs={{0,56},{8,0},{16,8},{24,16},{32,24},{40,32},{48,40},{56,48},{1,57}... | collective-permute-start | bytes 405512 | tf_op jit(solution)/shard_map/ppermute | solution.py:33
  84.7 3.0 %collective-permute-done.27.up.up2 = bf16[528,128]{1,0:T(8,128)(2,1)S(1)} collective-permute-done((bf16[528,128]{1,0:T(8,128)(2,1)S(1)}, bf16[528,128]{1,0:T(8,128)(2,1)S(1)}, u32[]{:S(2)}, u32[]{:S(2)}) %collective-permute-start.27) | collective-permute-done | bytes 135200 | tf_op jit(solution)/shard_map/ppermute | solution.py:33
  88.1 3.1 %collective-permute-start.30 = (bf16[528,128]{1,0:T(8,128)(2,1)S(1)}, bf16[528,128]{1,0:T(8,128)(2,1)S(1)}, u32[]{:S(2)}, u32[]{:S(2)}) collective-permute-start(bf16[528,128]{1,0:T(8,128)(2,1)S(1)} %get-tuple-element.47), channel_id=1, source_target_pairs={{0,56},{8,0},{16,8},{24,16},{32,24},{40,32},{48,40},{56,48},{1,57}... | collective-permute-start | bytes 405512 | tf_op jit(solution)/shard_map/ppermute | solution.py:33
  91.1 2.9 %collective-permute-done.29.up.up3 = bf16[528,128]{1,0:T(8,128)(2,1)S(1)} collective-permute-done((bf16[528,128]{1,0:T(8,128)(2,1)S(1)}, bf16[528,128]{1,0:T(8,128)(2,1)S(1)}, u32[]{:S(2)}, u32[]{:S(2)}) %collective-permute-start.29) | collective-permute-done | bytes 135200 | tf_op jit(solution)/shard_map/ppermute | solution.py:33
  95.2 2.3 %collective-permute-start.32 = (f32[16,128]{1,0:T(8,128)S(1)}, f32[16,128]{1,0:T(8,128)S(1)}, u32[]{:S(2)}, u32[]{:S(2)}) collective-permute-start(f32[16,128]{1,0:T(8,128)S(1)} %get-tuple-element.49), channel_id=1, source_target_pairs={{0,8},{1,10},{2,9},{3,11},{8,16},{9,18},{10,17},{11,19},{16,24},{1... | collective-permute-start | bytes 24584 | tf_op jit(solution)/shard_map/ppermute | solution.py:463
  97.5 2.6 %collective-permute-start.33 = (f32[16,128]{1,0:T(8,128)S(1)}, f32[16,128]{1,0:T(8,128)S(1)}, u32[]{:S(2)}, u32[]{:S(2)}) collective-permute-start(f32[16,128]{1,0:T(8,128)S(1)} %get-tuple-element.50), channel_id=1, source_target_pairs={{0,0},{1,2},{2,1},{3,3},{4,4},{5,6},{6,5},{7,7},{8,8},{9,10},{10,9... | collective-permute-start | bytes 24584 | tf_op jit(solution)/shard_map/ppermute | solution.py:464
  100.1 1.7 %collective-permute-done.32.hub_up = f32[16,128]{1,0:T(8,128)S(1)} collective-permute-done((f32[16,128]{1,0:T(8,128)S(1)}, f32[16,128]{1,0:T(8,128)S(1)}, u32[]{:S(2)}, u32[]{:S(2)}) %collective-permute-start.32) | collective-permute-done | bytes 8224 | tf_op jit(solution)/shard_map/ppermute | solution.py:463
  (68 shorter events, 28.3 us)
Async XLA Ops:
  1.8 8.5 %collective-permute-start.2 = (s32[16,512]{1,0:T(8,128)S(1)}, s32[16,512]{1,0:T(8,128)S(1)}, u32[]{:S(2)}, u32[]{:S(2)}) collective-permute-start(s32[16,512]{1,0:T(8,128)S(1)} %get-tuple-element.34), channel_id=1, source_target_pairs={{0,4},{4,0},{1,5},{5,1},{2,6},{6,2},{3,7},{7,3},{8,12},{12,8},{9,1... | collective-permute-start | bytes 98312 | tf_op jit(solution)/shard_map/ppermute | solution.py:37
  1.9 13.0 %collective-permute-start.6 = (bf16[272,128]{1,0:T(8,128)(2,1)S(1)}, bf16[272,128]{1,0:T(8,128)(2,1)S(1)}, u32[]{:S(2)}, u32[]{:S(2)}) collective-permute-start(bf16[272,128]{1,0:T(8,128)(2,1)S(1)} %get-tuple-element.35.t0), channel_id=1, source_target_pairs={{0,56},{8,0},{16,8},{24,16},{32,24},{40,32},{48,40},{56,48},{1,57}... | collective-permute-start | bytes 208904 | tf_op jit(solution)/shard_map/ppermute | solution.py:33
  7.8 7.3 %collective-permute-start.7 = (bf16[272,128]{1,0:T(8,128)(2,1)S(1)}, bf16[272,128]{1,0:T(8,128)(2,1)S(1)}, u32[]{:S(2)}, u32[]{:S(2)}) collective-permute-start(bf16[272,128]{1,0:T(8,128)(2,1)S(1)} %get-tuple-element.35.t0), channel_id=1, source_target_pairs={{0,48},{8,56},{16,0},{24,8},{32,16},{40,24},{48,32},{56,40},{1,49}... | collective-permute-start | bytes 208904 | tf_op jit(solution)/shard_map/ppermute | solution.py:33
  9.3 7.4 %collective-permute-start.8 = (bf16[272,128]{1,0:T(8,128)(2,1)S(1)}, bf16[272,128]{1,0:T(8,128)(2,1)S(1)}, u32[]{:S(2)}, u32[]{:S(2)}) collective-permute-start(bf16[272,128]{1,0:T(8,128)(2,1)S(1)} %get-tuple-element.35.t0), channel_id=1, source_target_pairs={{0,8},{8,16},{16,24},{24,32},{32,40},{40,48},{48,56},{56,0},{1,9},... | collective-permute-start | bytes 208904 | tf_op jit(solution)/shard_map/ppermute | solution.py:33
  10.3 8.1 %collective-permute-start.3 = (s32[2,16,512]{2,1,0:T(8,128)S(1)}, s32[2,16,512]{2,1,0:T(8,128)S(1)}, u32[]{:S(2)}, u32[]{:S(2)}) collective-permute-start(s32[2,16,512]{2,1,0:T(8,128)S(1)} %pad_add_fusion.ids0), channel_id=1, source_target_pairs={{0,64},{64,0},{128,192},{192,128},{1,65},{65,1},{129,193},{193,129... | collective-permute-start | bytes 196616 | tf_op jit(solution)/shard_map/ppermute | solution.py:37
  12.0 6.4 %collective-permute-start.4 = (s32[2,16,512]{2,1,0:T(8,128)S(1)}, s32[2,16,512]{2,1,0:T(8,128)S(1)}, u32[]{:S(2)}, u32[]{:S(2)}) collective-permute-start(s32[2,16,512]{2,1,0:T(8,128)S(1)} %pad_add_fusion.ids0), channel_id=1, source_target_pairs={{0,128},{64,192},{128,0},{192,64},{1,129},{65,193},{129,1},{193,65... | collective-permute-start | bytes 196616 | tf_op jit(solution)/shard_map/ppermute | solution.py:37
  15.1 15.1 %collective-permute-start.9 = (bf16[544,128]{1,0:T(8,128)(2,1)S(1)}, bf16[544,128]{1,0:T(8,128)(2,1)S(1)}, u32[]{:S(2)}, u32[]{:S(2)}) collective-permute-start(bf16[544,128]{1,0:T(8,128)(2,1)S(1)} %pad_maximum_fusion.1), channel_id=1, source_target_pairs={{0,48},{8,56},{16,0},{24,8},{32,16},{40,24},{48,32},{56,40},{1,49}... | collective-permute-start | bytes 417800 | tf_op jit(solution)/shard_map/ppermute | solution.py:33
  16.7 13.6 %collective-permute-start.10 = (bf16[544,128]{1,0:T(8,128)(2,1)S(1)}, bf16[544,128]{1,0:T(8,128)(2,1)S(1)}, u32[]{:S(2)}, u32[]{:S(2)}) collective-permute-start(bf16[544,128]{1,0:T(8,128)(2,1)S(1)} %pad_maximum_fusion.2), channel_id=1, source_target_pairs={{0,16},{8,24},{16,32},{24,40},{32,48},{40,56},{48,0},{56,8},{1,17}... | collective-permute-start | bytes 417800 | tf_op jit(solution)/shard_map/ppermute | solution.py:33
  32.5 8.3 %collective-permute-start = (bf16[512,128]{1,0:T(8,128)(2,1)S(1)}, bf16[512,128]{1,0:T(8,128)(2,1)S(1)}, u32[]{:S(2)}, u32[]{:S(2)}) collective-permute-start(bf16[512,128]{1,0:T(8,128)(2,1)S(1)} %get-tuple-element.30.fg0), channel_id=1, source_target_pairs={{0,1},{1,0},{2,3},{3,2},{4,5},{5,4},{6,7},{7,6},{8,9},{9,8},{10,11... | collective-permute-start | bytes 393224 | tf_op jit(solution)/shard_map/ppermute | solution.py:37
  36.0 6.4 %collective-permute-start.12 = (bf16[128,512]{1,0:T(8,128)(2,1)S(1)}, bf16[128,512]{1,0:T(8,128)(2,1)S(1)}, u32[]{:S(2)}, u32[]{:S(2)}) collective-permute-start(bf16[128,512]{1,0:T(8,128)(2,1)S(1)} %get-tuple-element.57), channel_id=1, source_target_pairs={{0,64},{64,0},{128,192},{192,128},{1,65},{65,1},{129,193},{193,129... | collective-permute-start | bytes 393224 | tf_op jit(solution)/shard_map/ppermute | solution.py:37
  36.1 7.5 %collective-permute-start.13 = (bf16[128,512]{1,0:T(8,128)(2,1)S(1)}, bf16[128,512]{1,0:T(8,128)(2,1)S(1)}, u32[]{:S(2)}, u32[]{:S(2)}) collective-permute-start(bf16[128,512]{1,0:T(8,128)(2,1)S(1)} %get-tuple-element.59), channel_id=1, source_target_pairs={{0,128},{64,192},{128,0},{192,64},{1,129},{65,193},{129,1},{193,65... | collective-permute-start | bytes 393224 | tf_op jit(solution)/shard_map/ppermute | solution.py:37
  37.1 9.1 %collective-permute-start.14 = (bf16[128,512]{1,0:T(8,128)(2,1)S(1)}, bf16[128,512]{1,0:T(8,128)(2,1)S(1)}, u32[]{:S(2)}, u32[]{:S(2)}) collective-permute-start(bf16[128,512]{1,0:T(8,128)(2,1)S(1)} %get-tuple-element.58), channel_id=1, source_target_pairs={{0,192},{64,128},{128,64},{192,0},{1,193},{65,129},{129,65},{193,1... | collective-permute-start | bytes 393224 | tf_op jit(solution)/shard_map/ppermute | solution.py:37
  40.8 10.7 %collective-permute-start.1 = (bf16[1024,128]{1,0:T(8,128)(2,1)S(1)}, bf16[1024,128]{1,0:T(8,128)(2,1)S(1)}, u32[]{:S(2)}, u32[]{:S(2)}) collective-permute-start(bf16[1024,128]{1,0:T(8,128)(2,1)S(1)} %pad_maximum_fusion), channel_id=1, source_target_pairs={{0,2},{1,3},{2,0},{3,1},{4,6},{5,7},{6,4},{7,5},{8,10},{9,11},{10,... | collective-permute-start | bytes 786440 | tf_op jit(solution)/shard_map/ppermute | solution.py:37
  46.3 6.4 %collective-permute-start.15 = (bf16[128,512]{1,0:T(8,128)(2,1)S(1)}, bf16[128,512]{1,0:T(8,128)(2,1)S(1)}, u32[]{:S(2)}, u32[]{:S(2)}) collective-permute-start(bf16[128,512]{1,0:T(8,128)(2,1)S(1)} %fusion.3.s0), channel_id=1, source_target_pairs={{0,1},{1,0},{2,3},{3,2},{4,5},{5,4},{6,7},{7,6},{8,9},{9,8},{10,11... | collective-permute-start | bytes 393224 | tf_op jit(solution)/shard_map/ppermute | solution.py:37
  47.2 8.4 %collective-permute-start.16 = (bf16[128,512]{1,0:T(8,128)(2,1)S(1)}, bf16[128,512]{1,0:T(8,128)(2,1)S(1)}, u32[]{:S(2)}, u32[]{:S(2)}) collective-permute-start(bf16[128,512]{1,0:T(8,128)(2,1)S(1)} %fusion.3.s0), channel_id=1, source_target_pairs={{0,2},{1,3},{2,0},{3,1},{4,6},{5,7},{6,4},{7,5},{8,10},{9,11},{10,... | collective-permute-start | bytes 393224 | tf_op jit(solution)/shard_map/ppermute | solution.py:37
  47.7 8.7 %collective-permute-start.17 = (bf16[128,512]{1,0:T(8,128)(2,1)S(1)}, bf16[128,512]{1,0:T(8,128)(2,1)S(1)}, u32[]{:S(2)}, u32[]{:S(2)}) collective-permute-start(bf16[128,512]{1,0:T(8,128)(2,1)S(1)} %fusion.3.s0), channel_id=1, source_target_pairs={{0,3},{1,2},{2,1},{3,0},{4,7},{5,6},{6,5},{7,4},{8,11},{9,10},{10,... | collective-permute-start | bytes 393224 | tf_op jit(solution)/shard_map/ppermute | solution.py:37
  58.0 7.8 %collective-permute-start.18 = (bf16[768,128]{1,0:T(8,128)(2,1)S(1)}, bf16[768,128]{1,0:T(8,128)(2,1)S(1)}, u32[]{:S(2)}, u32[]{:S(2)}) collective-permute-start(bf16[768,128]{1,0:T(8,128)(2,1)S(1)} %get-tuple-element.40.m0), channel_id=1, source_target_pairs={{0,64},{64,0},{128,192},{192,128},{1,65},{65,1},{129,193},{193,129... | collective-permute-start | bytes 589832 | tf_op jit(solution)/shard_map/ppermute | solution.py:37
  58.0 11.6 %collective-permute-start.19 = (bf16[768,128]{1,0:T(8,128)(2,1)S(1)}, bf16[768,128]{1,0:T(8,128)(2,1)S(1)}, u32[]{:S(2)}, u32[]{:S(2)}) collective-permute-start(bf16[768,128]{1,0:T(8,128)(2,1)S(1)} %get-tuple-element.40.m0), channel_id=1, source_target_pairs={{0,128},{64,192},{128,0},{192,64},{1,129},{65,193},{129,1},{193,65... | collective-permute-start | bytes 589832 | tf_op jit(solution)/shard_map/ppermute | solution.py:37
  61.6 10.4 %collective-permute-start.20 = (bf16[768,128]{1,0:T(8,128)(2,1)S(1)}, bf16[768,128]{1,0:T(8,128)(2,1)S(1)}, u32[]{:S(2)}, u32[]{:S(2)}) collective-permute-start(bf16[768,128]{1,0:T(8,128)(2,1)S(1)} %get-tuple-element.40.m0), channel_id=1, source_target_pairs={{0,192},{64,128},{128,64},{192,0},{1,193},{65,129},{129,65},{193,1... | collective-permute-start | bytes 589832 | tf_op jit(solution)/shard_map/ppermute | solution.py:37
  62.7 10.2 %collective-permute-start.21 = (bf16[768,128]{1,0:T(8,128)(2,1)S(1)}, bf16[768,128]{1,0:T(8,128)(2,1)S(1)}, u32[]{:S(2)}, u32[]{:S(2)}) collective-permute-start(bf16[768,128]{1,0:T(8,128)(2,1)S(1)} %get-tuple-element.40.m0), channel_id=1, source_target_pairs={{0,4},{4,0},{1,5},{5,1},{2,6},{6,2},{3,7},{7,3},{8,12},{12,8},{9,1... | collective-permute-start | bytes 589832 | tf_op jit(solution)/shard_map/ppermute | solution.py:37
  65.9 7.1 %collective-permute-start.22 = (bf16[768,128]{1,0:T(8,128)(2,1)S(1)}, bf16[768,128]{1,0:T(8,128)(2,1)S(1)}, u32[]{:S(2)}, u32[]{:S(2)}) collective-permute-start(bf16[768,128]{1,0:T(8,128)(2,1)S(1)} %collective-permute-done.18.m1), channel_id=1, source_target_pairs={{0,4},{4,0},{1,5},{5,1},{2,6},{6,2},{3,7},{7,3},{8,12},{12,8},{9,1... | collective-permute-start | bytes 589832 | tf_op jit(solution)/shard_map/ppermute | solution.py:37
  74.4 6.9 %collective-permute-start.25 = (bf16[528,128]{1,0:T(8,128)(2,1)S(1)}, bf16[528,128]{1,0:T(8,128)(2,1)S(1)}, u32[]{:S(2)}, u32[]{:S(2)}) collective-permute-start(bf16[528,128]{1,0:T(8,128)(2,1)S(1)} %get-tuple-element.41.first), channel_id=1, source_target_pairs={{0,8},{8,16},{16,24},{24,32},{32,40},{40,48},{48,56},{56,0},{1,9},... | collective-permute-start | bytes 405512 | tf_op jit(solution)/shard_map/ppermute | solution.py:33
  94.1 9.0 %collective-permute-start.31 = (bf16[512,128]{1,0:T(8,128)(2,1)S(1)}, bf16[512,128]{1,0:T(8,128)(2,1)S(1)}, u32[]{:S(2)}, u32[]{:S(2)}) collective-permute-start(bf16[512,128]{1,0:T(8,128)(2,1)S(1)} %get-tuple-element.48), channel_id=1, source_target_pairs={{0,8},{8,16},{16,24},{24,32},{32,40},{40,48},{48,56},{56,0},{1,9},... | collective-permute-start | bytes 393224 | tf_op jit(solution)/shard_map/ppermute | solution.py:33
  95.2 6.6 %collective-permute-start.32 = (f32[16,128]{1,0:T(8,128)S(1)}, f32[16,128]{1,0:T(8,128)S(1)}, u32[]{:S(2)}, u32[]{:S(2)}) collective-permute-start(f32[16,128]{1,0:T(8,128)S(1)} %get-tuple-element.49), channel_id=1, source_target_pairs={{0,8},{1,10},{2,9},{3,11},{8,16},{9,18},{10,17},{11,19},{16,24},{1... | collective-permute-start | bytes 24584 | tf_op jit(solution)/shard_map/ppermute | solution.py:463
  (12 other events, 97.1 us)
